TPU v7x, 128 devices: a whole 4x4x4 slice. The times are simulated.
128 devices in a mesh: rep: 2 (over x_hi), dp: 8 (over y, core), tensor: 8 (over z, x_lo).
Axes of the slice: x: 4 (x_hi: 2, x_lo: 2; x = x_hi * 2 + x_lo), y: 4, z: 4, core: 2. Of those that a mesh axis runs over, the one named last changes fastest.
Arguments:
- hidden_in: bfloat16 [8192, 8192], P(('rep', 'dp')), may hold values from -6 to 6
- out_grad: bfloat16 [8192, 8192], P(('rep', 'dp'), 'tensor'), may hold values from -0.0059814453 to 0.0059814453
- queries: bfloat16 [8192, 8192], P(('rep', 'dp'), 'tensor'), may hold values from -120 to 120
- keys: bfloat16 [8192, 1024], P(('rep', 'dp'), 'tensor'), may hold values from -5 to 5
- segment_ids: int32 [16, 512], P(('rep', 'dp')), may hold values from 0 to 3, never falling along the last dimension, each value on 1 to 256 neighbouring positions
- value_codes: int32 [8192, 1024], P(('rep', 'dp'), 'tensor'), may hold values from 0 to 15
- value_steps: float32 [64, 1024], P(('rep', 'dp'), 'tensor'), may hold values from 0.0012 to 0.005
- output_codes: int32 [8192, 8192], P('tensor', ('rep', 'dp')), may hold values from 0 to 15
- output_steps: float32 [64, 8192], P('tensor', ('rep', 'dp')), may hold values from 0.0012 to 0.005
Outputs:
- output_step_grad: float32 [64, 8192], P('tensor', ('rep', 'dp'))
- value_step_grad: float32 [64, 1024], P(('rep', 'dp'), 'tensor')
- output_weight_grad: float32 [8192, 8192], P('tensor', ('rep', 'dp'))
- value_weight_grad: float32 [8192, 1024], P(('rep', 'dp'), 'tensor')
All inputs are finite; a program needn't handle non-finite values.
Results may differ from a plain program's by a relative error of at most 0.02.
Values may be sent and summed in bfloat16 or wider, within the bound.
No kernel may reach another device: no remote copies, remote signals or barrier semaphores. Data moves between devices by JAX's collectives and lax.ppermute only.
A program may use at most 192 MiB of HBM per device.

v0:
```python
import jax
import jax.numpy as jnp
from jax import lax
from jax.experimental import pallas as pl
from jax.experimental.pallas import tpu as pltpu
from jax.sharding import Mesh, PartitionSpec as P

HD = 128
GROUP = 128
GQ = 8
SIZES = {"xh": 2, "y": 4, "c": 2, "z": 4, "xl": 2}
ROWS = ("xh", "y", "c")
HEADS_AXES = ("z", "xl")
F32 = jnp.float32
BF16 = jnp.bfloat16
TOGETHER = 2
LONG = pl.CostEstimate(flops=1 << 35, bytes_accessed=1 << 24, transcendentals=0)
BRIEF = pl.CostEstimate(flops=1 << 20, bytes_accessed=1 << 16, transcendentals=0)


def shift(x, axis, step):
    n = SIZES[axis]
    return lax.ppermute(x, axis, [(i, (i + step) % n) for i in range(n)])


def dequant_rows(codes, steps):
    rows, columns = codes.shape

    def kernel(codes_ref, steps_ref, out):
        for k in range(rows // GROUP):
            group = slice(k * GROUP, (k + 1) * GROUP)
            centered = (codes_ref[group, :] - 8).astype(F32)
            out[group, :] = (centered * steps_ref[k : k + 1, :]).astype(BF16)

    return pl.pallas_call(
        kernel,
        out_shape=jax.ShapeDtypeStruct((rows, columns), BF16),
        cost_estimate=BRIEF,
    )(codes, steps)


def dequant_transposed(codes, steps):
    rows, columns = codes.shape
    block = rows // 2
    groups = block // GROUP

    def kernel(codes_ref, steps_ref, out):
        for k in range(groups):
            group = slice(k * GROUP, (k + 1) * GROUP)
            centered = (codes_ref[group, :] - 8).astype(F32)
            step = steps_ref[pl.ds(pl.program_id(0) * groups + k, 1), :]
            out[:, group] = (centered * step).astype(BF16).T

    return pl.pallas_call(
        kernel,
        out_shape=jax.ShapeDtypeStruct((columns, rows), BF16),
        grid=(rows // block,),
        in_specs=[
            pl.BlockSpec((block, columns), lambda k: (k, 0)),
            pl.BlockSpec(steps.shape, lambda k: (0, 0)),
        ],
        out_specs=pl.BlockSpec((columns, block), lambda k: (0, k)),
        cost_estimate=BRIEF,
    )(codes, steps)


def attention_probs(queries, keys, segment_ids, first, count):
    length = keys.shape[0]

    def kernel(q_ref, k_ref, down_ref, along_ref, out, allowed):
        @pl.when(pl.program_id(0) == 0)
        def _():
            key_at = lax.broadcasted_iota(jnp.int32, (length, length), 0)
            query_at = lax.broadcasted_iota(jnp.int32, (length, length), 1)
            seen = (key_at <= query_at) & (down_ref[...] == along_ref[...])
            allowed[...] = seen.astype(F32)

        scores = lax.dot_general(
            k_ref[...], q_ref[...], (((1,), (1,)), ((), ())), preferred_element_type=F32
        ) * HD ** (-0.5)
        scores = jnp.where(allowed[...] > 0.5, scores, -1e30)
        powers = jnp.exp(scores - jnp.max(scores, axis=0, keepdims=True))
        out[0] = (powers / jnp.sum(powers, axis=0, keepdims=True)).astype(BF16)

    return pl.pallas_call(
        kernel,
        out_shape=jax.ShapeDtypeStruct((count, length, length), BF16),
        grid=(count,),
        in_specs=[
            pl.BlockSpec((length, HD), lambda h: (0, first + h)),
            pl.BlockSpec((length, HD), lambda h: (0, 0)),
            pl.BlockSpec((length, 1), lambda h: (0, 0)),
            pl.BlockSpec((1, length), lambda h: (0, 0)),
        ],
        out_specs=pl.BlockSpec((1, length, length), lambda h: (h, 0, 0)),
        scratch_shapes=[pltpu.VMEM((length, length), F32)],
        compiler_params=pltpu.CompilerParams(vmem_limit_bytes=32 << 20),
        cost_estimate=LONG,
    )(queries, keys, segment_ids.reshape(length, 1), segment_ids)


def attended_heads(hidden_in, value_weight, probs):
    width, columns = value_weight.shape
    rows = hidden_in.shape[0]
    heads = 2 * probs[0].shape[0]
    count = 8
    depth = width // count

    def kernel(h_ref, v_ref, p_low, p_high, out, total):
        k = pl.program_id(0)
        more = jnp.dot(h_ref[...], v_ref[...], preferred_element_type=F32)

        @pl.when(k == 0)
        def _():
            total[...] = more

        @pl.when(k > 0)
        def _():
            total[...] += more

        @pl.when(k == count - 1)
        def _():
            values = total[...].T.astype(BF16)
            for h in range(heads):
                p_ref = (p_low, p_high)[h // (heads // 2)]
                one = jnp.dot(values, p_ref[h % (heads // 2)], preferred_element_type=F32)
                out[h * columns : (h + 1) * columns, :] = one.astype(BF16)

    whole = pl.BlockSpec(probs[0].shape, lambda k: (0, 0, 0))
    return pl.pallas_call(
        kernel,
        out_shape=jax.ShapeDtypeStruct((heads * columns, rows), BF16),
        grid=(count,),
        in_specs=[
            pl.BlockSpec((rows, depth), lambda k: (0, k)),
            pl.BlockSpec((depth, columns), lambda k: (k, 0)),
            whole,
            whole,
        ],
        out_specs=pl.BlockSpec((heads * columns, rows), lambda k: (0, 0)),
        scratch_shapes=[pltpu.VMEM((rows, columns), F32)],
        compiler_params=pltpu.CompilerParams(vmem_limit_bytes=56 << 20),
        cost_estimate=LONG,
    )(hidden_in, value_weight, *probs)


def value_terms(hidden_in, here, there, probs, own_order, other_order):
    count = own_order.shape[0]
    rows, heads = here.shape
    width = hidden_in.shape[1] // (2 * count)
    half = probs[0].shape[0]

    def kernel(own_ref, other_ref, h_own, h_other, a_ref, b_ref, p_low, p_high, *refs):
        own_out, other_out, grad = refs

        @pl.when(pl.program_id(0) == 0)
        def _():
            total = jnp.zeros((rows, HD), F32)
            for h in range(2 * half):
                head = slice(h * HD, (h + 1) * HD)
                attended_grad = (a_ref[:, head] + b_ref[:, head].astype(F32)).astype(BF16)
                p_ref = (p_low, p_high)[h // half]
                total += jnp.dot(p_ref[h % half], attended_grad, preferred_element_type=F32)
            grad[...] = total.T.astype(BF16)

        own_out[0] = jnp.dot(grad[...], h_own[...], preferred_element_type=F32)
        other = jnp.dot(grad[...], h_other[...], preferred_element_type=F32)
        other_out[0] = other.astype(BF16)

    whole = pl.BlockSpec(probs[0].shape, lambda k, own, other: (0, 0, 0))
    return pl.pallas_call(
        kernel,
        out_shape=(
            jax.ShapeDtypeStruct((count, HD, width), F32),
            jax.ShapeDtypeStruct((count, HD, width), BF16),
        ),
        grid_spec=pltpu.PrefetchScalarGridSpec(
            num_scalar_prefetch=2,
            grid=(count,),
            in_specs=[
                pl.BlockSpec((rows, width), lambda k, own, other: (0, own[k])),
                pl.BlockSpec((rows, width), lambda k, own, other: (0, other[k])),
                pl.BlockSpec((rows, heads), lambda k, own, other: (0, 0)),
                pl.BlockSpec((rows, heads), lambda k, own, other: (0, 0)),
                whole,
                whole,
            ],
            out_specs=(
                pl.BlockSpec((1, HD, width), lambda k, own, other: (k, 0, 0)),
                pl.BlockSpec((1, HD, width), lambda k, own, other: (k, 0, 0)),
            ),
            scratch_shapes=[pltpu.VMEM((HD, rows), BF16)],
        ),
        compiler_params=pltpu.CompilerParams(vmem_limit_bytes=56 << 20),
        cost_estimate=BRIEF,
    )(own_order, other_order, hidden_in, hidden_in, here, there, *probs)


def value_grads(own, others, codes):
    columns, rows = own.shape

    def kernel(own_ref, *refs):
        refs, (codes_ref, step_out, out) = refs[: len(others)], refs[len(others) :]
        total = own_ref[...]
        for ref in refs:
            total += ref[...].astype(F32)
        total = total.T
        out[...] = total
        centered = (codes_ref[...] - 8).astype(F32) * total
        for k in range(rows // GROUP):
            group = centered[k * GROUP : (k + 1) * GROUP]
            step_out[k : k + 1, :] = jnp.sum(group, axis=0, keepdims=True)

    return pl.pallas_call(
        kernel,
        out_shape=(
            jax.ShapeDtypeStruct((rows // GROUP, columns), F32),
            jax.ShapeDtypeStruct((rows, columns), F32),
        ),
        cost_estimate=BRIEF,
    )(own, *others, codes)


def fetch_piece(which, pieces, target, sem):
    for i, piece in enumerate(pieces):

        @pl.when(which == i)
        def _():
            pltpu.make_async_copy(piece, target, sem).start()


def head_grads(grads, weights, order):
    count = len(weights)
    rows, depth = grads[0].shape
    heads = weights[0].shape[1]
    half = rows // 2
    steps = count // TOGETHER
    span = depth * TOGETHER

    def kernel(order_ref, *refs):
        g_refs, w_refs, refs = refs[:count], refs[count : 2 * count], refs[2 * count :]
        own, other, g_held, w_held, total, g_sems, w_sems = refs
        k = pl.program_id(0)

        def blocks(step):
            for i in range(TOGETHER):
                at = slice(i * depth, (i + 1) * depth)
                yield step * TOGETHER + i, g_held.at[step, :, at], w_held.at[step, at, :]

        @pl.when(k == 0)
        def _():
            for step in range(steps):
                for i, g_at, w_at in blocks(step):
                    fetch_piece(order_ref[i], g_refs, g_at, g_sems.at[step])
                    pltpu.make_async_copy(w_refs[i], w_at, w_sems.at[step]).start()
            total[...] = jnp.zeros_like(total)

        pltpu.make_async_copy(g_held.at[k], g_held.at[k], g_sems.at[k]).wait()
        pltpu.make_async_copy(w_held.at[k], w_held.at[k], w_sems.at[k]).wait()
        total[...] += jnp.dot(g_held[k], w_held[k], preferred_element_type=F32)

        @pl.when(k == steps - 1)
        def _():
            own[...] = total[:half]
            other[...] = total[half:].astype(BF16)

    return pl.pallas_call(
        kernel,
        out_shape=(
            jax.ShapeDtypeStruct((half, heads), F32),
            jax.ShapeDtypeStruct((half, heads), BF16),
        ),
        grid_spec=pltpu.PrefetchScalarGridSpec(
            num_scalar_prefetch=1,
            grid=(steps,),
            in_specs=[pl.BlockSpec(memory_space=pl.ANY)] * (2 * count),
            out_specs=(
                pl.BlockSpec((half, heads), lambda k, order: (0, 0)),
                pl.BlockSpec((half, heads), lambda k, order: (0, 0)),
            ),
            scratch_shapes=[
                pltpu.VMEM((steps, rows, span), BF16),
                pltpu.VMEM((steps, span, heads), BF16),
                pltpu.VMEM((rows, heads), F32),
                pltpu.SemaphoreType.DMA((steps,)),
                pltpu.SemaphoreType.DMA((steps,)),
            ],
        ),
        compiler_params=pltpu.CompilerParams(vmem_limit_bytes=52 << 20),
        cost_estimate=BRIEF,
    )(order, *grads, *weights)


def weight_parts(attended, grads, order):
    (count,) = order.shape
    rows, depth = grads[0].shape
    heads, half = attended[0].shape
    tile = 256

    def kernel(order_ref, first, second, *refs):
        g_refs, outs, refs = refs[: len(grads)], refs[len(grads) : -6], refs[-6:]
        a_held, held, done, a_sem, sems, out_sems = refs
        a_copies = [
            pltpu.make_async_copy(first, a_held.at[:, :half], a_sem.at[0]),
            pltpu.make_async_copy(second, a_held.at[:, half:], a_sem.at[1]),
        ]
        for copy in a_copies:
            copy.start()
        for k in range(count):
            fetch_piece(order_ref[k], g_refs, held.at[k], sems.at[k])
        for copy in a_copies:
            copy.wait()
        out_copies = []
        for k in range(count):
            pltpu.make_async_copy(g_refs[0], held.at[k], sems.at[k]).wait()
            for n in range(0, depth, tile):
                block = held[k, :, n : n + tile]
                one = jnp.dot(a_held[...], block, preferred_element_type=F32)
                done[k, :, n : n + tile] = one.astype(BF16)
            out_copies.append(pltpu.make_async_copy(done.at[k], outs[k], out_sems.at[k]))
            out_copies[-1].start()
        for copy in out_copies:
            copy.wait()

    anywhere = pl.BlockSpec(memory_space=pl.ANY)
    return pl.pallas_call(
        kernel,
        out_shape=(jax.ShapeDtypeStruct((heads, depth), BF16),) * count,
        grid_spec=pltpu.PrefetchScalarGridSpec(
            num_scalar_prefetch=1,
            in_specs=[anywhere] * (2 + len(grads)),
            out_specs=(anywhere,) * count,
            scratch_shapes=[
                pltpu.VMEM((heads, rows), BF16),
                pltpu.VMEM((count, rows, depth), BF16),
                pltpu.VMEM((count, heads, depth), BF16),
                pltpu.SemaphoreType.DMA((2,)),
                pltpu.SemaphoreType.DMA((count,)),
                pltpu.SemaphoreType.DMA((count,)),
            ],
        ),
        compiler_params=pltpu.CompilerParams(vmem_limit_bytes=48 << 20),
        cost_estimate=BRIEF,
    )(order, *attended, *grads)


def gate(arrays, *after):
    flat, tree = jax.tree.flatten((arrays, after))
    return jax.tree.unflatten(tree, lax.optimization_barrier(flat))[0]


def body(
    hidden_in,
    out_grad,
    queries,
    keys,
    segment_ids,
    value_codes,
    value_steps,
    output_codes,
    output_steps,
):
    xh, y, c, z, xl = (lax.axis_index(a) for a in SIZES)
    heads, half = output_codes.shape

    others = [(distance, side) for distance in range(4) for side in (0, 1)]

    def chip_at(distance, side):
        return (xh ^ side) * 4 + (y + distance) % 4

    chips = jnp.stack([chip_at(*key) for key in others]).astype(jnp.int32)
    own_order, other_order = chips * 2 + c, chips * 2 + 1 - c

    def piece_at(distance, side):
        chip = chip_at(distance, side)
        return ((chip // 2 - z) % 4) * 2 + ((chip % 2) ^ xl)

    def pieces_at(keys_of):
        return jnp.stack([piece_at(*key) for key in keys_of]).astype(jnp.int32)

    value_weight = lax.all_gather(dequant_rows(value_codes, value_steps), ROWS, axis=0, tiled=True)
    keep = lax.dynamic_slice_in_dim(out_grad, c * half, half, 1)
    give = lax.dynamic_slice_in_dim(out_grad, (1 - c) * half, half, 1)
    grads = jnp.concatenate([keep, shift(give, "c", 1)], axis=0)
    weight = dequant_transposed(output_codes, output_steps)
    grads, weight, queries = gate((grads, weight, queries))

    g, w = {(0, 0): grads}, {(0, 0): weight}
    w[3, 0], w[1, 0] = shift(weight, "y", 1), shift(weight, "y", -1)
    g[3, 0], g[1, 0] = shift(grads, "z", 1), shift(grads, "z", -1)
    g[0, 1] = shift(grads, "xl", 1)
    probs = [attention_probs(queries, keys, segment_ids, h, GQ // 2) for h in (0, GQ // 2)]
    g, w, probs = gate((g, w, probs))

    g[3, 1], g[1, 1] = shift(g[0, 1], "z", 1), shift(g[0, 1], "z", -1)
    w[0, 1] = shift(weight, "xh", 1)
    w[2, 0] = shift(w[3, 0], "y", 1)
    g, w, value_weight, probs = gate((g, w, value_weight, probs))

    w[3, 1], w[1, 1] = shift(w[0, 1], "y", 1), shift(w[0, 1], "y", -1)
    w[2, 1] = shift(w[2, 0], "xh", 1)
    g[2, 0], g[2, 1] = shift(g[3, 0], "z", 1), shift(g[1, 1], "z", -1)
    attended = attended_heads(hidden_in, value_weight, probs)
    g, w, attended, probs = gate((g, w, attended, probs))

    attended = attended, shift(attended, "c", 1)
    pieces = [g[key] for key in others]
    here, there = head_grads(pieces, [w[key] for key in others], pieces_at(others))
    here, there, pieces, attended = gate((here, there, pieces, attended))
    there = shift(there, "c", 1)
    up1, down1, cross = weight_parts(attended, pieces, pieces_at([(1, 1), (3, 1), (2, 1)]))
    here, there, up1, down1, cross = gate((here, there, up1, down1, cross))
    up1, down1, cross = shift(up1, "y", 1), shift(down1, "y", -1), shift(cross, "xh", 1)
    term, term_give = value_terms(hidden_in, here, there, probs, own_order, other_order)
    term, term_give, attended, pieces = gate((term, term_give, attended, pieces))
    far_part, across, up_part, down_part, stay = weight_parts(
        attended, pieces, pieces_at([(2, 0), (0, 1), (1, 0), (3, 0), (0, 0)])
    )
    term, term_give, up1, down1, cross, far_part, across, up_part, down_part, stay = gate(
        (term, term_give, up1, down1, cross, far_part, across, up_part, down_part, stay)
    )

    term = (term + shift(term_give, "c", 1).astype(F32)).reshape(4, 2, HD, half)
    term, term_give = term[:, 0], shift(term[:, 1].astype(BF16), "xh", 1)
    far_part = (far_part.astype(F32) + cross.astype(F32)).astype(BF16)
    low = shift(far_part[: heads // 2], "y", 1)
    high = shift(far_part[heads // 2 :], "y", -1)
    across = (across.astype(F32) + up1.astype(F32) + down1.astype(F32)).astype(BF16)
    low, high, across, up_part, down_part, stay, term, term_give = gate(
        (low, high, across, up_part, down_part, stay, term, term_give)
    )

    across = shift(across, "xh", 1)
    term = term + term_give.astype(F32)
    send = term.astype(BF16)
    low, high = low.astype(F32), high.astype(F32)
    up0, down0 = up_part.astype(F32), down_part.astype(F32)
    up0 = jnp.concatenate(
        [(up0[: heads // 2] + low).astype(BF16), up_part[heads // 2 :], send[1]], axis=0
    )
    down0 = jnp.concatenate(
        [down_part[: heads // 2], (down0[heads // 2 :] + high).astype(BF16), send[3]], axis=0
    )
    up0, down0 = shift(up0, "y", 1), shift(down0, "y", -1)
    term_far = shift(send[2], "y", 2)
    terms = (up0[heads:], down0[heads:], term_far)
    value_step_grad, value_weight_grad = value_grads(term[0], terms, value_codes)
    output_weight_grad = stay.astype(F32) + across.astype(F32)
    output_weight_grad += up0[:heads].astype(F32) + down0[:heads].astype(F32)
    centered_out = (output_codes - 8).astype(F32)
    output_step_grad = (centered_out * output_weight_grad).reshape(-1, GROUP, half).sum(axis=1)
    return (output_step_grad, value_step_grad, output_weight_grad, value_weight_grad)


def solution(mesh):
    fine = Mesh(mesh.devices.reshape(tuple(SIZES.values())), tuple(SIZES))
    return jax.shard_map(
        body,
        mesh=fine,
        in_specs=(
            P(ROWS, None),
            P(ROWS, HEADS_AXES),
            P(ROWS, HEADS_AXES),
            P(ROWS, HEADS_AXES),
            P(ROWS, None),
            P(ROWS, HEADS_AXES),
            P(ROWS, HEADS_AXES),
            P(HEADS_AXES, ROWS),
            P(HEADS_AXES, ROWS),
        ),
        out_specs=(
            P(HEADS_AXES, ROWS),
            P(ROWS, HEADS_AXES),
            P(HEADS_AXES, ROWS),
            P(ROWS, HEADS_AXES),
        ),
        check_vma=False,
    )
```

profile of v0, /device:TPU:1, one launch (start us, length us, event | category | flops | bytes accessed | tf_op | source)
XLA Modules:
  0.0 223.0 jit_solution(16716652302763174381)
XLA Ops:
  7.2 1.3 constant_dynamic-slice_fusion.1
  8.5 1.5 collective-permute-start
  10.0 1.6 shard_map.123
  11.9 2.7 %shard_map.120.refs_8_ = bf16[512,1024]{1,0:T(8,128)(2,1)} custom-call(s32[1024,512]{1,0:T(8,128)} %codes_ref.2, f32[8,512]{1,0:T(8,128)} %steps_ref.2), custom_call_target="tpu_custom_call" | custom-call | flops 1048576 | bytes 65536 | tf_op jit(solution)/shard_map/pallas_call | solution.py:54
  14.6 1.8 collective-permute-start.3
  16.4 2.2 collective-permute-start.2
  18.6 1.2 collective-permute-start.1
  19.8 1.3 collective-permute-start.5
  21.1 1.4 collective-permute-start.4
  22.6 2.9 %shard_map.122.p_high = bf16[4,512,512]{2,1,0:T(8,128)(2,1)S(1)} custom-call(bf16[512,1024]{1,0:T(8,128)(2,1)S(1)} %copy-done.5, bf16[512,128]{1,0:T(8,128)(2,1)S(1)} %copy-done.6, s32[512,1]{1,0:T(8,128)S(1)} %copy.13.down_ref, s32[1,512]{1,0:T(1,128)S(1)} %copy-done.4), custom_call_target="tpu_custom_call" | custom-call | flops 34359738368 | bytes 16777216 | tf_op jit(solution)/shard_map/pallas_call | solution.py:85
  25.5 1.3 copy-done.2
  26.8 2.9 %shard_map.121.p_low = bf16[4,512,512]{2,1,0:T(8,128)(2,1)S(1)} custom-call(bf16[512,1024]{1,0:T(8,128)(2,1)S(1)} %copy-done.5, bf16[512,128]{1,0:T(8,128)(2,1)S(1)} %copy-done.6, s32[512,1]{1,0:T(8,128)S(1)} %copy.13.down_ref, s32[1,512]{1,0:T(1,128)S(1)} %copy-done.4), custom_call_target="tpu_custom_call" | custom-call | flops 34359738368 | bytes 16777216 | tf_op jit(solution)/shard_map/pallas_call | solution.py:85
  29.7 1.3 copy-done.3
  31.0 11.0 %collective-permute-done.3.refs_6_ = bf16[1024,512]{1,0:T(8,128)(2,1)S(1)} collective-permute-done((bf16[1024,512]{1,0:T(8,128)(2,1)S(1)}, bf16[1024,512]{1,0:T(8,128)(2,1)S(1)}, u32[]{:S(2)}, u32[]{:S(2)}) %collective-permute-start.3) | collective-permute-done | bytes 1048608 | tf_op jit(solution)/shard_map/ppermute | solution.py:23
  42.1 2.7 %collective-permute-start.8 = (bf16[512,1024]{1,0:T(8,128)(2,1)S(1)}, bf16[512,1024]{1,0:T(8,128)(2,1)S(1)}, u32[]{:S(2)}, u32[]{:S(2)}) collective-permute-start(bf16[512,1024]{1,0:T(8,128)(2,1)S(1)} %copy-done.16), channel_id=1, source_target_pairs={{0,64},{64,0},{1,65},{65,1},{2,66},{66,2},{3,67},{67,3},{4,68},{68... | collective-permute-start | bytes 3145736 | tf_op jit(solution)/shard_map/ppermute | solution.py:23
  44.8 1.0 copy-done.9
  45.8 1.6 collective-permute-done.5.refs_14_
  47.4 0.9 collective-permute-start.9
  48.4 2.7 %collective-permute-start.6 = (bf16[1024,512]{1,0:T(8,128)(2,1)S(1)}, bf16[1024,512]{1,0:T(8,128)(2,1)S(1)}, u32[]{:S(2)}, u32[]{:S(2)}) collective-permute-start(bf16[1024,512]{1,0:T(8,128)(2,1)S(1)} %collective-permute-done.1.refs_1_), channel_id=1, source_target_pairs={{0,6},{2,0},{4,2},{6,4},{1,7},{3,1},{5,3},{7,5},{8,14},{10,8},{12,... | collective-permute-start | bytes 3145736 | tf_op jit(solution)/shard_map/ppermute | solution.py:23
  51.0 23.7 %collective-permute-done.8.refs_9_ = bf16[512,1024]{1,0:T(8,128)(2,1)S(1)} collective-permute-done((bf16[512,1024]{1,0:T(8,128)(2,1)S(1)}, bf16[512,1024]{1,0:T(8,128)(2,1)S(1)}, u32[]{:S(2)}, u32[]{:S(2)}) %collective-permute-start.8) | collective-permute-done | bytes 1048608 | tf_op jit(solution)/shard_map/ppermute | solution.py:23
  74.8 1.0 copy-done.20
  76.1 1.4 collective-permute-start.14
  77.4 1.5 collective-permute-start.12
  79.0 2.8 %collective-permute-start.11 = (bf16[1024,512]{1,0:T(8,128)(2,1)S(1)}, bf16[1024,512]{1,0:T(8,128)(2,1)S(1)}, u32[]{:S(2)}, u32[]{:S(2)}) collective-permute-start(bf16[1024,512]{1,0:T(8,128)(2,1)S(1)} %collective-permute-done.6.refs_3_), channel_id=1, source_target_pairs={{0,6},{2,0},{4,2},{6,4},{1,7},{3,1},{5,3},{7,5},{8,14},{10,8},{12,... | collective-permute-start | bytes 3145736 | tf_op jit(solution)/shard_map/ppermute | solution.py:23
  81.8 2.8 %collective-permute-start.13 = (bf16[512,1024]{1,0:T(8,128)(2,1)}, bf16[512,1024]{1,0:T(8,128)(2,1)}, u32[]{:S(2)}, u32[]{:S(2)}) collective-permute-start(bf16[512,1024]{1,0:T(8,128)(2,1)} %copy-done.21), channel_id=1, source_target_pairs={{0,64},{64,0},{1,65},{65,1},{2,66},{66,2},{3,67},{67,3},{4,68},{68... | collective-permute-start | bytes 3145736 | tf_op jit(solution)/shard_map/ppermute | solution.py:23
  84.6 10.8 %shard_map.124.first = bf16[1024,512]{1,0:T(8,128)(2,1)} custom-call(bf16[512,8192]{1,0:T(8,128)(2,1)} %h_other.1, bf16[8192,128]{1,0:T(8,128)(2,1)} %all-gather.2.cloned.1.call-done.v_ref, bf16[4,512,512]{2,1,0:T(8,128)(2,1)} %copy-done.3, bf16[4,512,512]{2,1,0:T(8,128)(2,1)} %copy-done.2), custom_call_target="tpu_custom_call" | custom-call | flops 34359738368 | bytes 16777216 | tf_op jit(solution)/shard_map/pallas_call | solution.py:130
  95.4 6.9 %collective-permute-done.11.refs_5_ = bf16[1024,512]{1,0:T(8,128)(2,1)S(1)} collective-permute-done((bf16[1024,512]{1,0:T(8,128)(2,1)S(1)}, bf16[1024,512]{1,0:T(8,128)(2,1)S(1)}, u32[]{:S(2)}, u32[]{:S(2)}) %collective-permute-start.11) | collective-permute-done | bytes 1048608 | tf_op jit(solution)/shard_map/ppermute | solution.py:23
  102.3 3.2 %collective-permute-done.10.refs_4_ = bf16[1024,512]{1,0:T(8,128)(2,1)S(1)} collective-permute-done((bf16[1024,512]{1,0:T(8,128)(2,1)S(1)}, bf16[1024,512]{1,0:T(8,128)(2,1)S(1)}, u32[]{:S(2)}, u32[]{:S(2)}) %collective-permute-start.10) | collective-permute-done | bytes 1048608 | tf_op jit(solution)/shard_map/ppermute | solution.py:23
  107.1 1.0 copy-done.23
  108.1 3.1 %collective-permute-start.15 = (bf16[1024,512]{1,0:T(8,128)(2,1)}, bf16[1024,512]{1,0:T(8,128)(2,1)S(1)}, u32[]{:S(2)}, u32[]{:S(2)}) collective-permute-start(bf16[1024,512]{1,0:T(8,128)(2,1)} %shard_map.124.first), channel_id=1, source_target_pairs={{0,8},{8,0},{1,9},{9,1},{2,10},{10,2},{3,11},{11,3},{4,12},{12,4},... | collective-permute-start | bytes 3145736 | tf_op jit(solution)/shard_map/ppermute | solution.py:23
  111.3 15.3 %shard_map.125 = (f32[512,1024]{1,0:T(8,128)}, bf16[512,1024]{1,0:T(8,128)(2,1)S(1)}) custom-call(s32[8]{0:T(128)S(1)} %stack.85.order_ref, bf16[1024,512]{1,0:T(8,128)(2,1)} %copy-done.7, bf16[1024,512]{1,0:T(8,128)(2,1)} %copy-done.10, bf16[1024,512]{1,0:T(8,128)(2,1)} %copy-done.9, bf16[1024,512]{1,0:T(8,128)(2,1)} %copy-done.12, ...), custom_call_target="tpu_custom_call" | custom-call | flops 1048576 | bytes 65536 | tf_op jit(solution)/shard_map/pallas_call | solution.py:267
  126.9 6.0 %shard_map.126 = (bf16[1024,512]{1,0:T(8,128)(2,1)}, bf16[1024,512]{1,0:T(8,128)(2,1)}, bf16[1024,512]{1,0:T(8,128)(2,1)S(1)}) custom-call(s32[3]{0:T(128)S(1)} %pad_add_fusion.order_ref, bf16[1024,512]{1,0:T(8,128)(2,1)S(1)} %copy-done, bf16[1024,512]{1,0:T(8,128)(2,1)S(1)} %collective-permute-done.15.second, bf16[1024,512]{1,0:T(8,128)(2,1)} %copy-done.7, ...), custom_call_target="tpu_custom_call" | custom-call | flops 1048576 | bytes 65536 | tf_op jit(solution)/shard_map/pallas_call | solution.py:326
  133.0 2.7 %collective-permute-start.18 = (bf16[1024,512]{1,0:T(8,128)(2,1)}, bf16[1024,512]{1,0:T(8,128)(2,1)}, u32[]{:S(2)}, u32[]{:S(2)}) collective-permute-start(bf16[1024,512]{1,0:T(8,128)(2,1)} %get-tuple-element.179), channel_id=1, source_target_pairs={{0,48},{16,0},{32,16},{48,32},{1,49},{17,1},{33,17},{49,33},{2,50}... | collective-permute-start | bytes 3145736 | tf_op jit(solution)/shard_map/ppermute | solution.py:23
  135.7 2.8 %collective-permute-start.19 = (bf16[1024,512]{1,0:T(8,128)(2,1)S(1)}, bf16[1024,512]{1,0:T(8,128)(2,1)S(1)}, u32[]{:S(2)}, u32[]{:S(2)}) collective-permute-start(bf16[1024,512]{1,0:T(8,128)(2,1)S(1)} %get-tuple-element.180), channel_id=1, source_target_pairs={{0,64},{64,0},{1,65},{65,1},{2,66},{66,2},{3,67},{67,3},{4,68},{68... | collective-permute-start | bytes 3145736 | tf_op jit(solution)/shard_map/ppermute | solution.py:23
  139.2 12.3 %shard_map.127 = (f32[8,128,512]{2,1,0:T(8,128)}, bf16[8,128,512]{2,1,0:T(8,128)(2,1)}) custom-call(s32[8]{0:T(128)} %get-tuple-element.228.own_ref, s32[8]{0:T(128)} %get-tuple-element.227.other_ref, bf16[512,8192]{1,0:T(8,128)(2,1)} %h_other.1, bf16[512,8192]{1,0:T(8,128)(2,1)} %h_other.1, f32[512,1024]{1,0:T(8,128)} %get-tuple-element.170.a_ref, ...), custom_call_target="tpu_custom_call" | custom-call | flops 1048576 | bytes 65536 | tf_op jit(solution)/shard_map/pallas_call | solution.py:171
  151.4 10.4 %shard_map.128 = (bf16[1024,512]{1,0:T(8,128)(2,1)S(1)}, bf16[1024,512]{1,0:T(8,128)(2,1)S(1)}, bf16[1024,512]{1,0:T(8,128)(2,1)S(1)}, bf16[1024,512]{1,0:T(8,128)(2,1)S(1)}, bf16[1024,512]{1,0:T(8,128)(2,1)S(1)}) custom-call(s32[5]{0:T(128)S(1)} %stack.87.order_ref, bf16[1024,512]{1,0:T(8,128)(2,1)} %shard_map.124.first, bf16[1024,512]{1,0:T(8,128)(2,1)} %copy-done.1, ...), custom_call_target="tpu_custom_call" | custom-call | flops 1048576 | bytes 65536 | tf_op jit(solution)/shard_map/pallas_call | solution.py:326
  161.9 1.4 collective-permute-start.22
  163.8 1.5 collective-permute-start.20
  166.1 2.4 %collective-permute-start.23 = (bf16[4,128,512]{2,1,0:T(8,128)(2,1)S(1)}, bf16[4,128,512]{2,1,0:T(8,128)(2,1)S(1)}, u32[]{:S(2)}, u32[]{:S(2)}) collective-permute-start(bf16[4,128,512]{2,1,0:T(8,128)(2,1)S(1)} %fusion), channel_id=1, source_target_pairs={{0,64},{64,0},{1,65},{65,1},{2,66},{66,2},{3,67},{67,3},{4,68},{68... | collective-permute-start | bytes 1572872 | tf_op jit(solution)/shard_map/ppermute | solution.py:23
  168.4 2.0 add_convert_fusion
  170.5 6.8 %collective-permute-done.21 = bf16[512,512]{1,0:T(8,128)(2,1)S(1)} collective-permute-done((bf16[512,512]{1,0:T(8,128)(2,1)S(1)}, bf16[512,512]{1,0:T(8,128)(2,1)S(1)}, u32[]{:S(2)}, u32[]{:S(2)}) %collective-permute-start.21) | collective-permute-done | bytes 524320 | tf_op jit(solution)/shard_map/ppermute | solution.py:23
  177.3 1.3 collective-permute-done.20
  178.6 2.2 collective-permute-done.23
  181.7 2.7 %collective-permute-start.26 = (bf16[1152,512]{1,0:T(8,128)(2,1)S(1)}, bf16[1152,512]{1,0:T(8,128)(2,1)S(1)}, u32[]{:S(2)}, u32[]{:S(2)}) collective-permute-start(bf16[1152,512]{1,0:T(8,128)(2,1)S(1)} %pad_maximum_fusion.1), channel_id=1, source_target_pairs={{0,48},{16,0},{32,16},{48,32},{1,49},{17,1},{33,17},{49,33},{2,50}... | collective-permute-start | bytes 3538952 | tf_op jit(solution)/shard_map/ppermute | solution.py:23
  184.4 2.3 %collective-permute-start.24 = (bf16[1024,512]{1,0:T(8,128)(2,1)S(1)}, bf16[1024,512]{1,0:T(8,128)(2,1)S(1)}, u32[]{:S(2)}, u32[]{:S(2)}) collective-permute-start(bf16[1024,512]{1,0:T(8,128)(2,1)S(1)} %add_convert_fusion), channel_id=1, source_target_pairs={{0,64},{64,0},{1,65},{65,1},{2,66},{66,2},{3,67},{67,3},{4,68},{68... | collective-permute-start | bytes 3145736 | tf_op jit(solution)/shard_map/ppermute | solution.py:23
  187.4 21.4 %collective-permute-done.24 = bf16[1024,512]{1,0:T(8,128)(2,1)S(1)} collective-permute-done((bf16[1024,512]{1,0:T(8,128)(2,1)S(1)}, bf16[1024,512]{1,0:T(8,128)(2,1)S(1)}, u32[]{:S(2)}, u32[]{:S(2)}) %collective-permute-start.24) | collective-permute-done | bytes 1048608 | tf_op jit(solution)/shard_map/ppermute | solution.py:23
  209.4 2.7 %bitcast_reduce_fusion = (f32[8,512]{1,0:T(8,128)}, f32[1024,512]{1,0:T(8,128)}) fusion(s32[1024,512]{1,0:T(8,128)S(1)} %copy-done.15, bf16[1152,512]{1,0:T(8,128)(2,1)S(1)} %collective-permute-done.26, bf16[1152,512]{1,0:T(8,128)(2,1)S(1)} %collective-permute-done.25, bf16[1024,512]{1,0:T(8,128)(2,1)S(1)} %collective-permute-done.24, ...), kind=kLoop, calls=%fused_computation | loop fusion | flops 5763072 | bytes 8404992 | tf_op jit(solution)/shard_map/reduce_sum | solution.py:451
  214.1 2.0 shard_map.129
  (101 shorter events, 8.9 us)
Async XLA Ops:
  7.2 4.5 %copy-start.4 = (s32[1,512]{1,0:T(1,128)S(1)}, s32[1,512]{1,0:T(1,128)}, u32[]{:S(2)}) copy-start(s32[1,512]{1,0:T(1,128)} %along_ref.3) | copy-start | bytes 6148
  7.2 68.9 %all-gather.2.cloned.1.call-start = ((), (), s32[]{:S(2)}) async-start(), calls=%async_computation | async-start | bytes 2228224 | tf_op jit(solution)/shard_map/all_gather | solution.py:381
  8.5 6.0 %collective-permute-start = (bf16[512,512]{1,0:T(8,128)(2,1)S(1)}, bf16[512,512]{1,0:T(8,128)(2,1)S(1)}, u32[]{:S(2)}, u32[]{:S(2)}) collective-permute-start(bf16[512,512]{1,0:T(8,128)(2,1)S(1)} %get-tuple-element.223), channel_id=1, source_target_pairs={{0,8},{8,0},{1,9},{9,1},{2,10},{10,2},{3,11},{11,3},{4,12},{12,4},... | collective-permute-start | bytes 1572872 | tf_op jit(solution)/shard_map/ppermute | solution.py:23
  11.8 10.7 %copy-start.5 = (bf16[512,1024]{1,0:T(8,128)(2,1)S(1)}, bf16[512,1024]{1,0:T(8,128)(2,1)}, u32[]{:S(2)}) copy-start(bf16[512,1024]{1,0:T(8,128)(2,1)} %q_ref.1) | copy-start | bytes 3145732
  11.8 10.7 %copy-start.6 = (bf16[512,128]{1,0:T(8,128)(2,1)S(1)}, bf16[512,128]{1,0:T(8,128)(2,1)}, u32[]{:S(2)}) copy-start(bf16[512,128]{1,0:T(8,128)(2,1)} %k_ref.3) | copy-start | bytes 393220
  14.5 5.3 %copy-start.16 = (bf16[512,1024]{1,0:T(8,128)(2,1)S(1)}, bf16[512,1024]{1,0:T(8,128)(2,1)}, u32[]{:S(2)}) copy-start(bf16[512,1024]{1,0:T(8,128)(2,1)} %shard_map.120.refs_8_) | copy-start | bytes 3145732
  14.6 10.8 %copy-start.7 = (bf16[1024,512]{1,0:T(8,128)(2,1)}, bf16[1024,512]{1,0:T(8,128)(2,1)S(1)}, u32[]{:S(2)}) copy-start(bf16[1024,512]{1,0:T(8,128)(2,1)S(1)} %pad_maximum_fusion.2.refs_0_) | copy-start | bytes 3145732
  14.6 27.4 %collective-permute-start.3 = (bf16[1024,512]{1,0:T(8,128)(2,1)S(1)}, bf16[1024,512]{1,0:T(8,128)(2,1)S(1)}, u32[]{:S(2)}, u32[]{:S(2)}) collective-permute-start(bf16[1024,512]{1,0:T(8,128)(2,1)S(1)} %pad_maximum_fusion.2.refs_0_), channel_id=1, source_target_pairs={{0,2},{2,4},{4,6},{6,0},{1,3},{3,5},{5,7},{7,1},{8,10},{10,12},{12... | collective-permute-start | bytes 3145736 | tf_op jit(solution)/shard_map/ppermute | solution.py:23
  16.4 28.4 %collective-permute-start.2 = (bf16[1024,512]{1,0:T(8,128)(2,1)S(1)}, bf16[1024,512]{1,0:T(8,128)(2,1)S(1)}, u32[]{:S(2)}, u32[]{:S(2)}) collective-permute-start(bf16[1024,512]{1,0:T(8,128)(2,1)S(1)} %pad_maximum_fusion.2.refs_0_), channel_id=1, source_target_pairs={{0,6},{2,0},{4,2},{6,4},{1,7},{3,1},{5,3},{7,5},{8,14},{10,8},{12,... | collective-permute-start | bytes 3145736 | tf_op jit(solution)/shard_map/ppermute | solution.py:23
  18.6 26.2 %collective-permute-start.1 = (bf16[1024,512]{1,0:T(8,128)(2,1)S(1)}, bf16[1024,512]{1,0:T(8,128)(2,1)S(1)}, u32[]{:S(2)}, u32[]{:S(2)}) collective-permute-start(bf16[1024,512]{1,0:T(8,128)(2,1)S(1)} %pad_maximum_fusion.2.refs_0_), channel_id=1, source_target_pairs={{0,1},{1,0},{2,3},{3,2},{4,5},{5,4},{6,7},{7,6},{8,9},{9,8},{10,11... | collective-permute-start | bytes 3145736 | tf_op jit(solution)/shard_map/ppermute | solution.py:23
  19.8 27.6 %collective-permute-start.5 = (bf16[512,1024]{1,0:T(8,128)(2,1)S(1)}, bf16[512,1024]{1,0:T(8,128)(2,1)S(1)}, u32[]{:S(2)}, u32[]{:S(2)}) collective-permute-start(bf16[512,1024]{1,0:T(8,128)(2,1)S(1)} %copy-done.16), channel_id=1, source_target_pairs={{0,16},{16,32},{32,48},{48,0},{1,17},{17,33},{33,49},{49,1},{2,18}... | collective-permute-start | bytes 3145736 | tf_op jit(solution)/shard_map/ppermute | solution.py:23
  21.1 26.3 %collective-permute-start.4 = (bf16[512,1024]{1,0:T(8,128)(2,1)S(1)}, bf16[512,1024]{1,0:T(8,128)(2,1)S(1)}, u32[]{:S(2)}, u32[]{:S(2)}) collective-permute-start(bf16[512,1024]{1,0:T(8,128)(2,1)S(1)} %copy-done.16), channel_id=1, source_target_pairs={{0,48},{16,0},{32,16},{48,32},{1,49},{17,1},{33,17},{49,33},{2,50}... | collective-permute-start | bytes 3145736 | tf_op jit(solution)/shard_map/ppermute | solution.py:23
  25.5 1.4 copy-start.2
  42.1 53.4 %copy-start.8 = (bf16[1024,512]{1,0:T(8,128)(2,1)}, bf16[1024,512]{1,0:T(8,128)(2,1)S(1)}, u32[]{:S(2)}) copy-start(bf16[1024,512]{1,0:T(8,128)(2,1)S(1)} %collective-permute-done.3.refs_6_) | copy-start | bytes 3145732
  42.1 32.7 %collective-permute-start.8 = (bf16[512,1024]{1,0:T(8,128)(2,1)S(1)}, bf16[512,1024]{1,0:T(8,128)(2,1)S(1)}, u32[]{:S(2)}, u32[]{:S(2)}) collective-permute-start(bf16[512,1024]{1,0:T(8,128)(2,1)S(1)} %copy-done.16), channel_id=1, source_target_pairs={{0,64},{64,0},{1,65},{65,1},{2,66},{66,2},{3,67},{67,3},{4,68},{68... | collective-permute-start | bytes 3145736 | tf_op jit(solution)/shard_map/ppermute | solution.py:23
  45.8 2.6 %copy-start.10 = (bf16[1024,512]{1,0:T(8,128)(2,1)}, bf16[1024,512]{1,0:T(8,128)(2,1)S(1)}, u32[]{:S(2)}) copy-start(bf16[1024,512]{1,0:T(8,128)(2,1)S(1)} %collective-permute-done.1.refs_1_) | copy-start | bytes 3145732
  47.4 27.4 %copy-start.18 = (bf16[512,1024]{1,0:T(8,128)(2,1)}, bf16[512,1024]{1,0:T(8,128)(2,1)S(1)}, u32[]{:S(2)}) copy-start(bf16[512,1024]{1,0:T(8,128)(2,1)S(1)} %collective-permute-done.5.refs_14_) | copy-start | bytes 3145732
  47.4 27.4 %copy-start.19 = (bf16[512,1024]{1,0:T(8,128)(2,1)}, bf16[512,1024]{1,0:T(8,128)(2,1)S(1)}, u32[]{:S(2)}) copy-start(bf16[512,1024]{1,0:T(8,128)(2,1)S(1)} %collective-permute-done.4.refs_10_) | copy-start | bytes 3145732
  47.4 27.3 %collective-permute-start.9 = (bf16[512,1024]{1,0:T(8,128)(2,1)S(1)}, bf16[512,1024]{1,0:T(8,128)(2,1)S(1)}, u32[]{:S(2)}, u32[]{:S(2)}) collective-permute-start(bf16[512,1024]{1,0:T(8,128)(2,1)S(1)} %collective-permute-done.5.refs_14_), channel_id=1, source_target_pairs={{0,16},{16,32},{32,48},{48,0},{1,17},{17,33},{33,49},{49,1},{2,18}... | collective-permute-start | bytes 3145736 | tf_op jit(solution)/shard_map/ppermute | solution.py:23
  48.3 26.4 %collective-permute-start.7 = (bf16[1024,512]{1,0:T(8,128)(2,1)S(1)}, bf16[1024,512]{1,0:T(8,128)(2,1)S(1)}, u32[]{:S(2)}, u32[]{:S(2)}) collective-permute-start(bf16[1024,512]{1,0:T(8,128)(2,1)S(1)} %collective-permute-done.1.refs_1_), channel_id=1, source_target_pairs={{0,2},{2,4},{4,6},{6,0},{1,3},{3,5},{5,7},{7,1},{8,10},{10,12},{12... | collective-permute-start | bytes 3145736 | tf_op jit(solution)/shard_map/ppermute | solution.py:23
  48.4 27.7 %collective-permute-start.6 = (bf16[1024,512]{1,0:T(8,128)(2,1)S(1)}, bf16[1024,512]{1,0:T(8,128)(2,1)S(1)}, u32[]{:S(2)}, u32[]{:S(2)}) collective-permute-start(bf16[1024,512]{1,0:T(8,128)(2,1)S(1)} %collective-permute-done.1.refs_1_), channel_id=1, source_target_pairs={{0,6},{2,0},{4,2},{6,4},{1,7},{3,1},{5,3},{7,5},{8,14},{10,8},{12,... | collective-permute-start | bytes 3145736 | tf_op jit(solution)/shard_map/ppermute | solution.py:23
  76.1 19.4 %copy-start.11 = (bf16[1024,512]{1,0:T(8,128)(2,1)}, bf16[1024,512]{1,0:T(8,128)(2,1)S(1)}, u32[]{:S(2)}) copy-start(bf16[1024,512]{1,0:T(8,128)(2,1)S(1)} %collective-permute-done.7.refs_7_) | copy-start | bytes 3145732
  76.1 19.4 %copy-start.12 = (bf16[1024,512]{1,0:T(8,128)(2,1)}, bf16[1024,512]{1,0:T(8,128)(2,1)S(1)}, u32[]{:S(2)}) copy-start(bf16[1024,512]{1,0:T(8,128)(2,1)S(1)} %collective-permute-done.6.refs_3_) | copy-start | bytes 3145732
  76.1 30.0 %collective-permute-start.14 = (bf16[512,1024]{1,0:T(8,128)(2,1)}, bf16[512,1024]{1,0:T(8,128)(2,1)S(1)}, u32[]{:S(2)}, u32[]{:S(2)}) collective-permute-start(bf16[512,1024]{1,0:T(8,128)(2,1)} %copy-done.20), channel_id=1, source_target_pairs={{0,16},{16,32},{32,48},{48,0},{1,17},{17,33},{33,49},{49,1},{2,18}... | collective-permute-start | bytes 3145736 | tf_op jit(solution)/shard_map/ppermute | solution.py:23
  77.4 28.6 %collective-permute-start.12 = (bf16[512,1024]{1,0:T(8,128)(2,1)}, bf16[512,1024]{1,0:T(8,128)(2,1)S(1)}, u32[]{:S(2)}, u32[]{:S(2)}) collective-permute-start(bf16[512,1024]{1,0:T(8,128)(2,1)} %copy-done.20), channel_id=1, source_target_pairs={{0,48},{16,0},{32,16},{48,32},{1,49},{17,1},{33,17},{49,33},{2,50}... | collective-permute-start | bytes 3145736 | tf_op jit(solution)/shard_map/ppermute | solution.py:23
  79.0 23.4 %collective-permute-start.11 = (bf16[1024,512]{1,0:T(8,128)(2,1)S(1)}, bf16[1024,512]{1,0:T(8,128)(2,1)S(1)}, u32[]{:S(2)}, u32[]{:S(2)}) collective-permute-start(bf16[1024,512]{1,0:T(8,128)(2,1)S(1)} %collective-permute-done.6.refs_3_), channel_id=1, source_target_pairs={{0,6},{2,0},{4,2},{6,4},{1,7},{3,1},{5,3},{7,5},{8,14},{10,8},{12,... | collective-permute-start | bytes 3145736 | tf_op jit(solution)/shard_map/ppermute | solution.py:23
  81.8 23.8 %collective-permute-start.10 = (bf16[1024,512]{1,0:T(8,128)(2,1)S(1)}, bf16[1024,512]{1,0:T(8,128)(2,1)S(1)}, u32[]{:S(2)}, u32[]{:S(2)}) collective-permute-start(bf16[1024,512]{1,0:T(8,128)(2,1)S(1)} %collective-permute-done.3.refs_6_), channel_id=1, source_target_pairs={{0,2},{2,4},{4,6},{6,0},{1,3},{3,5},{5,7},{7,1},{8,10},{10,12},{12... | collective-permute-start | bytes 3145736 | tf_op jit(solution)/shard_map/ppermute | solution.py:23
  81.8 24.3 %collective-permute-start.13 = (bf16[512,1024]{1,0:T(8,128)(2,1)}, bf16[512,1024]{1,0:T(8,128)(2,1)}, u32[]{:S(2)}, u32[]{:S(2)}) collective-permute-start(bf16[512,1024]{1,0:T(8,128)(2,1)} %copy-done.21), channel_id=1, source_target_pairs={{0,64},{64,0},{1,65},{65,1},{2,66},{66,2},{3,67},{67,3},{4,68},{68... | collective-permute-start | bytes 3145736 | tf_op jit(solution)/shard_map/ppermute | solution.py:23
  102.3 3.7 %copy-start.13 = (bf16[1024,512]{1,0:T(8,128)(2,1)}, bf16[1024,512]{1,0:T(8,128)(2,1)S(1)}, u32[]{:S(2)}) copy-start(bf16[1024,512]{1,0:T(8,128)(2,1)S(1)} %collective-permute-done.11.refs_5_) | copy-start | bytes 3145732
  108.1 18.5 %collective-permute-start.15 = (bf16[1024,512]{1,0:T(8,128)(2,1)}, bf16[1024,512]{1,0:T(8,128)(2,1)S(1)}, u32[]{:S(2)}, u32[]{:S(2)}) collective-permute-start(bf16[1024,512]{1,0:T(8,128)(2,1)} %shard_map.124.first), channel_id=1, source_target_pairs={{0,8},{8,0},{1,9},{9,1},{2,10},{10,2},{3,11},{11,3},{4,12},{12,4},... | collective-permute-start | bytes 3145736 | tf_op jit(solution)/shard_map/ppermute | solution.py:23
  111.3 15.6 %copy-start = (bf16[1024,512]{1,0:T(8,128)(2,1)S(1)}, bf16[1024,512]{1,0:T(8,128)(2,1)}, u32[]{:S(2)}) copy-start(bf16[1024,512]{1,0:T(8,128)(2,1)} %shard_map.124.first) | copy-start | bytes 3145732
  126.6 6.3 %copy-start.1 = (bf16[1024,512]{1,0:T(8,128)(2,1)}, bf16[1024,512]{1,0:T(8,128)(2,1)S(1)}, u32[]{:S(2)}) copy-start(bf16[1024,512]{1,0:T(8,128)(2,1)S(1)} %collective-permute-done.15.second) | copy-start | bytes 3145732
  126.6 6.4 %collective-permute-start.16 = (bf16[512,1024]{1,0:T(8,128)(2,1)S(1)}, bf16[512,1024]{1,0:T(8,128)(2,1)S(1)}, u32[]{:S(2)}, u32[]{:S(2)}) collective-permute-start(bf16[512,1024]{1,0:T(8,128)(2,1)S(1)} %get-tuple-element.156), channel_id=1, source_target_pairs={{0,8},{8,0},{1,9},{9,1},{2,10},{10,2},{3,11},{11,3},{4,12},{12,4},... | collective-permute-start | bytes 3145736 | tf_op jit(solution)/shard_map/ppermute | solution.py:23
  132.9 2.8 %copy-start.24 = (bf16[512,1024]{1,0:T(8,128)(2,1)}, bf16[512,1024]{1,0:T(8,128)(2,1)S(1)}, u32[]{:S(2)}) copy-start(bf16[512,1024]{1,0:T(8,128)(2,1)S(1)} %collective-permute-done.16.b_ref) | copy-start | bytes 3145732
  132.9 28.9 %collective-permute-start.17 = (bf16[1024,512]{1,0:T(8,128)(2,1)}, bf16[1024,512]{1,0:T(8,128)(2,1)}, u32[]{:S(2)}, u32[]{:S(2)}) collective-permute-start(bf16[1024,512]{1,0:T(8,128)(2,1)} %get-tuple-element.178), channel_id=1, source_target_pairs={{0,16},{16,32},{32,48},{48,0},{1,17},{17,33},{33,49},{49,1},{2,18}... | collective-permute-start | bytes 3145736 | tf_op jit(solution)/shard_map/ppermute | solution.py:23
  133.0 28.8 %collective-permute-start.18 = (bf16[1024,512]{1,0:T(8,128)(2,1)}, bf16[1024,512]{1,0:T(8,128)(2,1)}, u32[]{:S(2)}, u32[]{:S(2)}) collective-permute-start(bf16[1024,512]{1,0:T(8,128)(2,1)} %get-tuple-element.179), channel_id=1, source_target_pairs={{0,48},{16,0},{32,16},{48,32},{1,49},{17,1},{33,17},{49,33},{2,50}... | collective-permute-start | bytes 3145736 | tf_op jit(solution)/shard_map/ppermute | solution.py:23
  135.7 26.2 %collective-permute-start.19 = (bf16[1024,512]{1,0:T(8,128)(2,1)S(1)}, bf16[1024,512]{1,0:T(8,128)(2,1)S(1)}, u32[]{:S(2)}, u32[]{:S(2)}) collective-permute-start(bf16[1024,512]{1,0:T(8,128)(2,1)S(1)} %get-tuple-element.180), channel_id=1, source_target_pairs={{0,64},{64,0},{1,65},{65,1},{2,66},{66,2},{3,67},{67,3},{4,68},{68... | collective-permute-start | bytes 3145736 | tf_op jit(solution)/shard_map/ppermute | solution.py:23
  151.4 10.4 %copy-start.26 = (bf16[8,128,512]{2,1,0:T(8,128)(2,1)S(1)}, bf16[8,128,512]{2,1,0:T(8,128)(2,1)}, u32[]{:S(2)}) copy-start(bf16[8,128,512]{2,1,0:T(8,128)(2,1)} %get-tuple-element.205) | copy-start | bytes 3145732
  161.9 3.7 %copy-start.17 = (f32[8,128,512]{2,1,0:T(8,128)S(1)}, f32[8,128,512]{2,1,0:T(8,128)}, u32[]{:S(2)}) copy-start(f32[8,128,512]{2,1,0:T(8,128)} %get-tuple-element.204) | copy-start | bytes 6291460
  161.9 3.7 %collective-permute-start.22 = (bf16[8,128,512]{2,1,0:T(8,128)(2,1)S(1)}, bf16[8,128,512]{2,1,0:T(8,128)(2,1)S(1)}, u32[]{:S(2)}, u32[]{:S(2)}) collective-permute-start(bf16[8,128,512]{2,1,0:T(8,128)(2,1)S(1)} %copy-done.26), channel_id=1, source_target_pairs={{0,8},{8,0},{1,9},{9,1},{2,10},{10,2},{3,11},{11,3},{4,12},{12,4},... | collective-permute-start | bytes 3145736 | tf_op jit(solution)/shard_map/ppermute | solution.py:23
  163.7 13.6 %collective-permute-start.21 = (bf16[512,512]{1,0:T(8,128)(2,1)S(1)}, bf16[512,512]{1,0:T(8,128)(2,1)S(1)}, u32[]{:S(2)}, u32[]{:S(2)}) collective-permute-start(bf16[512,512]{1,0:T(8,128)(2,1)S(1)} %get-tuple-element.220), channel_id=1, source_target_pairs={{0,48},{16,0},{32,16},{48,32},{1,49},{17,1},{33,17},{49,33},{2,50}... | collective-permute-start | bytes 1572872 | tf_op jit(solution)/shard_map/ppermute | solution.py:23
  163.8 14.8 %collective-permute-start.20 = (bf16[512,512]{1,0:T(8,128)(2,1)S(1)}, bf16[512,512]{1,0:T(8,128)(2,1)S(1)}, u32[]{:S(2)}, u32[]{:S(2)}) collective-permute-start(bf16[512,512]{1,0:T(8,128)(2,1)S(1)} %get-tuple-element.221), channel_id=1, source_target_pairs={{0,16},{16,32},{32,48},{48,0},{1,17},{17,33},{33,49},{49,1},{2,18}... | collective-permute-start | bytes 1572872 | tf_op jit(solution)/shard_map/ppermute | solution.py:23
  166.1 14.7 %collective-permute-start.23 = (bf16[4,128,512]{2,1,0:T(8,128)(2,1)S(1)}, bf16[4,128,512]{2,1,0:T(8,128)(2,1)S(1)}, u32[]{:S(2)}, u32[]{:S(2)}) collective-permute-start(bf16[4,128,512]{2,1,0:T(8,128)(2,1)S(1)} %fusion), channel_id=1, source_target_pairs={{0,64},{64,0},{1,65},{65,1},{2,66},{66,2},{3,67},{67,3},{4,68},{68... | collective-permute-start | bytes 1572872 | tf_op jit(solution)/shard_map/ppermute | solution.py:23
  181.4 28.0 %copy-start.15 = (s32[1024,512]{1,0:T(8,128)S(1)}, s32[1024,512]{1,0:T(8,128)}, u32[]{:S(2)}) copy-start(s32[1024,512]{1,0:T(8,128)} %codes_ref.2) | copy-start | bytes 6291460
  181.5 27.9 %collective-permute-start.25 = (bf16[1152,512]{1,0:T(8,128)(2,1)S(1)}, bf16[1152,512]{1,0:T(8,128)(2,1)S(1)}, u32[]{:S(2)}, u32[]{:S(2)}) collective-permute-start(bf16[1152,512]{1,0:T(8,128)(2,1)S(1)} %pad_maximum_fusion), channel_id=1, source_target_pairs={{0,16},{16,32},{32,48},{48,0},{1,17},{17,33},{33,49},{49,1},{2,18}... | collective-permute-start | bytes 3538952 | tf_op jit(solution)/shard_map/ppermute | solution.py:23
  181.7 27.8 %collective-permute-start.26 = (bf16[1152,512]{1,0:T(8,128)(2,1)S(1)}, bf16[1152,512]{1,0:T(8,128)(2,1)S(1)}, u32[]{:S(2)}, u32[]{:S(2)}) collective-permute-start(bf16[1152,512]{1,0:T(8,128)(2,1)S(1)} %pad_maximum_fusion.1), channel_id=1, source_target_pairs={{0,48},{16,0},{32,16},{48,32},{1,49},{17,1},{33,17},{49,33},{2,50}... | collective-permute-start | bytes 3538952 | tf_op jit(solution)/shard_map/ppermute | solution.py:23
  184.4 24.4 %collective-permute-start.24 = (bf16[1024,512]{1,0:T(8,128)(2,1)S(1)}, bf16[1024,512]{1,0:T(8,128)(2,1)S(1)}, u32[]{:S(2)}, u32[]{:S(2)}) collective-permute-start(bf16[1024,512]{1,0:T(8,128)(2,1)S(1)} %add_convert_fusion), channel_id=1, source_target_pairs={{0,64},{64,0},{1,65},{65,1},{2,66},{66,2},{3,67},{67,3},{4,68},{68... | collective-permute-start | bytes 3145736 | tf_op jit(solution)/shard_map/ppermute | solution.py:23
  186.7 26.8 %collective-permute-start.27 = (bf16[128,512]{1,0:T(8,128)(2,1)S(1)}, bf16[128,512]{1,0:T(8,128)(2,1)S(1)}, u32[]{:S(2)}, u32[]{:S(2)}) collective-permute-start(bf16[128,512]{1,0:T(8,128)(2,1)S(1)} %get-tuple-element.224), channel_id=1, source_target_pairs={{0,32},{16,48},{32,0},{48,16},{1,33},{17,49},{33,1},{49,17},{2,34}... | collective-permute-start | bytes 393224 | tf_op jit(solution)/shard_map/ppermute | solution.py:23
  (8 other events, 8.3 us)
Sparse Core Ops, SparseCore 0:
  11.8 58.2 all-gather.1
where the time goes:
time: 227 us; the launch traced here: 223 us
  waiting for transfers between devices  79.8 us (35%)
  Pallas kernels  66.8 us (29%)
  starting transfers between devices  43.6 us (19%)
  between operations  14.5 us (6%)
  local copies, waits for them, and re-layouts  11.6 us (5%)
  other arithmetic  6.69 us (3%)
    ppermute x28, waiting for transfers between devices, shift(): return lax.ppermute(x, axis, [(i, (i + step) % n) for i in range(n)])  79.8 us
    ppermute x28, starting transfers between devices, shift(): return lax.ppermute(x, axis, [(i, (i + step) % n) for i in range(n)])  43.6 us
    pallas_call x2, Pallas kernels, weight_parts(): pl.pallas_call(kernel, out_shape=(jax.ShapeDtypeStruct((heads, depth), BF...  16.3 us
    pallas_call x1, Pallas kernels, head_grads(): pl.pallas_call(kernel, out_shape=(jax.ShapeDtypeStruct((half, heads), F32...  15.3 us
    pallas_call x1, Pallas kernels, value_terms(): pl.pallas_call(kernel, out_shape=(jax.ShapeDtypeStruct((count, HD, width)...  12.3 us
    pallas_call x1, Pallas kernels, attended_heads(): pl.pallas_call(kernel, out_shape=jax.ShapeDtypeStruct((heads * columns, r...  10.8 us
    unnamed x54, local copies, waits for them, and re-layouts  7.62 us
    pallas_call x2, Pallas kernels, attention_probs(): pl.pallas_call(kernel, out_shape=jax.ShapeDtypeStruct((count, length, len...  5.72 us
  transfers between devices with their start and end apart: 29, of which 12 were waited for; matrix products, arithmetic and copies ran while one was open for 4% of the time, Pallas kernels for 29%

commit v1 on v0

--- a/solution.py
+++ b/solution.py
@@ -13,7 +13,6 @@
 HEADS_AXES = ("z", "xl")
 F32 = jnp.float32
 BF16 = jnp.bfloat16
-TOGETHER = 2
 LONG = pl.CostEstimate(flops=1 << 35, bytes_accessed=1 << 24, transcendentals=0)
 BRIEF = pl.CostEstimate(flops=1 << 20, bytes_accessed=1 << 16, transcendentals=0)
 
@@ -145,29 +144,40 @@
 
 
 def value_terms(hidden_in, here, there, probs, own_order, other_order):
-    count = own_order.shape[0]
-    rows, heads = here.shape
+    (count,) = own_order.shape
+    rows = here.shape[0]
     width = hidden_in.shape[1] // (2 * count)
     half = probs[0].shape[0]
 
-    def kernel(own_ref, other_ref, h_own, h_other, a_ref, b_ref, p_low, p_high, *refs):
-        own_out, other_out, grad = refs
-
-        @pl.when(pl.program_id(0) == 0)
-        def _():
-            total = jnp.zeros((rows, HD), F32)
-            for h in range(2 * half):
-                head = slice(h * HD, (h + 1) * HD)
-                attended_grad = (a_ref[:, head] + b_ref[:, head].astype(F32)).astype(BF16)
-                p_ref = (p_low, p_high)[h // half]
-                total += jnp.dot(p_ref[h % half], attended_grad, preferred_element_type=F32)
-            grad[...] = total.T.astype(BF16)
-
-        own_out[0] = jnp.dot(grad[...], h_own[...], preferred_element_type=F32)
-        other = jnp.dot(grad[...], h_other[...], preferred_element_type=F32)
-        other_out[0] = other.astype(BF16)
-
-    whole = pl.BlockSpec(probs[0].shape, lambda k, own, other: (0, 0, 0))
+    def kernel(own_at, other_at, h_ref, a_ref, b_ref, p_low, p_high, *refs):
+        own_out, other_out, held, total, grad, sem = refs
+        fetch = pltpu.make_async_copy(h_ref, held, sem)
+        fetch.start()
+        for h in range(2 * half):
+            head = slice(h * HD, (h + 1) * HD)
+            attended_grad = (a_ref[:, head] + b_ref[:, head].astype(F32)).astype(BF16)
+            more = jnp.dot(
+                (p_low, p_high)[h // half][h % half], attended_grad, preferred_element_type=F32
+            )
+            if h == 0:
+                total[...] = more
+            else:
+                total[...] += more
+        grad[...] = total[...].T.astype(BF16)
+        fetch.wait()
+
+        def one(k, carry):
+            def product(at):
+                block = held[:, pl.ds(pl.multiple_of(at * width, width), width)]
+                return jnp.dot(grad[...], block, preferred_element_type=F32)
+
+            own_out[k] = product(own_at[k])
+            other_out[k] = product(other_at[k]).astype(BF16)
+            return carry
+
+        lax.fori_loop(0, count, one, 0)
+
+    whole = pl.BlockSpec(memory_space=pltpu.VMEM)
     return pl.pallas_call(
         kernel,
         out_shape=(
@@ -176,24 +186,18 @@
         ),
         grid_spec=pltpu.PrefetchScalarGridSpec(
             num_scalar_prefetch=2,
-            grid=(count,),
-            in_specs=[
-                pl.BlockSpec((rows, width), lambda k, own, other: (0, own[k])),
-                pl.BlockSpec((rows, width), lambda k, own, other: (0, other[k])),
-                pl.BlockSpec((rows, heads), lambda k, own, other: (0, 0)),
-                pl.BlockSpec((rows, heads), lambda k, own, other: (0, 0)),
-                whole,
-                whole,
+            in_specs=[pl.BlockSpec(memory_space=pl.ANY)] + [whole] * 4,
+            out_specs=(whole, whole),
+            scratch_shapes=[
+                pltpu.VMEM(hidden_in.shape, BF16),
+                pltpu.VMEM((rows, HD), F32),
+                pltpu.VMEM((HD, rows), BF16),
+                pltpu.SemaphoreType.DMA,
             ],
-            out_specs=(
-                pl.BlockSpec((1, HD, width), lambda k, own, other: (k, 0, 0)),
-                pl.BlockSpec((1, HD, width), lambda k, own, other: (k, 0, 0)),
-            ),
-            scratch_shapes=[pltpu.VMEM((HD, rows), BF16)],
         ),
         compiler_params=pltpu.CompilerParams(vmem_limit_bytes=56 << 20),
         cost_estimate=BRIEF,
-    )(own_order, other_order, hidden_in, hidden_in, here, there, *probs)
+    )(own_order, other_order, hidden_in, here, there, *probs)
 
 
 def value_grads(own, others, codes):
@@ -229,66 +233,81 @@
             pltpu.make_async_copy(piece, target, sem).start()
 
 
-def head_grads(grads, weights, order):
-    count = len(weights)
-    rows, depth = grads[0].shape
-    heads = weights[0].shape[1]
+def head_grads(grads, weights, which, use, so_far=None):
+    count, numbers = len(weights), list(grads)
+    (rows, depth), heads = grads[numbers[0]].shape, weights[0].shape[1]
     half = rows // 2
-    steps = count // TOGETHER
-    span = depth * TOGETHER
-
-    def kernel(order_ref, *refs):
-        g_refs, w_refs, refs = refs[:count], refs[count : 2 * count], refs[2 * count :]
-        own, other, g_held, w_held, total, g_sems, w_sems = refs
-        k = pl.program_id(0)
-
-        def blocks(step):
-            for i in range(TOGETHER):
-                at = slice(i * depth, (i + 1) * depth)
-                yield step * TOGETHER + i, g_held.at[step, :, at], w_held.at[step, at, :]
-
-        @pl.when(k == 0)
-        def _():
-            for step in range(steps):
-                for i, g_at, w_at in blocks(step):
-                    fetch_piece(order_ref[i], g_refs, g_at, g_sems.at[step])
-                    pltpu.make_async_copy(w_refs[i], w_at, w_sems.at[step]).start()
+    last = so_far is not None
+
+    def kernel(which_ref, use_ref, *refs):
+        g_refs, refs = refs[: len(grads)], refs[len(grads) :]
+        w_refs, refs = refs[:count], refs[count:]
+        g_held, w_held, g_sems, w_sems = refs[-4:]
+        if last:
+            before, own, other, total, sem = refs[:-4]
+            start = pltpu.make_async_copy(before, total, sem)
+            start.start()
+        else:
+            (total,) = refs[:-4]
+        for k in range(count):
+
+            @pl.when(use_ref[k] == 1)
+            def _():
+                for number, g_ref in zip(numbers, g_refs):
+
+                    @pl.when(which_ref[k] == number)
+                    def _():
+                        pltpu.make_async_copy(g_ref, g_held.at[k], g_sems.at[k]).start()
+
+                pltpu.make_async_copy(w_refs[k], w_held.at[k], w_sems.at[k]).start()
+
+        if last:
+            start.wait()
+        else:
             total[...] = jnp.zeros_like(total)
 
-        pltpu.make_async_copy(g_held.at[k], g_held.at[k], g_sems.at[k]).wait()
-        pltpu.make_async_copy(w_held.at[k], w_held.at[k], w_sems.at[k]).wait()
-        total[...] += jnp.dot(g_held[k], w_held[k], preferred_element_type=F32)
-
-        @pl.when(k == steps - 1)
-        def _():
+        def one(k, carry):
+            @pl.when(use_ref[k] == 1)
+            def _():
+                pltpu.make_async_copy(g_refs[0], g_held.at[k], g_sems.at[k]).wait()
+                pltpu.make_async_copy(w_refs[0], w_held.at[k], w_sems.at[k]).wait()
+                total[...] += jnp.dot(g_held[k], w_held[k], preferred_element_type=F32)
+
+            return carry
+
+        lax.fori_loop(0, count, one, 0)
+        if last:
             own[...] = total[:half]
             other[...] = total[half:].astype(BF16)
 
-    return pl.pallas_call(
-        kernel,
-        out_shape=(
+    whole = pl.BlockSpec(memory_space=pltpu.VMEM)
+    anywhere = pl.BlockSpec(memory_space=pl.ANY)
+    scratch = [
+        pltpu.VMEM((count, rows, depth), BF16),
+        pltpu.VMEM((count, depth, heads), BF16),
+        pltpu.SemaphoreType.DMA((count,)),
+        pltpu.SemaphoreType.DMA((count,)),
+    ]
+    if last:
+        scratch = [pltpu.VMEM((rows, heads), F32), pltpu.SemaphoreType.DMA] + scratch
+        out_shape = (
             jax.ShapeDtypeStruct((half, heads), F32),
             jax.ShapeDtypeStruct((half, heads), BF16),
-        ),
+        )
+    else:
+        out_shape = jax.ShapeDtypeStruct((rows, heads), F32)
+    return pl.pallas_call(
+        kernel,
+        out_shape=out_shape,
         grid_spec=pltpu.PrefetchScalarGridSpec(
-            num_scalar_prefetch=1,
-            grid=(steps,),
-            in_specs=[pl.BlockSpec(memory_space=pl.ANY)] * (2 * count),
-            out_specs=(
-                pl.BlockSpec((half, heads), lambda k, order: (0, 0)),
-                pl.BlockSpec((half, heads), lambda k, order: (0, 0)),
-            ),
-            scratch_shapes=[
-                pltpu.VMEM((steps, rows, span), BF16),
-                pltpu.VMEM((steps, span, heads), BF16),
-                pltpu.VMEM((rows, heads), F32),
-                pltpu.SemaphoreType.DMA((steps,)),
-                pltpu.SemaphoreType.DMA((steps,)),
-            ],
+            num_scalar_prefetch=2,
+            in_specs=[anywhere] * (len(grads) + count + last),
+            out_specs=(whole, whole) if last else whole,
+            scratch_shapes=scratch,
         ),
         compiler_params=pltpu.CompilerParams(vmem_limit_bytes=52 << 20),
         cost_estimate=BRIEF,
-    )(order, *grads, *weights)
+    )(which, use, *grads.values(), *weights, *([so_far] if last else []))
 
 
 def weight_parts(attended, grads, order):
@@ -401,11 +420,24 @@
     w[2, 1] = shift(w[2, 0], "xh", 1)
     g[2, 0], g[2, 1] = shift(g[3, 0], "z", 1), shift(g[1, 1], "z", -1)
     attended = attended_heads(hidden_in, value_weight, probs)
-    g, w, attended, probs = gate((g, w, attended, probs))
+
+    early = [(0, 0), (1, 0), (2, 0), (3, 0), (0, 1)]
+    at_hand = {2 * d + s: g[d, s] for d, s in others if d != 2}
+    at_hand, early_weights, attended = gate((at_hand, [w[key] for key in early], attended))
+    use = (pieces_at(early) // 2 != 2).astype(jnp.int32)
+    so_far = head_grads(at_hand, early_weights, pieces_at(early), use)
+    g, w, attended, probs, so_far = gate((g, w, attended, probs, so_far))
 
     attended = attended, shift(attended, "c", 1)
     pieces = [g[key] for key in others]
-    here, there = head_grads(pieces, [w[key] for key in others], pieces_at(others))
+    use = jnp.stack([jnp.where(key in early, piece_at(*key) // 2 == 2, True) for key in others])
+    here, there = head_grads(
+        dict(enumerate(pieces)),
+        [w[key] for key in others],
+        pieces_at(others),
+        use.astype(jnp.int32),
+        so_far,
+    )
     here, there, pieces, attended = gate((here, there, pieces, attended))
     there = shift(there, "c", 1)
     up1, down1, cross = weight_parts(attended, pieces, pieces_at([(1, 1), (3, 1), (2, 1)]))

time: 227 us -> 223 us (0.982)
  waiting for transfers between devices: 79.8 us -> 68.1 us
  Pallas kernels: 66.8 us -> 71 us
  starting transfers between devices: 43.6 us -> 47.1 us
    ppermute x28, waiting for transfers between devices: 79.8 us -> 68.1 us  [shift(): return lax.ppermute(x, axis, [(i, (i + step) % n) for i in range(n)])]
    pallas_call x1 -> x2, Pallas kernels: 15.3 us -> 20.4 us  [head_grads(): pl.pallas_call(kernel, out_shape=out_shape, grid_spec=pltpu.PrefetchScala...]
    ppermute x28, starting transfers between devices: 43.6 us -> 47.1 us  [shift(): return lax.ppermute(x, axis, [(i, (i + step) % n) for i in range(n)])]
    unnamed x54 -> x42, local copies, waits for them, and re-layouts: 7.62 us -> 7.9 us
  transfers between devices with their start and end apart: 29 -> 29, of which waited for: 12 -> 11; matrix products, arithmetic and copies ran while one was open for 4% -> 4% of each run, Pallas kernels for 29% -> 31%
where the time goes in v1:
time: 223 us; the launch traced here: 220 us
  Pallas kernels  71 us (32%)
  waiting for transfers between devices  68.1 us (31%)
  starting transfers between devices  47.1 us (21%)
  between operations  14.5 us (7%)
  local copies, waits for them, and re-layouts  12.1 us (5%)
  other arithmetic  6.75 us (3%)
    ppermute x28, waiting for transfers between devices, shift(): return lax.ppermute(x, axis, [(i, (i + step) % n) for i in range(n)])  68.1 us
    ppermute x28, starting transfers between devices, shift(): return lax.ppermute(x, axis, [(i, (i + step) % n) for i in range(n)])  47.1 us
    pallas_call x2, Pallas kernels, head_grads(): pl.pallas_call(kernel, out_shape=out_shape, grid_spec=pltpu.PrefetchScala...  20.4 us
    pallas_call x2, Pallas kernels, weight_parts(): pl.pallas_call(kernel, out_shape=(jax.ShapeDtypeStruct((heads, depth), BF...  16.4 us
    pallas_call x1, Pallas kernels, value_terms(): pl.pallas_call(kernel, out_shape=(jax.ShapeDtypeStruct((count, HD, width)...  11.3 us
    pallas_call x1, Pallas kernels, attended_heads(): pl.pallas_call(kernel, out_shape=jax.ShapeDtypeStruct((heads * columns, r...  10.9 us
    unnamed x42, local copies, waits for them, and re-layouts  7.9 us
    pallas_call x2, Pallas kernels, attention_probs(): pl.pallas_call(kernel, out_shape=jax.ShapeDtypeStruct((count, length, len...  5.72 us
  transfers between devices with their start and end apart: 29, of which 11 were waited for; matrix products, arithmetic and copies ran while one was open for 4% of the time, Pallas kernels for 31%

profile of v1, /device:TPU:1, one launch (start us, length us, event | category | flops | bytes accessed | tf_op | source)
XLA Modules:
  0.0 219.6 jit_solution(5770274200576481327)
XLA Ops:
  7.2 1.3 constant_dynamic-slice_fusion.1
  8.5 1.5 collective-permute-start
  10.0 1.6 shard_map.123
  11.9 2.7 %shard_map.120.refs_6_.refs_8_ = bf16[512,1024]{1,0:T(8,128)(2,1)} custom-call(s32[1024,512]{1,0:T(8,128)} %codes_ref.2, f32[8,512]{1,0:T(8,128)} %steps_ref.2), custom_call_target="tpu_custom_call" | custom-call | flops 1048576 | bytes 65536 | tf_op jit(solution)/shard_map/pallas_call | solution.py:53
  14.7 1.8 collective-permute-start.3
  16.5 2.2 %collective-permute-start.2 = (bf16[1024,512]{1,0:T(8,128)(2,1)S(1)}, bf16[1024,512]{1,0:T(8,128)(2,1)S(1)}, u32[]{:S(2)}, u32[]{:S(2)}) collective-permute-start(bf16[1024,512]{1,0:T(8,128)(2,1)S(1)} %pad_maximum_fusion.2.refs_0_), channel_id=1, source_target_pairs={{0,6},{2,0},{4,2},{6,4},{1,7},{3,1},{5,3},{7,5},{8,14},{10,8},{12,... | collective-permute-start | bytes 3145736 | tf_op jit(solution)/shard_map/ppermute | solution.py:22
  18.7 1.2 collective-permute-start.1
  19.9 1.3 collective-permute-start.5
  21.2 1.4 collective-permute-start.4
  22.6 2.9 %shard_map.122.p_high = bf16[4,512,512]{2,1,0:T(8,128)(2,1)S(1)} custom-call(bf16[512,1024]{1,0:T(8,128)(2,1)S(1)} %copy-done.6, bf16[512,128]{1,0:T(8,128)(2,1)S(1)} %copy-done.7, s32[512,1]{1,0:T(8,128)S(1)} %copy.13.down_ref, s32[1,512]{1,0:T(1,128)S(1)} %copy-done.5), custom_call_target="tpu_custom_call" | custom-call | flops 34359738368 | bytes 16777216 | tf_op jit(solution)/shard_map/pallas_call | solution.py:84
  25.5 1.4 copy-done.3
  26.9 2.9 %shard_map.121.p_low = bf16[4,512,512]{2,1,0:T(8,128)(2,1)S(1)} custom-call(bf16[512,1024]{1,0:T(8,128)(2,1)S(1)} %copy-done.6, bf16[512,128]{1,0:T(8,128)(2,1)S(1)} %copy-done.7, s32[512,1]{1,0:T(8,128)S(1)} %copy.13.down_ref, s32[1,512]{1,0:T(1,128)S(1)} %copy-done.5), custom_call_target="tpu_custom_call" | custom-call | flops 34359738368 | bytes 16777216 | tf_op jit(solution)/shard_map/pallas_call | solution.py:84
  29.7 1.4 copy-done.4
  31.1 11.1 %collective-permute-done.3.refs_4_.refs_6_ = bf16[1024,512]{1,0:T(8,128)(2,1)S(1)} collective-permute-done((bf16[1024,512]{1,0:T(8,128)(2,1)S(1)}, bf16[1024,512]{1,0:T(8,128)(2,1)S(1)}, u32[]{:S(2)}, u32[]{:S(2)}) %collective-permute-start.3) | collective-permute-done | bytes 1048608 | tf_op jit(solution)/shard_map/ppermute | solution.py:22
  42.2 2.7 %collective-permute-start.8 = (bf16[512,1024]{1,0:T(8,128)(2,1)}, bf16[512,1024]{1,0:T(8,128)(2,1)}, u32[]{:S(2)}, u32[]{:S(2)}) collective-permute-start(bf16[512,1024]{1,0:T(8,128)(2,1)} %shard_map.120.refs_6_.refs_8_), channel_id=1, source_target_pairs={{0,64},{64,0},{1,65},{65,1},{2,66},{66,2},{3,67},{67,3},{4,68},{68... | collective-permute-start | bytes 3145736 | tf_op jit(solution)/shard_map/ppermute | solution.py:22
  45.0 1.0 copy-done.9
  46.0 1.8 collective-permute-done.5.refs_9_.refs_14_
  47.8 1.0 copy-done.14
  48.8 0.9 collective-permute-start.9
  49.7 2.7 %collective-permute-start.6 = (bf16[1024,512]{1,0:T(8,128)(2,1)}, bf16[1024,512]{1,0:T(8,128)(2,1)}, u32[]{:S(2)}, u32[]{:S(2)}) collective-permute-start(bf16[1024,512]{1,0:T(8,128)(2,1)} %collective-permute-done.1.refs_1_), channel_id=1, source_target_pairs={{0,6},{2,0},{4,2},{6,4},{1,7},{3,1},{5,3},{7,5},{8,14},{10,8},{12,... | collective-permute-start | bytes 3145736 | tf_op jit(solution)/shard_map/ppermute | solution.py:22
  52.5 22.4 %collective-permute-done.8.refs_10_.refs_9_ = bf16[512,1024]{1,0:T(8,128)(2,1)} collective-permute-done((bf16[512,1024]{1,0:T(8,128)(2,1)}, bf16[512,1024]{1,0:T(8,128)(2,1)}, u32[]{:S(2)}, u32[]{:S(2)}) %collective-permute-start.8) | collective-permute-done | bytes 1048608 | tf_op jit(solution)/shard_map/ppermute | solution.py:22
  75.4 0.9 collective-permute-start.14
  76.3 1.8 collective-permute-start.12
  78.2 2.3 %collective-permute-start.11 = (bf16[1024,512]{1,0:T(8,128)(2,1)}, bf16[1024,512]{1,0:T(8,128)(2,1)S(1)}, u32[]{:S(2)}, u32[]{:S(2)}) collective-permute-start(bf16[1024,512]{1,0:T(8,128)(2,1)} %collective-permute-done.6.refs_3_), channel_id=1, source_target_pairs={{0,6},{2,0},{4,2},{6,4},{1,7},{3,1},{5,3},{7,5},{8,14},{10,8},{12,... | collective-permute-start | bytes 3145736 | tf_op jit(solution)/shard_map/ppermute | solution.py:22
  80.5 2.6 %collective-permute-start.13 = (bf16[512,1024]{1,0:T(8,128)(2,1)}, bf16[512,1024]{1,0:T(8,128)(2,1)}, u32[]{:S(2)}, u32[]{:S(2)}) collective-permute-start(bf16[512,1024]{1,0:T(8,128)(2,1)} %collective-permute-done.9.refs_8_.refs_12_), channel_id=1, source_target_pairs={{0,64},{64,0},{1,65},{65,1},{2,66},{66,2},{3,67},{67,3},{4,68},{68... | collective-permute-start | bytes 3145736 | tf_op jit(solution)/shard_map/ppermute | solution.py:22
  83.1 10.9 %shard_map.124.first = bf16[1024,512]{1,0:T(8,128)(2,1)} custom-call(bf16[512,8192]{1,0:T(8,128)(2,1)} %h_ref.3, bf16[8192,128]{1,0:T(8,128)(2,1)} %all-gather.2.cloned.1.call-done.v_ref, bf16[4,512,512]{2,1,0:T(8,128)(2,1)} %copy-done.4, bf16[4,512,512]{2,1,0:T(8,128)(2,1)} %copy-done.3), custom_call_target="tpu_custom_call" | custom-call | flops 34359738368 | bytes 16777216 | tf_op jit(solution)/shard_map/pallas_call | solution.py:129
  94.0 9.0 %shard_map.125.refs_16_ = f32[1024,1024]{1,0:T(8,128)} custom-call(s32[5]{0:T(128)S(1)} %stack.127.which_ref, s32[5]{0:T(128)S(1)} %compare_convert_fusion.use_ref, bf16[1024,512]{1,0:T(8,128)(2,1)S(1)} %pad_maximum_fusion.2.refs_0_, bf16[1024,512]{1,0:T(8,128)(2,1)} %collective-permute-done.1.refs_1_, bf16[1024,512]{1,0:T(8,128)(2,1)} %copy-done.9, ...), custom_call_target="tpu_custom_call" | custom-call | flops 1048576 | bytes 65536 | tf_op jit(solution)/shard_map/pallas_call | solution.py:299
  105.0 1.0 copy-done.18
  106.0 3.9 %collective-permute-start.15 = (bf16[1024,512]{1,0:T(8,128)(2,1)S(1)}, bf16[1024,512]{1,0:T(8,128)(2,1)S(1)}, u32[]{:S(2)}, u32[]{:S(2)}) collective-permute-start(bf16[1024,512]{1,0:T(8,128)(2,1)S(1)} %copy-done.1), channel_id=1, source_target_pairs={{0,8},{8,0},{1,9},{9,1},{2,10},{10,2},{3,11},{11,3},{4,12},{12,4},... | collective-permute-start | bytes 3145736 | tf_op jit(solution)/shard_map/ppermute | solution.py:22
  110.1 11.4 %shard_map.126 = (f32[512,1024]{1,0:T(8,128)}, bf16[512,1024]{1,0:T(8,128)(2,1)S(1)}) custom-call(s32[8]{0:T(128)S(1)} %stack.120.which_ref, s32[8]{0:T(128)S(1)} %convert_element_type.70.use_ref, bf16[1024,512]{1,0:T(8,128)(2,1)} %copy-done, bf16[1024,512]{1,0:T(8,128)(2,1)} %collective-permute-done.1.refs_1_, bf16[1024,512]{1,0:T(8,128)(2,1)} %copy-done.9, ...), custom_call_target="tpu_custom_call" | custom-call | flops 1048576 | bytes 65536 | tf_op jit(solution)/shard_map/pallas_call | solution.py:299
  121.9 6.0 %shard_map.127 = (bf16[1024,512]{1,0:T(8,128)(2,1)}, bf16[1024,512]{1,0:T(8,128)(2,1)}, bf16[1024,512]{1,0:T(8,128)(2,1)S(1)}) custom-call(s32[3]{0:T(128)S(1)} %pad_add_fusion.order_ref, bf16[1024,512]{1,0:T(8,128)(2,1)S(1)} %copy-done.1, bf16[1024,512]{1,0:T(8,128)(2,1)S(1)} %collective-permute-done.15.second, bf16[1024,512]{1,0:T(8,128)(2,1)} %copy-done, ...), custom_call_target="tpu_custom_call" | custom-call | flops 1048576 | bytes 65536 | tf_op jit(solution)/shard_map/pallas_call | solution.py:345
  128.0 2.7 %collective-permute-start.18 = (bf16[1024,512]{1,0:T(8,128)(2,1)}, bf16[1024,512]{1,0:T(8,128)(2,1)}, u32[]{:S(2)}, u32[]{:S(2)}) collective-permute-start(bf16[1024,512]{1,0:T(8,128)(2,1)} %get-tuple-element.205), channel_id=1, source_target_pairs={{0,48},{16,0},{32,16},{48,32},{1,49},{17,1},{33,17},{49,33},{2,50}... | collective-permute-start | bytes 3145736 | tf_op jit(solution)/shard_map/ppermute | solution.py:22
  130.6 4.7 %collective-permute-start.19 = (bf16[1024,512]{1,0:T(8,128)(2,1)S(1)}, bf16[1024,512]{1,0:T(8,128)(2,1)S(1)}, u32[]{:S(2)}, u32[]{:S(2)}) collective-permute-start(bf16[1024,512]{1,0:T(8,128)(2,1)S(1)} %get-tuple-element.206), channel_id=1, source_target_pairs={{0,64},{64,0},{1,65},{65,1},{2,66},{66,2},{3,67},{67,3},{4,68},{68... | collective-permute-start | bytes 3145736 | tf_op jit(solution)/shard_map/ppermute | solution.py:22
  136.1 11.3 %shard_map.128 = (f32[8,128,512]{2,1,0:T(8,128)}, bf16[8,128,512]{2,1,0:T(8,128)(2,1)}) custom-call(s32[8]{0:T(128)} %get-tuple-element.254.own_at, s32[8]{0:T(128)} %get-tuple-element.253.other_at, bf16[512,8192]{1,0:T(8,128)(2,1)} %h_ref.3, f32[512,1024]{1,0:T(8,128)} %get-tuple-element.196.a_ref, bf16[512,1024]{1,0:T(8,128)(2,1)} %copy-done.16, ...), custom_call_target="tpu_custom_call" | custom-call | flops 1048576 | bytes 65536 | tf_op jit(solution)/shard_map/pallas_call | solution.py:181
  147.4 10.4 %shard_map.129 = (bf16[1024,512]{1,0:T(8,128)(2,1)S(1)}, bf16[1024,512]{1,0:T(8,128)(2,1)S(1)}, bf16[1024,512]{1,0:T(8,128)(2,1)S(1)}, bf16[1024,512]{1,0:T(8,128)(2,1)S(1)}, bf16[1024,512]{1,0:T(8,128)(2,1)S(1)}) custom-call(s32[5]{0:T(128)S(1)} %stack.129.order_ref, bf16[1024,512]{1,0:T(8,128)(2,1)} %shard_map.124.first, bf16[1024,512]{1,0:T(8,128)(2,1)} %copy-done.2, ...), custom_call_target="tpu_custom_call" | custom-call | flops 1048576 | bytes 65536 | tf_op jit(solution)/shard_map/pallas_call | solution.py:345
  157.8 1.7 collective-permute-start.22
  160.0 1.5 collective-permute-start.20
  162.3 3.0 %collective-permute-start.23 = (bf16[4,128,512]{2,1,0:T(8,128)(2,1)S(1)}, bf16[4,128,512]{2,1,0:T(8,128)(2,1)S(1)}, u32[]{:S(2)}, u32[]{:S(2)}) collective-permute-start(bf16[4,128,512]{2,1,0:T(8,128)(2,1)S(1)} %fusion), channel_id=1, source_target_pairs={{0,64},{64,0},{1,65},{65,1},{2,66},{66,2},{3,67},{67,3},{4,68},{68... | collective-permute-start | bytes 1572872 | tf_op jit(solution)/shard_map/ppermute | solution.py:22
  165.3 2.0 add_convert_fusion
  167.4 6.1 %collective-permute-done.21 = bf16[512,512]{1,0:T(8,128)(2,1)S(1)} collective-permute-done((bf16[512,512]{1,0:T(8,128)(2,1)S(1)}, bf16[512,512]{1,0:T(8,128)(2,1)S(1)}, u32[]{:S(2)}, u32[]{:S(2)}) %collective-permute-start.21) | collective-permute-done | bytes 524320 | tf_op jit(solution)/shard_map/ppermute | solution.py:22
  173.5 1.1 collective-permute-done.20
  174.6 2.4 %collective-permute-done.23 = bf16[4,128,512]{2,1,0:T(8,128)(2,1)S(1)} collective-permute-done((bf16[4,128,512]{2,1,0:T(8,128)(2,1)S(1)}, bf16[4,128,512]{2,1,0:T(8,128)(2,1)S(1)}, u32[]{:S(2)}, u32[]{:S(2)}) %collective-permute-start.23) | collective-permute-done | bytes 524320 | tf_op jit(solution)/shard_map/ppermute | solution.py:22
  177.9 2.7 %collective-permute-start.26 = (bf16[1152,512]{1,0:T(8,128)(2,1)S(1)}, bf16[1152,512]{1,0:T(8,128)(2,1)S(1)}, u32[]{:S(2)}, u32[]{:S(2)}) collective-permute-start(bf16[1152,512]{1,0:T(8,128)(2,1)S(1)} %pad_maximum_fusion.1), channel_id=1, source_target_pairs={{0,48},{16,0},{32,16},{48,32},{1,49},{17,1},{33,17},{49,33},{2,50}... | collective-permute-start | bytes 3538952 | tf_op jit(solution)/shard_map/ppermute | solution.py:22
  180.6 3.0 %collective-permute-start.24 = (bf16[1024,512]{1,0:T(8,128)(2,1)S(1)}, bf16[1024,512]{1,0:T(8,128)(2,1)S(1)}, u32[]{:S(2)}, u32[]{:S(2)}) collective-permute-start(bf16[1024,512]{1,0:T(8,128)(2,1)S(1)} %add_convert_fusion), channel_id=1, source_target_pairs={{0,64},{64,0},{1,65},{65,1},{2,66},{66,2},{3,67},{67,3},{4,68},{68... | collective-permute-start | bytes 3145736 | tf_op jit(solution)/shard_map/ppermute | solution.py:22
  184.3 20.7 %collective-permute-done.24 = bf16[1024,512]{1,0:T(8,128)(2,1)S(1)} collective-permute-done((bf16[1024,512]{1,0:T(8,128)(2,1)S(1)}, bf16[1024,512]{1,0:T(8,128)(2,1)S(1)}, u32[]{:S(2)}, u32[]{:S(2)}) %collective-permute-start.24) | collective-permute-done | bytes 1048608 | tf_op jit(solution)/shard_map/ppermute | solution.py:22
  205.0 1.0 collective-permute-done.25
  206.0 2.7 %bitcast_reduce_fusion = (f32[8,512]{1,0:T(8,128)}, f32[1024,512]{1,0:T(8,128)}) fusion(s32[1024,512]{1,0:T(8,128)S(1)} %copy-done.13, bf16[1152,512]{1,0:T(8,128)(2,1)S(1)} %collective-permute-done.26, bf16[1152,512]{1,0:T(8,128)(2,1)S(1)} %collective-permute-done.25, bf16[1024,512]{1,0:T(8,128)(2,1)S(1)} %collective-permute-done.24, ...), kind=kLoop, calls=%fused_computation | loop fusion | flops 5763072 | bytes 8404992 | tf_op jit(solution)/shard_map/reduce_sum | solution.py:483
  210.7 2.0 shard_map.130
  (94 shorter events, 9.1 us)
Async XLA Ops:
  7.2 4.5 %copy-start.5 = (s32[1,512]{1,0:T(1,128)S(1)}, s32[1,512]{1,0:T(1,128)}, u32[]{:S(2)}) copy-start(s32[1,512]{1,0:T(1,128)} %along_ref.3) | copy-start | bytes 6148
  7.2 68.3 %all-gather.2.cloned.1.call-start = ((), (), s32[]{:S(2)}) async-start(), calls=%async_computation | async-start | bytes 2228224 | tf_op jit(solution)/shard_map/all_gather | solution.py:400
  8.5 6.1 %collective-permute-start = (bf16[512,512]{1,0:T(8,128)(2,1)S(1)}, bf16[512,512]{1,0:T(8,128)(2,1)S(1)}, u32[]{:S(2)}, u32[]{:S(2)}) collective-permute-start(bf16[512,512]{1,0:T(8,128)(2,1)S(1)} %get-tuple-element.249), channel_id=1, source_target_pairs={{0,8},{8,0},{1,9},{9,1},{2,10},{10,2},{3,11},{11,3},{4,12},{12,4},... | collective-permute-start | bytes 1572872 | tf_op jit(solution)/shard_map/ppermute | solution.py:22
  11.8 10.8 %copy-start.6 = (bf16[512,1024]{1,0:T(8,128)(2,1)S(1)}, bf16[512,1024]{1,0:T(8,128)(2,1)}, u32[]{:S(2)}) copy-start(bf16[512,1024]{1,0:T(8,128)(2,1)} %q_ref.1) | copy-start | bytes 3145732
  11.8 10.8 %copy-start.7 = (bf16[512,128]{1,0:T(8,128)(2,1)S(1)}, bf16[512,128]{1,0:T(8,128)(2,1)}, u32[]{:S(2)}) copy-start(bf16[512,128]{1,0:T(8,128)(2,1)} %k_ref.3) | copy-start | bytes 393220
  14.7 79.3 %copy-start = (bf16[1024,512]{1,0:T(8,128)(2,1)}, bf16[1024,512]{1,0:T(8,128)(2,1)S(1)}, u32[]{:S(2)}) copy-start(bf16[1024,512]{1,0:T(8,128)(2,1)S(1)} %pad_maximum_fusion.2.refs_0_) | copy-start | bytes 3145732
  14.7 27.5 %collective-permute-start.3 = (bf16[1024,512]{1,0:T(8,128)(2,1)S(1)}, bf16[1024,512]{1,0:T(8,128)(2,1)S(1)}, u32[]{:S(2)}, u32[]{:S(2)}) collective-permute-start(bf16[1024,512]{1,0:T(8,128)(2,1)S(1)} %pad_maximum_fusion.2.refs_0_), channel_id=1, source_target_pairs={{0,2},{2,4},{4,6},{6,0},{1,3},{3,5},{5,7},{7,1},{8,10},{10,12},{12... | collective-permute-start | bytes 3145736 | tf_op jit(solution)/shard_map/ppermute | solution.py:22
  16.5 28.5 %collective-permute-start.2 = (bf16[1024,512]{1,0:T(8,128)(2,1)S(1)}, bf16[1024,512]{1,0:T(8,128)(2,1)S(1)}, u32[]{:S(2)}, u32[]{:S(2)}) collective-permute-start(bf16[1024,512]{1,0:T(8,128)(2,1)S(1)} %pad_maximum_fusion.2.refs_0_), channel_id=1, source_target_pairs={{0,6},{2,0},{4,2},{6,4},{1,7},{3,1},{5,3},{7,5},{8,14},{10,8},{12,... | collective-permute-start | bytes 3145736 | tf_op jit(solution)/shard_map/ppermute | solution.py:22
  18.7 26.3 %collective-permute-start.1 = (bf16[1024,512]{1,0:T(8,128)(2,1)S(1)}, bf16[1024,512]{1,0:T(8,128)(2,1)}, u32[]{:S(2)}, u32[]{:S(2)}) collective-permute-start(bf16[1024,512]{1,0:T(8,128)(2,1)S(1)} %pad_maximum_fusion.2.refs_0_), channel_id=1, source_target_pairs={{0,1},{1,0},{2,3},{3,2},{4,5},{5,4},{6,7},{7,6},{8,9},{9,8},{10,11... | collective-permute-start | bytes 3145736 | tf_op jit(solution)/shard_map/ppermute | solution.py:22
  19.9 27.9 %collective-permute-start.5 = (bf16[512,1024]{1,0:T(8,128)(2,1)}, bf16[512,1024]{1,0:T(8,128)(2,1)}, u32[]{:S(2)}, u32[]{:S(2)}) collective-permute-start(bf16[512,1024]{1,0:T(8,128)(2,1)} %shard_map.120.refs_6_.refs_8_), channel_id=1, source_target_pairs={{0,16},{16,32},{32,48},{48,0},{1,17},{17,33},{33,49},{49,1},{2,18}... | collective-permute-start | bytes 3145736 | tf_op jit(solution)/shard_map/ppermute | solution.py:22
  21.2 26.6 %collective-permute-start.4 = (bf16[512,1024]{1,0:T(8,128)(2,1)}, bf16[512,1024]{1,0:T(8,128)(2,1)S(1)}, u32[]{:S(2)}, u32[]{:S(2)}) collective-permute-start(bf16[512,1024]{1,0:T(8,128)(2,1)} %shard_map.120.refs_6_.refs_8_), channel_id=1, source_target_pairs={{0,48},{16,0},{32,16},{48,32},{1,49},{17,1},{33,17},{49,33},{2,50}... | collective-permute-start | bytes 3145736 | tf_op jit(solution)/shard_map/ppermute | solution.py:22
  25.5 1.4 copy-start.3
  29.7 1.4 copy-start.4
  42.2 51.8 %copy-start.8 = (bf16[1024,512]{1,0:T(8,128)(2,1)}, bf16[1024,512]{1,0:T(8,128)(2,1)S(1)}, u32[]{:S(2)}) copy-start(bf16[1024,512]{1,0:T(8,128)(2,1)S(1)} %collective-permute-done.3.refs_4_.refs_6_) | copy-start | bytes 3145732
  42.2 32.7 %collective-permute-start.8 = (bf16[512,1024]{1,0:T(8,128)(2,1)}, bf16[512,1024]{1,0:T(8,128)(2,1)}, u32[]{:S(2)}, u32[]{:S(2)}) collective-permute-start(bf16[512,1024]{1,0:T(8,128)(2,1)} %shard_map.120.refs_6_.refs_8_), channel_id=1, source_target_pairs={{0,64},{64,0},{1,65},{65,1},{2,66},{66,2},{3,67},{67,3},{4,68},{68... | collective-permute-start | bytes 3145736 | tf_op jit(solution)/shard_map/ppermute | solution.py:22
  45.0 1.0 copy-start.9
  47.8 1.0 copy-start.14
  48.8 26.6 %collective-permute-start.9 = (bf16[512,1024]{1,0:T(8,128)(2,1)}, bf16[512,1024]{1,0:T(8,128)(2,1)}, u32[]{:S(2)}, u32[]{:S(2)}) collective-permute-start(bf16[512,1024]{1,0:T(8,128)(2,1)} %collective-permute-done.5.refs_9_.refs_14_), channel_id=1, source_target_pairs={{0,16},{16,32},{32,48},{48,0},{1,17},{17,33},{33,49},{49,1},{2,18}... | collective-permute-start | bytes 3145736 | tf_op jit(solution)/shard_map/ppermute | solution.py:22
  49.7 25.7 %collective-permute-start.7 = (bf16[1024,512]{1,0:T(8,128)(2,1)}, bf16[1024,512]{1,0:T(8,128)(2,1)S(1)}, u32[]{:S(2)}, u32[]{:S(2)}) collective-permute-start(bf16[1024,512]{1,0:T(8,128)(2,1)} %collective-permute-done.1.refs_1_), channel_id=1, source_target_pairs={{0,2},{2,4},{4,6},{6,0},{1,3},{3,5},{5,7},{7,1},{8,10},{10,12},{12... | collective-permute-start | bytes 3145736 | tf_op jit(solution)/shard_map/ppermute | solution.py:22
  49.7 25.7 %collective-permute-start.6 = (bf16[1024,512]{1,0:T(8,128)(2,1)}, bf16[1024,512]{1,0:T(8,128)(2,1)}, u32[]{:S(2)}, u32[]{:S(2)}) collective-permute-start(bf16[1024,512]{1,0:T(8,128)(2,1)} %collective-permute-done.1.refs_1_), channel_id=1, source_target_pairs={{0,6},{2,0},{4,2},{6,4},{1,7},{3,1},{5,3},{7,5},{8,14},{10,8},{12,... | collective-permute-start | bytes 3145736 | tf_op jit(solution)/shard_map/ppermute | solution.py:22
  75.4 7.7 %copy-start.10 = (bf16[1024,512]{1,0:T(8,128)(2,1)}, bf16[1024,512]{1,0:T(8,128)(2,1)S(1)}, u32[]{:S(2)}) copy-start(bf16[1024,512]{1,0:T(8,128)(2,1)S(1)} %collective-permute-done.7.refs_5_.refs_7_) | copy-start | bytes 3145732
  75.4 28.1 %collective-permute-start.14 = (bf16[512,1024]{1,0:T(8,128)(2,1)}, bf16[512,1024]{1,0:T(8,128)(2,1)S(1)}, u32[]{:S(2)}, u32[]{:S(2)}) collective-permute-start(bf16[512,1024]{1,0:T(8,128)(2,1)} %collective-permute-done.8.refs_10_.refs_9_), channel_id=1, source_target_pairs={{0,16},{16,32},{32,48},{48,0},{1,17},{17,33},{33,49},{49,1},{2,18}... | collective-permute-start | bytes 3145736 | tf_op jit(solution)/shard_map/ppermute | solution.py:22
  76.3 27.7 %collective-permute-start.12 = (bf16[512,1024]{1,0:T(8,128)(2,1)}, bf16[512,1024]{1,0:T(8,128)(2,1)S(1)}, u32[]{:S(2)}, u32[]{:S(2)}) collective-permute-start(bf16[512,1024]{1,0:T(8,128)(2,1)} %collective-permute-done.8.refs_10_.refs_9_), channel_id=1, source_target_pairs={{0,48},{16,0},{32,16},{48,32},{1,49},{17,1},{33,17},{49,33},{2,50}... | collective-permute-start | bytes 3145736 | tf_op jit(solution)/shard_map/ppermute | solution.py:22
  78.2 24.8 %collective-permute-start.11 = (bf16[1024,512]{1,0:T(8,128)(2,1)}, bf16[1024,512]{1,0:T(8,128)(2,1)S(1)}, u32[]{:S(2)}, u32[]{:S(2)}) collective-permute-start(bf16[1024,512]{1,0:T(8,128)(2,1)} %collective-permute-done.6.refs_3_), channel_id=1, source_target_pairs={{0,6},{2,0},{4,2},{6,4},{1,7},{3,1},{5,3},{7,5},{8,14},{10,8},{12,... | collective-permute-start | bytes 3145736 | tf_op jit(solution)/shard_map/ppermute | solution.py:22
  80.5 23.1 %collective-permute-start.10 = (bf16[1024,512]{1,0:T(8,128)(2,1)S(1)}, bf16[1024,512]{1,0:T(8,128)(2,1)S(1)}, u32[]{:S(2)}, u32[]{:S(2)}) collective-permute-start(bf16[1024,512]{1,0:T(8,128)(2,1)S(1)} %collective-permute-done.3.refs_4_.refs_6_), channel_id=1, source_target_pairs={{0,2},{2,4},{4,6},{6,0},{1,3},{3,5},{5,7},{7,1},{8,10},{10,12},{12... | collective-permute-start | bytes 3145736 | tf_op jit(solution)/shard_map/ppermute | solution.py:22
  80.5 23.1 %collective-permute-start.13 = (bf16[512,1024]{1,0:T(8,128)(2,1)}, bf16[512,1024]{1,0:T(8,128)(2,1)}, u32[]{:S(2)}, u32[]{:S(2)}) collective-permute-start(bf16[512,1024]{1,0:T(8,128)(2,1)} %collective-permute-done.9.refs_8_.refs_12_), channel_id=1, source_target_pairs={{0,64},{64,0},{1,65},{65,1},{2,66},{66,2},{3,67},{67,3},{4,68},{68... | collective-permute-start | bytes 3145736 | tf_op jit(solution)/shard_map/ppermute | solution.py:22
  94.0 12.0 %copy-start.1 = (bf16[1024,512]{1,0:T(8,128)(2,1)S(1)}, bf16[1024,512]{1,0:T(8,128)(2,1)}, u32[]{:S(2)}) copy-start(bf16[1024,512]{1,0:T(8,128)(2,1)} %shard_map.124.first) | copy-start | bytes 3145732
  103.0 1.0 copy-start.11
  103.6 1.0 copy-start.12
  105.0 1.0 copy-start.18
  106.0 15.5 %collective-permute-start.15 = (bf16[1024,512]{1,0:T(8,128)(2,1)S(1)}, bf16[1024,512]{1,0:T(8,128)(2,1)S(1)}, u32[]{:S(2)}, u32[]{:S(2)}) collective-permute-start(bf16[1024,512]{1,0:T(8,128)(2,1)S(1)} %copy-done.1), channel_id=1, source_target_pairs={{0,8},{8,0},{1,9},{9,1},{2,10},{10,2},{3,11},{11,3},{4,12},{12,4},... | collective-permute-start | bytes 3145736 | tf_op jit(solution)/shard_map/ppermute | solution.py:22
  121.5 6.4 %copy-start.2 = (bf16[1024,512]{1,0:T(8,128)(2,1)}, bf16[1024,512]{1,0:T(8,128)(2,1)S(1)}, u32[]{:S(2)}) copy-start(bf16[1024,512]{1,0:T(8,128)(2,1)S(1)} %collective-permute-done.15.second) | copy-start | bytes 3145732
  121.5 6.4 %collective-permute-start.16 = (bf16[512,1024]{1,0:T(8,128)(2,1)S(1)}, bf16[512,1024]{1,0:T(8,128)(2,1)S(1)}, u32[]{:S(2)}, u32[]{:S(2)}) collective-permute-start(bf16[512,1024]{1,0:T(8,128)(2,1)S(1)} %get-tuple-element.182), channel_id=1, source_target_pairs={{0,8},{8,0},{1,9},{9,1},{2,10},{10,2},{3,11},{11,3},{4,12},{12,4},... | collective-permute-start | bytes 3145736 | tf_op jit(solution)/shard_map/ppermute | solution.py:22
  127.9 2.8 %copy-start.16 = (bf16[512,1024]{1,0:T(8,128)(2,1)}, bf16[512,1024]{1,0:T(8,128)(2,1)S(1)}, u32[]{:S(2)}) copy-start(bf16[512,1024]{1,0:T(8,128)(2,1)S(1)} %collective-permute-done.16.b_ref) | copy-start | bytes 3145732
  127.9 29.9 %collective-permute-start.17 = (bf16[1024,512]{1,0:T(8,128)(2,1)}, bf16[1024,512]{1,0:T(8,128)(2,1)}, u32[]{:S(2)}, u32[]{:S(2)}) collective-permute-start(bf16[1024,512]{1,0:T(8,128)(2,1)} %get-tuple-element.204), channel_id=1, source_target_pairs={{0,16},{16,32},{32,48},{48,0},{1,17},{17,33},{33,49},{49,1},{2,18}... | collective-permute-start | bytes 3145736 | tf_op jit(solution)/shard_map/ppermute | solution.py:22
  128.0 29.8 %collective-permute-start.18 = (bf16[1024,512]{1,0:T(8,128)(2,1)}, bf16[1024,512]{1,0:T(8,128)(2,1)}, u32[]{:S(2)}, u32[]{:S(2)}) collective-permute-start(bf16[1024,512]{1,0:T(8,128)(2,1)} %get-tuple-element.205), channel_id=1, source_target_pairs={{0,48},{16,0},{32,16},{48,32},{1,49},{17,1},{33,17},{49,33},{2,50}... | collective-permute-start | bytes 3145736 | tf_op jit(solution)/shard_map/ppermute | solution.py:22
  130.6 27.2 %collective-permute-start.19 = (bf16[1024,512]{1,0:T(8,128)(2,1)S(1)}, bf16[1024,512]{1,0:T(8,128)(2,1)S(1)}, u32[]{:S(2)}, u32[]{:S(2)}) collective-permute-start(bf16[1024,512]{1,0:T(8,128)(2,1)S(1)} %get-tuple-element.206), channel_id=1, source_target_pairs={{0,64},{64,0},{1,65},{65,1},{2,66},{66,2},{3,67},{67,3},{4,68},{68... | collective-permute-start | bytes 3145736 | tf_op jit(solution)/shard_map/ppermute | solution.py:22
  147.4 10.5 %copy-start.20 = (bf16[8,128,512]{2,1,0:T(8,128)(2,1)S(1)}, bf16[8,128,512]{2,1,0:T(8,128)(2,1)}, u32[]{:S(2)}) copy-start(bf16[8,128,512]{2,1,0:T(8,128)(2,1)} %get-tuple-element.231) | copy-start | bytes 3145732
  157.8 4.0 %copy-start.15 = (f32[8,128,512]{2,1,0:T(8,128)S(1)}, f32[8,128,512]{2,1,0:T(8,128)}, u32[]{:S(2)}) copy-start(f32[8,128,512]{2,1,0:T(8,128)} %get-tuple-element.230) | copy-start | bytes 6291460
  157.8 4.0 %collective-permute-start.22 = (bf16[8,128,512]{2,1,0:T(8,128)(2,1)S(1)}, bf16[8,128,512]{2,1,0:T(8,128)(2,1)S(1)}, u32[]{:S(2)}, u32[]{:S(2)}) collective-permute-start(bf16[8,128,512]{2,1,0:T(8,128)(2,1)S(1)} %copy-done.20), channel_id=1, source_target_pairs={{0,8},{8,0},{1,9},{9,1},{2,10},{10,2},{3,11},{11,3},{4,12},{12,4},... | collective-permute-start | bytes 3145736 | tf_op jit(solution)/shard_map/ppermute | solution.py:22
  159.9 13.6 %collective-permute-start.21 = (bf16[512,512]{1,0:T(8,128)(2,1)S(1)}, bf16[512,512]{1,0:T(8,128)(2,1)S(1)}, u32[]{:S(2)}, u32[]{:S(2)}) collective-permute-start(bf16[512,512]{1,0:T(8,128)(2,1)S(1)} %get-tuple-element.246), channel_id=1, source_target_pairs={{0,48},{16,0},{32,16},{48,32},{1,49},{17,1},{33,17},{49,33},{2,50}... | collective-permute-start | bytes 1572872 | tf_op jit(solution)/shard_map/ppermute | solution.py:22
  160.0 14.6 %collective-permute-start.20 = (bf16[512,512]{1,0:T(8,128)(2,1)S(1)}, bf16[512,512]{1,0:T(8,128)(2,1)S(1)}, u32[]{:S(2)}, u32[]{:S(2)}) collective-permute-start(bf16[512,512]{1,0:T(8,128)(2,1)S(1)} %get-tuple-element.247), channel_id=1, source_target_pairs={{0,16},{16,32},{32,48},{48,0},{1,17},{17,33},{33,49},{49,1},{2,18}... | collective-permute-start | bytes 1572872 | tf_op jit(solution)/shard_map/ppermute | solution.py:22
  162.3 14.7 %collective-permute-start.23 = (bf16[4,128,512]{2,1,0:T(8,128)(2,1)S(1)}, bf16[4,128,512]{2,1,0:T(8,128)(2,1)S(1)}, u32[]{:S(2)}, u32[]{:S(2)}) collective-permute-start(bf16[4,128,512]{2,1,0:T(8,128)(2,1)S(1)} %fusion), channel_id=1, source_target_pairs={{0,64},{64,0},{1,65},{65,1},{2,66},{66,2},{3,67},{67,3},{4,68},{68... | collective-permute-start | bytes 1572872 | tf_op jit(solution)/shard_map/ppermute | solution.py:22
  177.6 28.4 %copy-start.13 = (s32[1024,512]{1,0:T(8,128)S(1)}, s32[1024,512]{1,0:T(8,128)}, u32[]{:S(2)}) copy-start(s32[1024,512]{1,0:T(8,128)} %codes_ref.2) | copy-start | bytes 6291460
  177.7 28.3 %collective-permute-start.25 = (bf16[1152,512]{1,0:T(8,128)(2,1)S(1)}, bf16[1152,512]{1,0:T(8,128)(2,1)S(1)}, u32[]{:S(2)}, u32[]{:S(2)}) collective-permute-start(bf16[1152,512]{1,0:T(8,128)(2,1)S(1)} %pad_maximum_fusion), channel_id=1, source_target_pairs={{0,16},{16,32},{32,48},{48,0},{1,17},{17,33},{33,49},{49,1},{2,18}... | collective-permute-start | bytes 3538952 | tf_op jit(solution)/shard_map/ppermute | solution.py:22
  177.9 28.1 %collective-permute-start.26 = (bf16[1152,512]{1,0:T(8,128)(2,1)S(1)}, bf16[1152,512]{1,0:T(8,128)(2,1)S(1)}, u32[]{:S(2)}, u32[]{:S(2)}) collective-permute-start(bf16[1152,512]{1,0:T(8,128)(2,1)S(1)} %pad_maximum_fusion.1), channel_id=1, source_target_pairs={{0,48},{16,0},{32,16},{48,32},{1,49},{17,1},{33,17},{49,33},{2,50}... | collective-permute-start | bytes 3538952 | tf_op jit(solution)/shard_map/ppermute | solution.py:22
  180.6 24.4 %collective-permute-start.24 = (bf16[1024,512]{1,0:T(8,128)(2,1)S(1)}, bf16[1024,512]{1,0:T(8,128)(2,1)S(1)}, u32[]{:S(2)}, u32[]{:S(2)}) collective-permute-start(bf16[1024,512]{1,0:T(8,128)(2,1)S(1)} %add_convert_fusion), channel_id=1, source_target_pairs={{0,64},{64,0},{1,65},{65,1},{2,66},{66,2},{3,67},{67,3},{4,68},{68... | collective-permute-start | bytes 3145736 | tf_op jit(solution)/shard_map/ppermute | solution.py:22
  183.5 26.5 %collective-permute-start.27 = (bf16[128,512]{1,0:T(8,128)(2,1)S(1)}, bf16[128,512]{1,0:T(8,128)(2,1)S(1)}, u32[]{:S(2)}, u32[]{:S(2)}) collective-permute-start(bf16[128,512]{1,0:T(8,128)(2,1)S(1)} %get-tuple-element.250), channel_id=1, source_target_pairs={{0,32},{16,48},{32,0},{48,16},{1,33},{17,49},{33,1},{49,17},{2,34}... | collective-permute-start | bytes 393224 | tf_op jit(solution)/shard_map/ppermute | solution.py:22
  (2 other events, 1.6 us)
Sparse Core Ops, SparseCore 0:
  11.8 58.4 all-gather.1

commit v2 on v1

--- a/solution.py
+++ b/solution.py
@@ -200,29 +200,62 @@
     )(own_order, other_order, hidden_in, here, there, *probs)
 
 
-def value_grads(own, others, codes):
-    columns, rows = own.shape
-
-    def kernel(own_ref, *refs):
-        refs, (codes_ref, step_out, out) = refs[: len(others)], refs[len(others) :]
-        total = own_ref[...]
-        for ref in refs:
+def final_grads(weight_terms, value_terms, output_codes, value_codes):
+    rows, columns = output_codes.shape
+    depth, width = value_codes.shape
+    steps = 4
+    block = rows // steps
+    groups = block // GROUP
+    count = len(weight_terms)
+
+    def centered_sums(codes, total, step_out, first):
+        centered = (codes - 8).astype(F32) * total
+        for k in range(total.shape[0] // GROUP):
+            group = centered[k * GROUP : (k + 1) * GROUP]
+            step_out[pl.ds(first + k, 1), :] = jnp.sum(group, axis=0, keepdims=True)
+
+    def kernel(*refs):
+        terms, refs = refs[:count], refs[count:]
+        value_refs, refs = refs[: 2 + len(value_terms)], refs[2 + len(value_terms) :]
+        codes_ref, value_codes_ref, step_out, value_step_out, out, value_out = refs
+        k = pl.program_id(0)
+        total = terms[0][...].astype(F32)
+        for ref in terms[1:]:
             total += ref[...].astype(F32)
-        total = total.T
         out[...] = total
-        centered = (codes_ref[...] - 8).astype(F32) * total
-        for k in range(rows // GROUP):
-            group = centered[k * GROUP : (k + 1) * GROUP]
-            step_out[k : k + 1, :] = jnp.sum(group, axis=0, keepdims=True)
-
-    return pl.pallas_call(
-        kernel,
-        out_shape=(
-            jax.ShapeDtypeStruct((rows // GROUP, columns), F32),
-            jax.ShapeDtypeStruct((rows, columns), F32),
-        ),
+        centered_sums(codes_ref[...], total, step_out, k * groups)
+
+        @pl.when(k == 0)
+        def _():
+            value = value_refs[0][...].astype(F32)
+            for ref in value_refs[1:]:
+                value += ref[...].astype(F32)
+            value = value.T
+            value_out[...] = value
+            centered_sums(value_codes_ref[...], value, value_step_out, 0)
+
+    part = pl.BlockSpec((block, columns), lambda k: (k, 0))
+    below = pl.BlockSpec((width, columns), lambda k: (rows // width, 0))
+
+    def whole(shape):
+        return pl.BlockSpec(shape, lambda k: (0,) * len(shape))
+
+    step_shape, value_step_shape = (rows // GROUP, columns), (depth // GROUP, width)
+    return pl.pallas_call(
+        kernel,
+        out_shape=tuple(
+            jax.ShapeDtypeStruct(shape, F32)
+            for shape in (step_shape, value_step_shape, output_codes.shape, value_codes.shape)
+        ),
+        grid=(steps,),
+        in_specs=[part] * count
+        + [below] * 2
+        + [whole(x.shape) for x in value_terms]
+        + [part, whole(value_codes.shape)],
+        out_specs=(whole(step_shape), whole(value_step_shape), part, whole(value_codes.shape)),
+        compiler_params=pltpu.CompilerParams(vmem_limit_bytes=32 << 20),
         cost_estimate=BRIEF,
-    )(own, *others, codes)
+    )(*weight_terms, *weight_terms[-2:], *value_terms, output_codes, value_codes)
 
 
 def fetch_piece(which, pieces, target, sem):
@@ -475,13 +508,7 @@
     )
     up0, down0 = shift(up0, "y", 1), shift(down0, "y", -1)
     term_far = shift(send[2], "y", 2)
-    terms = (up0[heads:], down0[heads:], term_far)
-    value_step_grad, value_weight_grad = value_grads(term[0], terms, value_codes)
-    output_weight_grad = stay.astype(F32) + across.astype(F32)
-    output_weight_grad += up0[:heads].astype(F32) + down0[:heads].astype(F32)
-    centered_out = (output_codes - 8).astype(F32)
-    output_step_grad = (centered_out * output_weight_grad).reshape(-1, GROUP, half).sum(axis=1)
-    return (output_step_grad, value_step_grad, output_weight_grad, value_weight_grad)
+    return final_grads((stay, across, up0, down0), (term[0], term_far), output_codes, value_codes)
 
 
 def solution(mesh):

time: 223 us -> 219 us (0.982)
  other arithmetic: 6.75 us -> 4.04 us
  local copies, waits for them, and re-layouts: 12.1 us -> 9.41 us
    reduce_sum x1 -> x0, other arithmetic: 2.73 us -> none  [body(): (centered_out * output_weight_grad).reshape(-1, GROUP, half).sum(axis=1)]
  transfers between devices with their start and end apart: 29 -> 29, of which waited for: 11 -> 10; matrix products, arithmetic and copies ran while one was open for 4% -> 2% of each run, Pallas kernels for 31% -> 32%
where the time goes in v2:
time: 219 us; the launch traced here: 217 us
  Pallas kernels  71.6 us (33%)
  waiting for transfers between devices  70.2 us (32%)
  starting transfers between devices  47.1 us (22%)
  between operations  14.5 us (7%)
  local copies, waits for them, and re-layouts  9.41 us (4%)
  other arithmetic  4.04 us (2%)
    ppermute x28, waiting for transfers between devices, shift(): return lax.ppermute(x, axis, [(i, (i + step) % n) for i in range(n)])  70.1 us
    ppermute x28, starting transfers between devices, shift(): return lax.ppermute(x, axis, [(i, (i + step) % n) for i in range(n)])  47.1 us
    pallas_call x2, Pallas kernels, head_grads(): pl.pallas_call(kernel, out_shape=out_shape, grid_spec=pltpu.PrefetchScala...  20.4 us
    pallas_call x2, Pallas kernels, weight_parts(): pl.pallas_call(kernel, out_shape=(jax.ShapeDtypeStruct((heads, depth), BF...  16.4 us
    pallas_call x1, Pallas kernels, value_terms(): pl.pallas_call(kernel, out_shape=(jax.ShapeDtypeStruct((count, HD, width)...  11.3 us
    pallas_call x1, Pallas kernels, attended_heads(): pl.pallas_call(kernel, out_shape=jax.ShapeDtypeStruct((heads * columns, r...  10.9 us
    unnamed x42, local copies, waits for them, and re-layouts  7.22 us
    pallas_call x2, Pallas kernels, attention_probs(): pl.pallas_call(kernel, out_shape=jax.ShapeDtypeStruct((count, length, len...  5.72 us
  transfers between devices with their start and end apart: 29, of which 10 were waited for; matrix products, arithmetic and copies ran while one was open for 2% of the time, Pallas kernels for 32%

profile of v2, /device:TPU:1, one launch (start us, length us, event | category | flops | bytes accessed | tf_op | source)
XLA Modules:
  0.0 216.9 jit_solution(3122300390380384719)
XLA Ops:
  7.2 1.3 constant_dynamic-slice_fusion.1
  8.5 1.5 collective-permute-start
  10.0 1.6 shard_map.123
  11.9 2.7 %shard_map.120.refs_6_.refs_8_ = bf16[512,1024]{1,0:T(8,128)(2,1)} custom-call(s32[1024,512]{1,0:T(8,128)} %refs_8_.1, f32[8,512]{1,0:T(8,128)} %steps_ref.2), custom_call_target="tpu_custom_call" | custom-call | flops 1048576 | bytes 65536 | tf_op jit(solution)/shard_map/pallas_call | solution.py:53
  14.7 1.8 collective-permute-start.3
  16.5 2.2 %collective-permute-start.2 = (bf16[1024,512]{1,0:T(8,128)(2,1)S(1)}, bf16[1024,512]{1,0:T(8,128)(2,1)S(1)}, u32[]{:S(2)}, u32[]{:S(2)}) collective-permute-start(bf16[1024,512]{1,0:T(8,128)(2,1)S(1)} %pad_maximum_fusion.2.refs_0_), channel_id=1, source_target_pairs={{0,6},{2,0},{4,2},{6,4},{1,7},{3,1},{5,3},{7,5},{8,14},{10,8},{12,... | collective-permute-start | bytes 3145736 | tf_op jit(solution)/shard_map/ppermute | solution.py:22
  18.7 1.2 collective-permute-start.1
  19.9 1.3 collective-permute-start.5
  21.2 1.4 collective-permute-start.4
  22.6 2.9 %shard_map.122.p_high = bf16[4,512,512]{2,1,0:T(8,128)(2,1)S(1)} custom-call(bf16[512,1024]{1,0:T(8,128)(2,1)S(1)} %copy-done.8, bf16[512,128]{1,0:T(8,128)(2,1)S(1)} %copy-done.9, s32[512,1]{1,0:T(8,128)S(1)} %copy.13.down_ref, s32[1,512]{1,0:T(1,128)S(1)} %copy-done.7), custom_call_target="tpu_custom_call" | custom-call | flops 34359738368 | bytes 16777216 | tf_op jit(solution)/shard_map/pallas_call | solution.py:84
  25.5 1.4 copy-done.4
  26.9 2.9 %shard_map.121.p_low = bf16[4,512,512]{2,1,0:T(8,128)(2,1)S(1)} custom-call(bf16[512,1024]{1,0:T(8,128)(2,1)S(1)} %copy-done.8, bf16[512,128]{1,0:T(8,128)(2,1)S(1)} %copy-done.9, s32[512,1]{1,0:T(8,128)S(1)} %copy.13.down_ref, s32[1,512]{1,0:T(1,128)S(1)} %copy-done.7), custom_call_target="tpu_custom_call" | custom-call | flops 34359738368 | bytes 16777216 | tf_op jit(solution)/shard_map/pallas_call | solution.py:84
  29.7 1.3 copy-done.5
  31.0 11.2 %collective-permute-done.3.refs_4_.refs_6_ = bf16[1024,512]{1,0:T(8,128)(2,1)S(1)} collective-permute-done((bf16[1024,512]{1,0:T(8,128)(2,1)S(1)}, bf16[1024,512]{1,0:T(8,128)(2,1)S(1)}, u32[]{:S(2)}, u32[]{:S(2)}) %collective-permute-start.3) | collective-permute-done | bytes 1048608 | tf_op jit(solution)/shard_map/ppermute | solution.py:22
  42.2 2.7 %collective-permute-start.8 = (bf16[512,1024]{1,0:T(8,128)(2,1)}, bf16[512,1024]{1,0:T(8,128)(2,1)}, u32[]{:S(2)}, u32[]{:S(2)}) collective-permute-start(bf16[512,1024]{1,0:T(8,128)(2,1)} %shard_map.120.refs_6_.refs_8_), channel_id=1, source_target_pairs={{0,64},{64,0},{1,65},{65,1},{2,66},{66,2},{3,67},{67,3},{4,68},{68... | collective-permute-start | bytes 3145736 | tf_op jit(solution)/shard_map/ppermute | solution.py:22
  45.0 1.0 copy-done.11
  46.0 1.8 collective-permute-done.5.refs_9_.refs_14_
  47.8 1.0 copy-done.15
  48.8 0.9 collective-permute-start.9
  49.7 2.7 %collective-permute-start.6 = (bf16[1024,512]{1,0:T(8,128)(2,1)}, bf16[1024,512]{1,0:T(8,128)(2,1)}, u32[]{:S(2)}, u32[]{:S(2)}) collective-permute-start(bf16[1024,512]{1,0:T(8,128)(2,1)} %collective-permute-done.1.refs_1_), channel_id=1, source_target_pairs={{0,6},{2,0},{4,2},{6,4},{1,7},{3,1},{5,3},{7,5},{8,14},{10,8},{12,... | collective-permute-start | bytes 3145736 | tf_op jit(solution)/shard_map/ppermute | solution.py:22
  52.5 22.4 %collective-permute-done.8.refs_10_.refs_9_ = bf16[512,1024]{1,0:T(8,128)(2,1)} collective-permute-done((bf16[512,1024]{1,0:T(8,128)(2,1)}, bf16[512,1024]{1,0:T(8,128)(2,1)}, u32[]{:S(2)}, u32[]{:S(2)}) %collective-permute-start.8) | collective-permute-done | bytes 1048608 | tf_op jit(solution)/shard_map/ppermute | solution.py:22
  75.4 0.9 collective-permute-start.14
  76.3 1.8 collective-permute-start.12
  78.2 2.3 %collective-permute-start.11 = (bf16[1024,512]{1,0:T(8,128)(2,1)}, bf16[1024,512]{1,0:T(8,128)(2,1)S(1)}, u32[]{:S(2)}, u32[]{:S(2)}) collective-permute-start(bf16[1024,512]{1,0:T(8,128)(2,1)} %collective-permute-done.6.refs_3_), channel_id=1, source_target_pairs={{0,6},{2,0},{4,2},{6,4},{1,7},{3,1},{5,3},{7,5},{8,14},{10,8},{12,... | collective-permute-start | bytes 3145736 | tf_op jit(solution)/shard_map/ppermute | solution.py:22
  80.5 2.6 %collective-permute-start.13 = (bf16[512,1024]{1,0:T(8,128)(2,1)}, bf16[512,1024]{1,0:T(8,128)(2,1)}, u32[]{:S(2)}, u32[]{:S(2)}) collective-permute-start(bf16[512,1024]{1,0:T(8,128)(2,1)} %collective-permute-done.9.refs_8_.refs_12_), channel_id=1, source_target_pairs={{0,64},{64,0},{1,65},{65,1},{2,66},{66,2},{3,67},{67,3},{4,68},{68... | collective-permute-start | bytes 3145736 | tf_op jit(solution)/shard_map/ppermute | solution.py:22
  83.1 10.9 %shard_map.124.first = bf16[1024,512]{1,0:T(8,128)(2,1)} custom-call(bf16[512,8192]{1,0:T(8,128)(2,1)} %h_ref.3, bf16[8192,128]{1,0:T(8,128)(2,1)} %all-gather.2.cloned.1.call-done.v_ref, bf16[4,512,512]{2,1,0:T(8,128)(2,1)} %copy-done.5, bf16[4,512,512]{2,1,0:T(8,128)(2,1)} %copy-done.4), custom_call_target="tpu_custom_call" | custom-call | flops 34359738368 | bytes 16777216 | tf_op jit(solution)/shard_map/pallas_call | solution.py:129
  94.0 9.0 %shard_map.125.refs_16_ = f32[1024,1024]{1,0:T(8,128)} custom-call(s32[5]{0:T(128)S(1)} %stack.127.which_ref, s32[5]{0:T(128)S(1)} %compare_convert_fusion.use_ref, bf16[1024,512]{1,0:T(8,128)(2,1)S(1)} %pad_maximum_fusion.2.refs_0_, bf16[1024,512]{1,0:T(8,128)(2,1)} %collective-permute-done.1.refs_1_, bf16[1024,512]{1,0:T(8,128)(2,1)} %copy-done.11, ...), custom_call_target="tpu_custom_call" | custom-call | flops 1048576 | bytes 65536 | tf_op jit(solution)/shard_map/pallas_call | solution.py:332
  103.0 0.6 collective-permute-done.10.refs_4_
  104.0 0.5 copy-done.14
  105.0 1.0 copy-done.19
  106.0 3.9 %collective-permute-start.15 = (bf16[1024,512]{1,0:T(8,128)(2,1)S(1)}, bf16[1024,512]{1,0:T(8,128)(2,1)S(1)}, u32[]{:S(2)}, u32[]{:S(2)}) collective-permute-start(bf16[1024,512]{1,0:T(8,128)(2,1)S(1)} %copy-done.2), channel_id=1, source_target_pairs={{0,8},{8,0},{1,9},{9,1},{2,10},{10,2},{3,11},{11,3},{4,12},{12,4},... | collective-permute-start | bytes 3145736 | tf_op jit(solution)/shard_map/ppermute | solution.py:22
  110.1 11.4 %shard_map.126 = (f32[512,1024]{1,0:T(8,128)}, bf16[512,1024]{1,0:T(8,128)(2,1)S(1)}) custom-call(s32[8]{0:T(128)S(1)} %stack.120.which_ref, s32[8]{0:T(128)S(1)} %convert_element_type.54.use_ref, bf16[1024,512]{1,0:T(8,128)(2,1)} %copy-done, bf16[1024,512]{1,0:T(8,128)(2,1)} %collective-permute-done.1.refs_1_, bf16[1024,512]{1,0:T(8,128)(2,1)} %copy-done.11, ...), custom_call_target="tpu_custom_call" | custom-call | flops 1048576 | bytes 65536 | tf_op jit(solution)/shard_map/pallas_call | solution.py:332
  121.9 6.0 %shard_map.127 = (bf16[1024,512]{1,0:T(8,128)(2,1)}, bf16[1024,512]{1,0:T(8,128)(2,1)}, bf16[1024,512]{1,0:T(8,128)(2,1)S(1)}) custom-call(s32[3]{0:T(128)S(1)} %pad_add_fusion.order_ref, bf16[1024,512]{1,0:T(8,128)(2,1)S(1)} %copy-done.2, bf16[1024,512]{1,0:T(8,128)(2,1)S(1)} %collective-permute-done.15.second, bf16[1024,512]{1,0:T(8,128)(2,1)} %copy-done, ...), custom_call_target="tpu_custom_call" | custom-call | flops 1048576 | bytes 65536 | tf_op jit(solution)/shard_map/pallas_call | solution.py:378
  128.0 2.7 %collective-permute-start.18 = (bf16[1024,512]{1,0:T(8,128)(2,1)}, bf16[1024,512]{1,0:T(8,128)(2,1)}, u32[]{:S(2)}, u32[]{:S(2)}) collective-permute-start(bf16[1024,512]{1,0:T(8,128)(2,1)} %get-tuple-element.203), channel_id=1, source_target_pairs={{0,48},{16,0},{32,16},{48,32},{1,49},{17,1},{33,17},{49,33},{2,50}... | collective-permute-start | bytes 3145736 | tf_op jit(solution)/shard_map/ppermute | solution.py:22
  130.7 4.7 %collective-permute-start.19 = (bf16[1024,512]{1,0:T(8,128)(2,1)S(1)}, bf16[1024,512]{1,0:T(8,128)(2,1)S(1)}, u32[]{:S(2)}, u32[]{:S(2)}) collective-permute-start(bf16[1024,512]{1,0:T(8,128)(2,1)S(1)} %get-tuple-element.204), channel_id=1, source_target_pairs={{0,64},{64,0},{1,65},{65,1},{2,66},{66,2},{3,67},{67,3},{4,68},{68... | collective-permute-start | bytes 3145736 | tf_op jit(solution)/shard_map/ppermute | solution.py:22
  136.1 11.3 %shard_map.128 = (f32[8,128,512]{2,1,0:T(8,128)}, bf16[8,128,512]{2,1,0:T(8,128)(2,1)}) custom-call(s32[8]{0:T(128)} %get-tuple-element.248.own_at, s32[8]{0:T(128)} %get-tuple-element.247.other_at, bf16[512,8192]{1,0:T(8,128)(2,1)} %h_ref.3, f32[512,1024]{1,0:T(8,128)} %get-tuple-element.194.a_ref, bf16[512,1024]{1,0:T(8,128)(2,1)} %copy-done.17, ...), custom_call_target="tpu_custom_call" | custom-call | flops 1048576 | bytes 65536 | tf_op jit(solution)/shard_map/pallas_call | solution.py:181
  147.4 10.4 %shard_map.129 = (bf16[1024,512]{1,0:T(8,128)(2,1)S(1)}, bf16[1024,512]{1,0:T(8,128)(2,1)S(1)}, bf16[1024,512]{1,0:T(8,128)(2,1)S(1)}, bf16[1024,512]{1,0:T(8,128)(2,1)S(1)}, bf16[1024,512]{1,0:T(8,128)(2,1)S(1)}) custom-call(s32[5]{0:T(128)S(1)} %stack.129.order_ref, bf16[1024,512]{1,0:T(8,128)(2,1)} %shard_map.124.first, bf16[1024,512]{1,0:T(8,128)(2,1)} %copy-done.3, ...), custom_call_target="tpu_custom_call" | custom-call | flops 1048576 | bytes 65536 | tf_op jit(solution)/shard_map/pallas_call | solution.py:378
  157.9 1.7 collective-permute-start.22
  160.0 1.5 collective-permute-start.20
  162.3 3.0 %collective-permute-start.23 = (bf16[4,128,512]{2,1,0:T(8,128)(2,1)S(1)}, bf16[4,128,512]{2,1,0:T(8,128)(2,1)S(1)}, u32[]{:S(2)}, u32[]{:S(2)}) collective-permute-start(bf16[4,128,512]{2,1,0:T(8,128)(2,1)S(1)} %fusion), channel_id=1, source_target_pairs={{0,64},{64,0},{1,65},{65,1},{2,66},{66,2},{3,67},{67,3},{4,68},{68... | collective-permute-start | bytes 1572872 | tf_op jit(solution)/shard_map/ppermute | solution.py:22
  165.4 2.0 add_convert_fusion
  167.4 6.1 %collective-permute-done.21 = bf16[512,512]{1,0:T(8,128)(2,1)S(1)} collective-permute-done((bf16[512,512]{1,0:T(8,128)(2,1)S(1)}, bf16[512,512]{1,0:T(8,128)(2,1)S(1)}, u32[]{:S(2)}, u32[]{:S(2)}) %collective-permute-start.21) | collective-permute-done | bytes 524320 | tf_op jit(solution)/shard_map/ppermute | solution.py:22
  173.6 1.1 collective-permute-done.20
  174.6 2.4 %collective-permute-done.23 = bf16[4,128,512]{2,1,0:T(8,128)(2,1)S(1)} collective-permute-done((bf16[4,128,512]{2,1,0:T(8,128)(2,1)S(1)}, bf16[4,128,512]{2,1,0:T(8,128)(2,1)S(1)}, u32[]{:S(2)}, u32[]{:S(2)}) %collective-permute-start.23) | collective-permute-done | bytes 524320 | tf_op jit(solution)/shard_map/ppermute | solution.py:22
  177.9 2.7 %collective-permute-start.26 = (bf16[1152,512]{1,0:T(8,128)(2,1)S(1)}, bf16[1152,512]{1,0:T(8,128)(2,1)S(1)}, u32[]{:S(2)}, u32[]{:S(2)}) collective-permute-start(bf16[1152,512]{1,0:T(8,128)(2,1)S(1)} %pad_maximum_fusion.1), channel_id=1, source_target_pairs={{0,48},{16,0},{32,16},{48,32},{1,49},{17,1},{33,17},{49,33},{2,50}... | collective-permute-start | bytes 3538952 | tf_op jit(solution)/shard_map/ppermute | solution.py:22
  180.7 3.0 %collective-permute-start.24 = (bf16[1024,512]{1,0:T(8,128)(2,1)S(1)}, bf16[1024,512]{1,0:T(8,128)(2,1)S(1)}, u32[]{:S(2)}, u32[]{:S(2)}) collective-permute-start(bf16[1024,512]{1,0:T(8,128)(2,1)S(1)} %add_convert_fusion), channel_id=1, source_target_pairs={{0,64},{64,0},{1,65},{65,1},{2,66},{66,2},{3,67},{67,3},{4,68},{68... | collective-permute-start | bytes 3145736 | tf_op jit(solution)/shard_map/ppermute | solution.py:22
  183.7 23.7 %collective-permute-done.27.refs_7_ = bf16[128,512]{1,0:T(8,128)(2,1)S(1)} collective-permute-done((bf16[128,512]{1,0:T(8,128)(2,1)S(1)}, bf16[128,512]{1,0:T(8,128)(2,1)S(1)}, u32[]{:S(2)}, u32[]{:S(2)}) %collective-permute-start.27) | collective-permute-done | bytes 131104 | tf_op jit(solution)/shard_map/ppermute | solution.py:22
  207.4 2.6 %shard_map.130 = (f32[8,512]{1,0:T(8,128)}, f32[4,128]{1,0:T(4,128)}, f32[1024,512]{1,0:T(8,128)}, f32[512,128]{1,0:T(8,128)}) custom-call(bf16[1024,512]{1,0:T(8,128)(2,1)S(1)} %get-tuple-element.230.refs_0_, bf16[1024,512]{1,0:T(8,128)(2,1)S(1)} %collective-permute-done.24.refs_1_, bf16[1152,512]{1,0:T(8,128)(2,1)S(1)} %collective-permute-done.25.refs_2_.refs_4_, ...), custom_call_target="tpu_custom_call" | custom-call | flops 1048576 | bytes 65536 | tf_op jit(solution)/shard_map/pallas_call | solution.py:244
  (91 shorter events, 5.4 us)
Async XLA Ops:
  7.2 4.5 %copy-start.7 = (s32[1,512]{1,0:T(1,128)S(1)}, s32[1,512]{1,0:T(1,128)}, u32[]{:S(2)}) copy-start(s32[1,512]{1,0:T(1,128)} %along_ref.3) | copy-start | bytes 6148
  7.2 68.3 %all-gather.2.cloned.1.call-start = ((), (), s32[]{:S(2)}) async-start(), calls=%async_computation | async-start | bytes 2228224 | tf_op jit(solution)/shard_map/all_gather | solution.py:433
  8.5 6.1 %collective-permute-start = (bf16[512,512]{1,0:T(8,128)(2,1)S(1)}, bf16[512,512]{1,0:T(8,128)(2,1)S(1)}, u32[]{:S(2)}, u32[]{:S(2)}) collective-permute-start(bf16[512,512]{1,0:T(8,128)(2,1)S(1)} %get-tuple-element.243), channel_id=1, source_target_pairs={{0,8},{8,0},{1,9},{9,1},{2,10},{10,2},{3,11},{11,3},{4,12},{12,4},... | collective-permute-start | bytes 1572872 | tf_op jit(solution)/shard_map/ppermute | solution.py:22
  11.8 10.8 %copy-start.8 = (bf16[512,1024]{1,0:T(8,128)(2,1)S(1)}, bf16[512,1024]{1,0:T(8,128)(2,1)}, u32[]{:S(2)}) copy-start(bf16[512,1024]{1,0:T(8,128)(2,1)} %q_ref.1) | copy-start | bytes 3145732
  11.8 10.8 %copy-start.9 = (bf16[512,128]{1,0:T(8,128)(2,1)S(1)}, bf16[512,128]{1,0:T(8,128)(2,1)}, u32[]{:S(2)}) copy-start(bf16[512,128]{1,0:T(8,128)(2,1)} %k_ref.3) | copy-start | bytes 393220
  14.7 79.3 %copy-start = (bf16[1024,512]{1,0:T(8,128)(2,1)}, bf16[1024,512]{1,0:T(8,128)(2,1)S(1)}, u32[]{:S(2)}) copy-start(bf16[1024,512]{1,0:T(8,128)(2,1)S(1)} %pad_maximum_fusion.2.refs_0_) | copy-start | bytes 3145732
  14.7 27.5 %collective-permute-start.3 = (bf16[1024,512]{1,0:T(8,128)(2,1)S(1)}, bf16[1024,512]{1,0:T(8,128)(2,1)S(1)}, u32[]{:S(2)}, u32[]{:S(2)}) collective-permute-start(bf16[1024,512]{1,0:T(8,128)(2,1)S(1)} %pad_maximum_fusion.2.refs_0_), channel_id=1, source_target_pairs={{0,2},{2,4},{4,6},{6,0},{1,3},{3,5},{5,7},{7,1},{8,10},{10,12},{12... | collective-permute-start | bytes 3145736 | tf_op jit(solution)/shard_map/ppermute | solution.py:22
  16.5 28.5 %collective-permute-start.2 = (bf16[1024,512]{1,0:T(8,128)(2,1)S(1)}, bf16[1024,512]{1,0:T(8,128)(2,1)S(1)}, u32[]{:S(2)}, u32[]{:S(2)}) collective-permute-start(bf16[1024,512]{1,0:T(8,128)(2,1)S(1)} %pad_maximum_fusion.2.refs_0_), channel_id=1, source_target_pairs={{0,6},{2,0},{4,2},{6,4},{1,7},{3,1},{5,3},{7,5},{8,14},{10,8},{12,... | collective-permute-start | bytes 3145736 | tf_op jit(solution)/shard_map/ppermute | solution.py:22
  18.7 26.3 %collective-permute-start.1 = (bf16[1024,512]{1,0:T(8,128)(2,1)S(1)}, bf16[1024,512]{1,0:T(8,128)(2,1)}, u32[]{:S(2)}, u32[]{:S(2)}) collective-permute-start(bf16[1024,512]{1,0:T(8,128)(2,1)S(1)} %pad_maximum_fusion.2.refs_0_), channel_id=1, source_target_pairs={{0,1},{1,0},{2,3},{3,2},{4,5},{5,4},{6,7},{7,6},{8,9},{9,8},{10,11... | collective-permute-start | bytes 3145736 | tf_op jit(solution)/shard_map/ppermute | solution.py:22
  19.9 27.9 %collective-permute-start.5 = (bf16[512,1024]{1,0:T(8,128)(2,1)}, bf16[512,1024]{1,0:T(8,128)(2,1)}, u32[]{:S(2)}, u32[]{:S(2)}) collective-permute-start(bf16[512,1024]{1,0:T(8,128)(2,1)} %shard_map.120.refs_6_.refs_8_), channel_id=1, source_target_pairs={{0,16},{16,32},{32,48},{48,0},{1,17},{17,33},{33,49},{49,1},{2,18}... | collective-permute-start | bytes 3145736 | tf_op jit(solution)/shard_map/ppermute | solution.py:22
  21.2 26.6 %collective-permute-start.4 = (bf16[512,1024]{1,0:T(8,128)(2,1)}, bf16[512,1024]{1,0:T(8,128)(2,1)S(1)}, u32[]{:S(2)}, u32[]{:S(2)}) collective-permute-start(bf16[512,1024]{1,0:T(8,128)(2,1)} %shard_map.120.refs_6_.refs_8_), channel_id=1, source_target_pairs={{0,48},{16,0},{32,16},{48,32},{1,49},{17,1},{33,17},{49,33},{2,50}... | collective-permute-start | bytes 3145736 | tf_op jit(solution)/shard_map/ppermute | solution.py:22
  25.5 1.4 copy-start.4
  29.7 1.3 copy-start.5
  42.2 51.8 %copy-start.10 = (bf16[1024,512]{1,0:T(8,128)(2,1)}, bf16[1024,512]{1,0:T(8,128)(2,1)S(1)}, u32[]{:S(2)}) copy-start(bf16[1024,512]{1,0:T(8,128)(2,1)S(1)} %collective-permute-done.3.refs_4_.refs_6_) | copy-start | bytes 3145732
  42.2 32.7 %collective-permute-start.8 = (bf16[512,1024]{1,0:T(8,128)(2,1)}, bf16[512,1024]{1,0:T(8,128)(2,1)}, u32[]{:S(2)}, u32[]{:S(2)}) collective-permute-start(bf16[512,1024]{1,0:T(8,128)(2,1)} %shard_map.120.refs_6_.refs_8_), channel_id=1, source_target_pairs={{0,64},{64,0},{1,65},{65,1},{2,66},{66,2},{3,67},{67,3},{4,68},{68... | collective-permute-start | bytes 3145736 | tf_op jit(solution)/shard_map/ppermute | solution.py:22
  45.0 1.0 copy-start.11
  47.8 1.0 copy-start.15
  48.8 26.6 %collective-permute-start.9 = (bf16[512,1024]{1,0:T(8,128)(2,1)}, bf16[512,1024]{1,0:T(8,128)(2,1)}, u32[]{:S(2)}, u32[]{:S(2)}) collective-permute-start(bf16[512,1024]{1,0:T(8,128)(2,1)} %collective-permute-done.5.refs_9_.refs_14_), channel_id=1, source_target_pairs={{0,16},{16,32},{32,48},{48,0},{1,17},{17,33},{33,49},{49,1},{2,18}... | collective-permute-start | bytes 3145736 | tf_op jit(solution)/shard_map/ppermute | solution.py:22
  49.7 25.7 %collective-permute-start.7 = (bf16[1024,512]{1,0:T(8,128)(2,1)}, bf16[1024,512]{1,0:T(8,128)(2,1)S(1)}, u32[]{:S(2)}, u32[]{:S(2)}) collective-permute-start(bf16[1024,512]{1,0:T(8,128)(2,1)} %collective-permute-done.1.refs_1_), channel_id=1, source_target_pairs={{0,2},{2,4},{4,6},{6,0},{1,3},{3,5},{5,7},{7,1},{8,10},{10,12},{12... | collective-permute-start | bytes 3145736 | tf_op jit(solution)/shard_map/ppermute | solution.py:22
  49.7 25.7 %collective-permute-start.6 = (bf16[1024,512]{1,0:T(8,128)(2,1)}, bf16[1024,512]{1,0:T(8,128)(2,1)}, u32[]{:S(2)}, u32[]{:S(2)}) collective-permute-start(bf16[1024,512]{1,0:T(8,128)(2,1)} %collective-permute-done.1.refs_1_), channel_id=1, source_target_pairs={{0,6},{2,0},{4,2},{6,4},{1,7},{3,1},{5,3},{7,5},{8,14},{10,8},{12,... | collective-permute-start | bytes 3145736 | tf_op jit(solution)/shard_map/ppermute | solution.py:22
  75.4 7.7 %copy-start.12 = (bf16[1024,512]{1,0:T(8,128)(2,1)}, bf16[1024,512]{1,0:T(8,128)(2,1)S(1)}, u32[]{:S(2)}) copy-start(bf16[1024,512]{1,0:T(8,128)(2,1)S(1)} %collective-permute-done.7.refs_5_.refs_7_) | copy-start | bytes 3145732
  75.4 28.1 %collective-permute-start.14 = (bf16[512,1024]{1,0:T(8,128)(2,1)}, bf16[512,1024]{1,0:T(8,128)(2,1)S(1)}, u32[]{:S(2)}, u32[]{:S(2)}) collective-permute-start(bf16[512,1024]{1,0:T(8,128)(2,1)} %collective-permute-done.8.refs_10_.refs_9_), channel_id=1, source_target_pairs={{0,16},{16,32},{32,48},{48,0},{1,17},{17,33},{33,49},{49,1},{2,18}... | collective-permute-start | bytes 3145736 | tf_op jit(solution)/shard_map/ppermute | solution.py:22
  76.3 27.7 %collective-permute-start.12 = (bf16[512,1024]{1,0:T(8,128)(2,1)}, bf16[512,1024]{1,0:T(8,128)(2,1)S(1)}, u32[]{:S(2)}, u32[]{:S(2)}) collective-permute-start(bf16[512,1024]{1,0:T(8,128)(2,1)} %collective-permute-done.8.refs_10_.refs_9_), channel_id=1, source_target_pairs={{0,48},{16,0},{32,16},{48,32},{1,49},{17,1},{33,17},{49,33},{2,50}... | collective-permute-start | bytes 3145736 | tf_op jit(solution)/shard_map/ppermute | solution.py:22
  78.2 24.8 %collective-permute-start.11 = (bf16[1024,512]{1,0:T(8,128)(2,1)}, bf16[1024,512]{1,0:T(8,128)(2,1)S(1)}, u32[]{:S(2)}, u32[]{:S(2)}) collective-permute-start(bf16[1024,512]{1,0:T(8,128)(2,1)} %collective-permute-done.6.refs_3_), channel_id=1, source_target_pairs={{0,6},{2,0},{4,2},{6,4},{1,7},{3,1},{5,3},{7,5},{8,14},{10,8},{12,... | collective-permute-start | bytes 3145736 | tf_op jit(solution)/shard_map/ppermute | solution.py:22
  80.5 23.1 %collective-permute-start.10 = (bf16[1024,512]{1,0:T(8,128)(2,1)S(1)}, bf16[1024,512]{1,0:T(8,128)(2,1)S(1)}, u32[]{:S(2)}, u32[]{:S(2)}) collective-permute-start(bf16[1024,512]{1,0:T(8,128)(2,1)S(1)} %collective-permute-done.3.refs_4_.refs_6_), channel_id=1, source_target_pairs={{0,2},{2,4},{4,6},{6,0},{1,3},{3,5},{5,7},{7,1},{8,10},{10,12},{12... | collective-permute-start | bytes 3145736 | tf_op jit(solution)/shard_map/ppermute | solution.py:22
  80.5 23.1 %collective-permute-start.13 = (bf16[512,1024]{1,0:T(8,128)(2,1)}, bf16[512,1024]{1,0:T(8,128)(2,1)}, u32[]{:S(2)}, u32[]{:S(2)}) collective-permute-start(bf16[512,1024]{1,0:T(8,128)(2,1)} %collective-permute-done.9.refs_8_.refs_12_), channel_id=1, source_target_pairs={{0,64},{64,0},{1,65},{65,1},{2,66},{66,2},{3,67},{67,3},{4,68},{68... | collective-permute-start | bytes 3145736 | tf_op jit(solution)/shard_map/ppermute | solution.py:22
  94.0 12.0 %copy-start.2 = (bf16[1024,512]{1,0:T(8,128)(2,1)S(1)}, bf16[1024,512]{1,0:T(8,128)(2,1)}, u32[]{:S(2)}) copy-start(bf16[1024,512]{1,0:T(8,128)(2,1)} %shard_map.124.first) | copy-start | bytes 3145732
  103.0 1.0 copy-start.13
  105.0 1.0 copy-start.19
  106.0 15.5 %collective-permute-start.15 = (bf16[1024,512]{1,0:T(8,128)(2,1)S(1)}, bf16[1024,512]{1,0:T(8,128)(2,1)S(1)}, u32[]{:S(2)}, u32[]{:S(2)}) collective-permute-start(bf16[1024,512]{1,0:T(8,128)(2,1)S(1)} %copy-done.2), channel_id=1, source_target_pairs={{0,8},{8,0},{1,9},{9,1},{2,10},{10,2},{3,11},{11,3},{4,12},{12,4},... | collective-permute-start | bytes 3145736 | tf_op jit(solution)/shard_map/ppermute | solution.py:22
  121.5 6.3 %copy-start.3 = (bf16[1024,512]{1,0:T(8,128)(2,1)}, bf16[1024,512]{1,0:T(8,128)(2,1)S(1)}, u32[]{:S(2)}) copy-start(bf16[1024,512]{1,0:T(8,128)(2,1)S(1)} %collective-permute-done.15.second) | copy-start | bytes 3145732
  121.6 6.4 %collective-permute-start.16 = (bf16[512,1024]{1,0:T(8,128)(2,1)S(1)}, bf16[512,1024]{1,0:T(8,128)(2,1)S(1)}, u32[]{:S(2)}, u32[]{:S(2)}) collective-permute-start(bf16[512,1024]{1,0:T(8,128)(2,1)S(1)} %get-tuple-element.180), channel_id=1, source_target_pairs={{0,8},{8,0},{1,9},{9,1},{2,10},{10,2},{3,11},{11,3},{4,12},{12,4},... | collective-permute-start | bytes 3145736 | tf_op jit(solution)/shard_map/ppermute | solution.py:22
  127.9 2.8 %copy-start.17 = (bf16[512,1024]{1,0:T(8,128)(2,1)}, bf16[512,1024]{1,0:T(8,128)(2,1)S(1)}, u32[]{:S(2)}) copy-start(bf16[512,1024]{1,0:T(8,128)(2,1)S(1)} %collective-permute-done.16.b_ref) | copy-start | bytes 3145732
  127.9 29.9 %collective-permute-start.17 = (bf16[1024,512]{1,0:T(8,128)(2,1)}, bf16[1024,512]{1,0:T(8,128)(2,1)}, u32[]{:S(2)}, u32[]{:S(2)}) collective-permute-start(bf16[1024,512]{1,0:T(8,128)(2,1)} %get-tuple-element.202), channel_id=1, source_target_pairs={{0,16},{16,32},{32,48},{48,0},{1,17},{17,33},{33,49},{49,1},{2,18}... | collective-permute-start | bytes 3145736 | tf_op jit(solution)/shard_map/ppermute | solution.py:22
  128.0 29.8 %collective-permute-start.18 = (bf16[1024,512]{1,0:T(8,128)(2,1)}, bf16[1024,512]{1,0:T(8,128)(2,1)}, u32[]{:S(2)}, u32[]{:S(2)}) collective-permute-start(bf16[1024,512]{1,0:T(8,128)(2,1)} %get-tuple-element.203), channel_id=1, source_target_pairs={{0,48},{16,0},{32,16},{48,32},{1,49},{17,1},{33,17},{49,33},{2,50}... | collective-permute-start | bytes 3145736 | tf_op jit(solution)/shard_map/ppermute | solution.py:22
  130.7 27.2 %collective-permute-start.19 = (bf16[1024,512]{1,0:T(8,128)(2,1)S(1)}, bf16[1024,512]{1,0:T(8,128)(2,1)S(1)}, u32[]{:S(2)}, u32[]{:S(2)}) collective-permute-start(bf16[1024,512]{1,0:T(8,128)(2,1)S(1)} %get-tuple-element.204), channel_id=1, source_target_pairs={{0,64},{64,0},{1,65},{65,1},{2,66},{66,2},{3,67},{67,3},{4,68},{68... | collective-permute-start | bytes 3145736 | tf_op jit(solution)/shard_map/ppermute | solution.py:22
  147.4 10.5 %copy-start.20 = (bf16[8,128,512]{2,1,0:T(8,128)(2,1)S(1)}, bf16[8,128,512]{2,1,0:T(8,128)(2,1)}, u32[]{:S(2)}) copy-start(bf16[8,128,512]{2,1,0:T(8,128)(2,1)} %get-tuple-element.229) | copy-start | bytes 3145732
  157.9 3.9 %copy-start.16 = (f32[8,128,512]{2,1,0:T(8,128)S(1)}, f32[8,128,512]{2,1,0:T(8,128)}, u32[]{:S(2)}) copy-start(f32[8,128,512]{2,1,0:T(8,128)} %get-tuple-element.228) | copy-start | bytes 6291460
  157.9 3.9 %collective-permute-start.22 = (bf16[8,128,512]{2,1,0:T(8,128)(2,1)S(1)}, bf16[8,128,512]{2,1,0:T(8,128)(2,1)S(1)}, u32[]{:S(2)}, u32[]{:S(2)}) collective-permute-start(bf16[8,128,512]{2,1,0:T(8,128)(2,1)S(1)} %copy-done.20), channel_id=1, source_target_pairs={{0,8},{8,0},{1,9},{9,1},{2,10},{10,2},{3,11},{11,3},{4,12},{12,4},... | collective-permute-start | bytes 3145736 | tf_op jit(solution)/shard_map/ppermute | solution.py:22
  159.9 13.6 %collective-permute-start.21 = (bf16[512,512]{1,0:T(8,128)(2,1)S(1)}, bf16[512,512]{1,0:T(8,128)(2,1)S(1)}, u32[]{:S(2)}, u32[]{:S(2)}) collective-permute-start(bf16[512,512]{1,0:T(8,128)(2,1)S(1)} %get-tuple-element.240), channel_id=1, source_target_pairs={{0,48},{16,0},{32,16},{48,32},{1,49},{17,1},{33,17},{49,33},{2,50}... | collective-permute-start | bytes 1572872 | tf_op jit(solution)/shard_map/ppermute | solution.py:22
  160.0 14.6 %collective-permute-start.20 = (bf16[512,512]{1,0:T(8,128)(2,1)S(1)}, bf16[512,512]{1,0:T(8,128)(2,1)S(1)}, u32[]{:S(2)}, u32[]{:S(2)}) collective-permute-start(bf16[512,512]{1,0:T(8,128)(2,1)S(1)} %get-tuple-element.241), channel_id=1, source_target_pairs={{0,16},{16,32},{32,48},{48,0},{1,17},{17,33},{33,49},{49,1},{2,18}... | collective-permute-start | bytes 1572872 | tf_op jit(solution)/shard_map/ppermute | solution.py:22
  162.3 14.7 %collective-permute-start.23 = (bf16[4,128,512]{2,1,0:T(8,128)(2,1)S(1)}, bf16[4,128,512]{2,1,0:T(8,128)(2,1)S(1)}, u32[]{:S(2)}, u32[]{:S(2)}) collective-permute-start(bf16[4,128,512]{2,1,0:T(8,128)(2,1)S(1)} %fusion), channel_id=1, source_target_pairs={{0,64},{64,0},{1,65},{65,1},{2,66},{66,2},{3,67},{67,3},{4,68},{68... | collective-permute-start | bytes 1572872 | tf_op jit(solution)/shard_map/ppermute | solution.py:22
  177.7 29.7 %copy-start.1 = (s32[1024,512]{1,0:T(8,128)S(1)}, s32[1024,512]{1,0:T(8,128)}, u32[]{:S(2)}) copy-start(s32[1024,512]{1,0:T(8,128)} %refs_8_.1) | copy-start | bytes 6291460
  177.7 29.7 %copy-start.6 = (s32[512,128]{1,0:T(8,128)S(1)}, s32[512,128]{1,0:T(8,128)}, u32[]{:S(2)}) copy-start(s32[512,128]{1,0:T(8,128)} %refs_9_.1) | copy-start | bytes 786436
  177.8 29.6 %collective-permute-start.25 = (bf16[1152,512]{1,0:T(8,128)(2,1)S(1)}, bf16[1152,512]{1,0:T(8,128)(2,1)S(1)}, u32[]{:S(2)}, u32[]{:S(2)}) collective-permute-start(bf16[1152,512]{1,0:T(8,128)(2,1)S(1)} %pad_maximum_fusion), channel_id=1, source_target_pairs={{0,16},{16,32},{32,48},{48,0},{1,17},{17,33},{33,49},{49,1},{2,18}... | collective-permute-start | bytes 3538952 | tf_op jit(solution)/shard_map/ppermute | solution.py:22
  177.9 29.4 %collective-permute-start.26 = (bf16[1152,512]{1,0:T(8,128)(2,1)S(1)}, bf16[1152,512]{1,0:T(8,128)(2,1)S(1)}, u32[]{:S(2)}, u32[]{:S(2)}) collective-permute-start(bf16[1152,512]{1,0:T(8,128)(2,1)S(1)} %pad_maximum_fusion.1), channel_id=1, source_target_pairs={{0,48},{16,0},{32,16},{48,32},{1,49},{17,1},{33,17},{49,33},{2,50}... | collective-permute-start | bytes 3538952 | tf_op jit(solution)/shard_map/ppermute | solution.py:22
  180.7 26.7 %collective-permute-start.24 = (bf16[1024,512]{1,0:T(8,128)(2,1)S(1)}, bf16[1024,512]{1,0:T(8,128)(2,1)S(1)}, u32[]{:S(2)}, u32[]{:S(2)}) collective-permute-start(bf16[1024,512]{1,0:T(8,128)(2,1)S(1)} %add_convert_fusion), channel_id=1, source_target_pairs={{0,64},{64,0},{1,65},{65,1},{2,66},{66,2},{3,67},{67,3},{4,68},{68... | collective-permute-start | bytes 3145736 | tf_op jit(solution)/shard_map/ppermute | solution.py:22
  183.6 23.7 %collective-permute-start.27 = (bf16[128,512]{1,0:T(8,128)(2,1)S(1)}, bf16[128,512]{1,0:T(8,128)(2,1)S(1)}, u32[]{:S(2)}, u32[]{:S(2)}) collective-permute-start(bf16[128,512]{1,0:T(8,128)(2,1)S(1)} %get-tuple-element.244), channel_id=1, source_target_pairs={{0,32},{16,48},{32,0},{48,16},{1,33},{17,49},{33,1},{49,17},{2,34}... | collective-permute-start | bytes 393224 | tf_op jit(solution)/shard_map/ppermute | solution.py:22
  (2 other events, 1.9 us)
Sparse Core Ops, SparseCore 0:
  11.8 58.4 all-gather.1

commit v3 on v2

--- a/solution.py
+++ b/solution.py
@@ -277,9 +277,7 @@
         w_refs, refs = refs[:count], refs[count:]
         g_held, w_held, g_sems, w_sems = refs[-4:]
         if last:
-            before, own, other, total, sem = refs[:-4]
-            start = pltpu.make_async_copy(before, total, sem)
-            start.start()
+            before, own, other, total, earlier, sem = refs[:-4]
         else:
             (total,) = refs[:-4]
         for k in range(count):
@@ -295,9 +293,9 @@
                 pltpu.make_async_copy(w_refs[k], w_held.at[k], w_sems.at[k]).start()
 
         if last:
-            start.wait()
-        else:
-            total[...] = jnp.zeros_like(total)
+            start = pltpu.make_async_copy(before, earlier, sem)
+            start.start()
+        total[...] = jnp.zeros_like(total)
 
         def one(k, carry):
             @pl.when(use_ref[k] == 1)
@@ -310,8 +308,9 @@
 
         lax.fori_loop(0, count, one, 0)
         if last:
-            own[...] = total[:half]
-            other[...] = total[half:].astype(BF16)
+            start.wait()
+            own[...] = total[:half] + earlier[:half]
+            other[...] = (total[half:] + earlier[half:]).astype(BF16)
 
     whole = pl.BlockSpec(memory_space=pltpu.VMEM)
     anywhere = pl.BlockSpec(memory_space=pl.ANY)
@@ -322,7 +321,8 @@
         pltpu.SemaphoreType.DMA((count,)),
     ]
     if last:
-        scratch = [pltpu.VMEM((rows, heads), F32), pltpu.SemaphoreType.DMA] + scratch
+        sums = [pltpu.VMEM((rows, heads), F32)] * 2
+        scratch = sums + [pltpu.SemaphoreType.DMA] + scratch
         out_shape = (
             jax.ShapeDtypeStruct((half, heads), F32),
             jax.ShapeDtypeStruct((half, heads), BF16),

time: 219 us -> 217 us (level)
  transfers between devices with their start and end apart: 29 -> 29, of which waited for: 10 -> 10; matrix products, arithmetic and copies ran while one was open for 2% -> 2% of each run, Pallas kernels for 32% -> 31%
where the time goes in v3:
time: 217 us; the launch traced here: 214 us
  waiting for transfers between devices  70.2 us (32%)
  Pallas kernels  69.8 us (32%)
  starting transfers between devices  46.6 us (21%)
  between operations  14.5 us (7%)
  local copies, waits for them, and re-layouts  9.41 us (4%)
  other arithmetic  4.04 us (2%)
    ppermute x28, waiting for transfers between devices, shift(): return lax.ppermute(x, axis, [(i, (i + step) % n) for i in range(n)])  70.1 us
    ppermute x28, starting transfers between devices, shift(): return lax.ppermute(x, axis, [(i, (i + step) % n) for i in range(n)])  46.5 us
    pallas_call x2, Pallas kernels, head_grads(): pl.pallas_call(kernel, out_shape=out_shape, grid_spec=pltpu.PrefetchScala...  18.6 us
    pallas_call x2, Pallas kernels, weight_parts(): pl.pallas_call(kernel, out_shape=(jax.ShapeDtypeStruct((heads, depth), BF...  16.4 us
    pallas_call x1, Pallas kernels, value_terms(): pl.pallas_call(kernel, out_shape=(jax.ShapeDtypeStruct((count, HD, width)...  11.3 us
    pallas_call x1, Pallas kernels, attended_heads(): pl.pallas_call(kernel, out_shape=jax.ShapeDtypeStruct((heads * columns, r...  10.9 us
    unnamed x42, local copies, waits for them, and re-layouts  7.22 us
    pallas_call x2, Pallas kernels, attention_probs(): pl.pallas_call(kernel, out_shape=jax.ShapeDtypeStruct((count, length, len...  5.72 us
  transfers between devices with their start and end apart: 29, of which 10 were waited for; matrix products, arithmetic and copies ran while one was open for 2% of the time, Pallas kernels for 31%

profile of v3, /device:TPU:1, one launch (start us, length us, event | category | flops | bytes accessed | tf_op | source)
XLA Modules:
  0.0 214.5 jit_solution(12522203322679756947)
XLA Ops:
  7.2 1.3 constant_dynamic-slice_fusion.1
  8.5 1.5 collective-permute-start
  10.0 1.6 shard_map.123
  11.9 2.7 %shard_map.120.refs_6_.refs_8_ = bf16[512,1024]{1,0:T(8,128)(2,1)} custom-call(s32[1024,512]{1,0:T(8,128)} %refs_8_.1, f32[8,512]{1,0:T(8,128)} %steps_ref.2), custom_call_target="tpu_custom_call" | custom-call | flops 1048576 | bytes 65536 | tf_op jit(solution)/shard_map/pallas_call | solution.py:53
  14.7 1.8 collective-permute-start.3
  16.5 2.2 %collective-permute-start.2 = (bf16[1024,512]{1,0:T(8,128)(2,1)S(1)}, bf16[1024,512]{1,0:T(8,128)(2,1)S(1)}, u32[]{:S(2)}, u32[]{:S(2)}) collective-permute-start(bf16[1024,512]{1,0:T(8,128)(2,1)S(1)} %pad_maximum_fusion.2.refs_0_), channel_id=1, source_target_pairs={{0,6},{2,0},{4,2},{6,4},{1,7},{3,1},{5,3},{7,5},{8,14},{10,8},{12,... | collective-permute-start | bytes 3145736 | tf_op jit(solution)/shard_map/ppermute | solution.py:22
  18.7 1.2 collective-permute-start.1
  19.9 1.3 collective-permute-start.5
  21.2 1.4 collective-permute-start.4
  22.6 2.9 %shard_map.122.p_high = bf16[4,512,512]{2,1,0:T(8,128)(2,1)S(1)} custom-call(bf16[512,1024]{1,0:T(8,128)(2,1)S(1)} %copy-done.8, bf16[512,128]{1,0:T(8,128)(2,1)S(1)} %copy-done.9, s32[512,1]{1,0:T(8,128)S(1)} %copy.13.down_ref, s32[1,512]{1,0:T(1,128)S(1)} %copy-done.7), custom_call_target="tpu_custom_call" | custom-call | flops 34359738368 | bytes 16777216 | tf_op jit(solution)/shard_map/pallas_call | solution.py:84
  25.5 1.4 copy-done.4
  26.9 2.9 %shard_map.121.p_low = bf16[4,512,512]{2,1,0:T(8,128)(2,1)S(1)} custom-call(bf16[512,1024]{1,0:T(8,128)(2,1)S(1)} %copy-done.8, bf16[512,128]{1,0:T(8,128)(2,1)S(1)} %copy-done.9, s32[512,1]{1,0:T(8,128)S(1)} %copy.13.down_ref, s32[1,512]{1,0:T(1,128)S(1)} %copy-done.7), custom_call_target="tpu_custom_call" | custom-call | flops 34359738368 | bytes 16777216 | tf_op jit(solution)/shard_map/pallas_call | solution.py:84
  29.7 1.3 copy-done.5
  31.0 11.2 %collective-permute-done.3.refs_4_.refs_6_ = bf16[1024,512]{1,0:T(8,128)(2,1)S(1)} collective-permute-done((bf16[1024,512]{1,0:T(8,128)(2,1)S(1)}, bf16[1024,512]{1,0:T(8,128)(2,1)S(1)}, u32[]{:S(2)}, u32[]{:S(2)}) %collective-permute-start.3) | collective-permute-done | bytes 1048608 | tf_op jit(solution)/shard_map/ppermute | solution.py:22
  42.2 2.7 %collective-permute-start.8 = (bf16[512,1024]{1,0:T(8,128)(2,1)}, bf16[512,1024]{1,0:T(8,128)(2,1)}, u32[]{:S(2)}, u32[]{:S(2)}) collective-permute-start(bf16[512,1024]{1,0:T(8,128)(2,1)} %shard_map.120.refs_6_.refs_8_), channel_id=1, source_target_pairs={{0,64},{64,0},{1,65},{65,1},{2,66},{66,2},{3,67},{67,3},{4,68},{68... | collective-permute-start | bytes 3145736 | tf_op jit(solution)/shard_map/ppermute | solution.py:22
  45.0 1.0 copy-done.11
  46.0 1.8 collective-permute-done.5.refs_9_.refs_14_
  47.8 1.0 copy-done.15
  48.8 0.9 collective-permute-start.9
  49.7 2.7 %collective-permute-start.6 = (bf16[1024,512]{1,0:T(8,128)(2,1)}, bf16[1024,512]{1,0:T(8,128)(2,1)}, u32[]{:S(2)}, u32[]{:S(2)}) collective-permute-start(bf16[1024,512]{1,0:T(8,128)(2,1)} %collective-permute-done.1.refs_1_), channel_id=1, source_target_pairs={{0,6},{2,0},{4,2},{6,4},{1,7},{3,1},{5,3},{7,5},{8,14},{10,8},{12,... | collective-permute-start | bytes 3145736 | tf_op jit(solution)/shard_map/ppermute | solution.py:22
  52.5 22.4 %collective-permute-done.8.refs_10_.refs_9_ = bf16[512,1024]{1,0:T(8,128)(2,1)} collective-permute-done((bf16[512,1024]{1,0:T(8,128)(2,1)}, bf16[512,1024]{1,0:T(8,128)(2,1)}, u32[]{:S(2)}, u32[]{:S(2)}) %collective-permute-start.8) | collective-permute-done | bytes 1048608 | tf_op jit(solution)/shard_map/ppermute | solution.py:22
  75.4 0.9 collective-permute-start.14
  76.3 1.8 collective-permute-start.12
  78.2 2.3 %collective-permute-start.11 = (bf16[1024,512]{1,0:T(8,128)(2,1)}, bf16[1024,512]{1,0:T(8,128)(2,1)S(1)}, u32[]{:S(2)}, u32[]{:S(2)}) collective-permute-start(bf16[1024,512]{1,0:T(8,128)(2,1)} %collective-permute-done.6.refs_3_), channel_id=1, source_target_pairs={{0,6},{2,0},{4,2},{6,4},{1,7},{3,1},{5,3},{7,5},{8,14},{10,8},{12,... | collective-permute-start | bytes 3145736 | tf_op jit(solution)/shard_map/ppermute | solution.py:22
  80.5 2.6 %collective-permute-start.13 = (bf16[512,1024]{1,0:T(8,128)(2,1)}, bf16[512,1024]{1,0:T(8,128)(2,1)}, u32[]{:S(2)}, u32[]{:S(2)}) collective-permute-start(bf16[512,1024]{1,0:T(8,128)(2,1)} %collective-permute-done.9.refs_8_.refs_12_), channel_id=1, source_target_pairs={{0,64},{64,0},{1,65},{65,1},{2,66},{66,2},{3,67},{67,3},{4,68},{68... | collective-permute-start | bytes 3145736 | tf_op jit(solution)/shard_map/ppermute | solution.py:22
  83.1 10.9 %shard_map.124.first = bf16[1024,512]{1,0:T(8,128)(2,1)} custom-call(bf16[512,8192]{1,0:T(8,128)(2,1)} %h_ref.3, bf16[8192,128]{1,0:T(8,128)(2,1)} %all-gather.2.cloned.1.call-done.v_ref, bf16[4,512,512]{2,1,0:T(8,128)(2,1)} %copy-done.5, bf16[4,512,512]{2,1,0:T(8,128)(2,1)} %copy-done.4), custom_call_target="tpu_custom_call" | custom-call | flops 34359738368 | bytes 16777216 | tf_op jit(solution)/shard_map/pallas_call | solution.py:129
  94.0 9.0 %shard_map.125.refs_16_ = f32[1024,1024]{1,0:T(8,128)} custom-call(s32[5]{0:T(128)S(1)} %stack.127.which_ref, s32[5]{0:T(128)S(1)} %compare_convert_fusion.use_ref, bf16[1024,512]{1,0:T(8,128)(2,1)S(1)} %pad_maximum_fusion.2.refs_0_, bf16[1024,512]{1,0:T(8,128)(2,1)} %collective-permute-done.1.refs_1_, bf16[1024,512]{1,0:T(8,128)(2,1)} %copy-done.11, ...), custom_call_target="tpu_custom_call" | custom-call | flops 1048576 | bytes 65536 | tf_op jit(solution)/shard_map/pallas_call | solution.py:332
  103.0 0.6 collective-permute-done.10.refs_4_
  104.0 0.5 copy-done.14
  105.0 1.0 copy-done.19
  106.0 3.9 %collective-permute-start.15 = (bf16[1024,512]{1,0:T(8,128)(2,1)S(1)}, bf16[1024,512]{1,0:T(8,128)(2,1)S(1)}, u32[]{:S(2)}, u32[]{:S(2)}) collective-permute-start(bf16[1024,512]{1,0:T(8,128)(2,1)S(1)} %copy-done.2), channel_id=1, source_target_pairs={{0,8},{8,0},{1,9},{9,1},{2,10},{10,2},{3,11},{11,3},{4,12},{12,4},... | collective-permute-start | bytes 3145736 | tf_op jit(solution)/shard_map/ppermute | solution.py:22
  110.1 9.6 %shard_map.126 = (f32[512,1024]{1,0:T(8,128)}, bf16[512,1024]{1,0:T(8,128)(2,1)S(1)}) custom-call(s32[8]{0:T(128)S(1)} %stack.120.which_ref, s32[8]{0:T(128)S(1)} %convert_element_type.54.use_ref, bf16[1024,512]{1,0:T(8,128)(2,1)} %copy-done, bf16[1024,512]{1,0:T(8,128)(2,1)} %collective-permute-done.1.refs_1_, bf16[1024,512]{1,0:T(8,128)(2,1)} %copy-done.11, ...), custom_call_target="tpu_custom_call" | custom-call | flops 1048576 | bytes 65536 | tf_op jit(solution)/shard_map/pallas_call | solution.py:332
  119.9 6.0 %shard_map.127 = (bf16[1024,512]{1,0:T(8,128)(2,1)}, bf16[1024,512]{1,0:T(8,128)(2,1)}, bf16[1024,512]{1,0:T(8,128)(2,1)S(1)}) custom-call(s32[3]{0:T(128)S(1)} %pad_add_fusion.order_ref, bf16[1024,512]{1,0:T(8,128)(2,1)S(1)} %copy-done.2, bf16[1024,512]{1,0:T(8,128)(2,1)S(1)} %collective-permute-done.15.second, bf16[1024,512]{1,0:T(8,128)(2,1)} %copy-done, ...), custom_call_target="tpu_custom_call" | custom-call | flops 1048576 | bytes 65536 | tf_op jit(solution)/shard_map/pallas_call | solution.py:378
  126.0 2.7 %collective-permute-start.18 = (bf16[1024,512]{1,0:T(8,128)(2,1)}, bf16[1024,512]{1,0:T(8,128)(2,1)}, u32[]{:S(2)}, u32[]{:S(2)}) collective-permute-start(bf16[1024,512]{1,0:T(8,128)(2,1)} %get-tuple-element.203), channel_id=1, source_target_pairs={{0,48},{16,0},{32,16},{48,32},{1,49},{17,1},{33,17},{49,33},{2,50}... | collective-permute-start | bytes 3145736 | tf_op jit(solution)/shard_map/ppermute | solution.py:22
  128.7 4.2 %collective-permute-start.19 = (bf16[1024,512]{1,0:T(8,128)(2,1)S(1)}, bf16[1024,512]{1,0:T(8,128)(2,1)S(1)}, u32[]{:S(2)}, u32[]{:S(2)}) collective-permute-start(bf16[1024,512]{1,0:T(8,128)(2,1)S(1)} %get-tuple-element.204), channel_id=1, source_target_pairs={{0,64},{64,0},{1,65},{65,1},{2,66},{66,2},{3,67},{67,3},{4,68},{68... | collective-permute-start | bytes 3145736 | tf_op jit(solution)/shard_map/ppermute | solution.py:22
  133.5 11.3 %shard_map.128 = (f32[8,128,512]{2,1,0:T(8,128)}, bf16[8,128,512]{2,1,0:T(8,128)(2,1)}) custom-call(s32[8]{0:T(128)} %get-tuple-element.248.own_at, s32[8]{0:T(128)} %get-tuple-element.247.other_at, bf16[512,8192]{1,0:T(8,128)(2,1)} %h_ref.3, f32[512,1024]{1,0:T(8,128)} %get-tuple-element.194.a_ref, bf16[512,1024]{1,0:T(8,128)(2,1)} %copy-done.17, ...), custom_call_target="tpu_custom_call" | custom-call | flops 1048576 | bytes 65536 | tf_op jit(solution)/shard_map/pallas_call | solution.py:181
  144.8 10.4 %shard_map.129 = (bf16[1024,512]{1,0:T(8,128)(2,1)S(1)}, bf16[1024,512]{1,0:T(8,128)(2,1)S(1)}, bf16[1024,512]{1,0:T(8,128)(2,1)S(1)}, bf16[1024,512]{1,0:T(8,128)(2,1)S(1)}, bf16[1024,512]{1,0:T(8,128)(2,1)S(1)}) custom-call(s32[5]{0:T(128)S(1)} %stack.129.order_ref, bf16[1024,512]{1,0:T(8,128)(2,1)} %shard_map.124.first, bf16[1024,512]{1,0:T(8,128)(2,1)} %copy-done.3, ...), custom_call_target="tpu_custom_call" | custom-call | flops 1048576 | bytes 65536 | tf_op jit(solution)/shard_map/pallas_call | solution.py:378
  155.3 1.7 collective-permute-start.22
  157.4 1.5 collective-permute-start.20
  159.7 3.3 %collective-permute-start.23 = (bf16[4,128,512]{2,1,0:T(8,128)(2,1)S(1)}, bf16[4,128,512]{2,1,0:T(8,128)(2,1)S(1)}, u32[]{:S(2)}, u32[]{:S(2)}) collective-permute-start(bf16[4,128,512]{2,1,0:T(8,128)(2,1)S(1)} %fusion), channel_id=1, source_target_pairs={{0,64},{64,0},{1,65},{65,1},{2,66},{66,2},{3,67},{67,3},{4,68},{68... | collective-permute-start | bytes 1572872 | tf_op jit(solution)/shard_map/ppermute | solution.py:22
  163.0 2.0 add_convert_fusion
  165.0 5.9 %collective-permute-done.21 = bf16[512,512]{1,0:T(8,128)(2,1)S(1)} collective-permute-done((bf16[512,512]{1,0:T(8,128)(2,1)S(1)}, bf16[512,512]{1,0:T(8,128)(2,1)S(1)}, u32[]{:S(2)}, u32[]{:S(2)}) %collective-permute-start.21) | collective-permute-done | bytes 524320 | tf_op jit(solution)/shard_map/ppermute | solution.py:22
  171.0 1.1 collective-permute-done.20
  172.0 2.6 %collective-permute-done.23 = bf16[4,128,512]{2,1,0:T(8,128)(2,1)S(1)} collective-permute-done((bf16[4,128,512]{2,1,0:T(8,128)(2,1)S(1)}, bf16[4,128,512]{2,1,0:T(8,128)(2,1)S(1)}, u32[]{:S(2)}, u32[]{:S(2)}) %collective-permute-start.23) | collective-permute-done | bytes 524320 | tf_op jit(solution)/shard_map/ppermute | solution.py:22
  175.6 2.7 %collective-permute-start.26 = (bf16[1152,512]{1,0:T(8,128)(2,1)S(1)}, bf16[1152,512]{1,0:T(8,128)(2,1)S(1)}, u32[]{:S(2)}, u32[]{:S(2)}) collective-permute-start(bf16[1152,512]{1,0:T(8,128)(2,1)S(1)} %pad_maximum_fusion.1), channel_id=1, source_target_pairs={{0,48},{16,0},{32,16},{48,32},{1,49},{17,1},{33,17},{49,33},{2,50}... | collective-permute-start | bytes 3538952 | tf_op jit(solution)/shard_map/ppermute | solution.py:22
  178.3 3.0 %collective-permute-start.24 = (bf16[1024,512]{1,0:T(8,128)(2,1)S(1)}, bf16[1024,512]{1,0:T(8,128)(2,1)S(1)}, u32[]{:S(2)}, u32[]{:S(2)}) collective-permute-start(bf16[1024,512]{1,0:T(8,128)(2,1)S(1)} %add_convert_fusion), channel_id=1, source_target_pairs={{0,64},{64,0},{1,65},{65,1},{2,66},{66,2},{3,67},{67,3},{4,68},{68... | collective-permute-start | bytes 3145736 | tf_op jit(solution)/shard_map/ppermute | solution.py:22
  181.3 23.7 %collective-permute-done.27.refs_7_ = bf16[128,512]{1,0:T(8,128)(2,1)S(1)} collective-permute-done((bf16[128,512]{1,0:T(8,128)(2,1)S(1)}, bf16[128,512]{1,0:T(8,128)(2,1)S(1)}, u32[]{:S(2)}, u32[]{:S(2)}) %collective-permute-start.27) | collective-permute-done | bytes 131104 | tf_op jit(solution)/shard_map/ppermute | solution.py:22
  205.0 2.6 %shard_map.130 = (f32[8,512]{1,0:T(8,128)}, f32[4,128]{1,0:T(4,128)}, f32[1024,512]{1,0:T(8,128)}, f32[512,128]{1,0:T(8,128)}) custom-call(bf16[1024,512]{1,0:T(8,128)(2,1)S(1)} %get-tuple-element.230.refs_0_, bf16[1024,512]{1,0:T(8,128)(2,1)S(1)} %collective-permute-done.24.refs_1_, bf16[1152,512]{1,0:T(8,128)(2,1)S(1)} %collective-permute-done.25.refs_2_.refs_4_, ...), custom_call_target="tpu_custom_call" | custom-call | flops 1048576 | bytes 65536 | tf_op jit(solution)/shard_map/pallas_call | solution.py:244
  (91 shorter events, 5.2 us)
Async XLA Ops:
  7.2 4.5 %copy-start.7 = (s32[1,512]{1,0:T(1,128)S(1)}, s32[1,512]{1,0:T(1,128)}, u32[]{:S(2)}) copy-start(s32[1,512]{1,0:T(1,128)} %along_ref.3) | copy-start | bytes 6148
  7.2 68.3 %all-gather.2.cloned.1.call-start = ((), (), s32[]{:S(2)}) async-start(), calls=%async_computation | async-start | bytes 2228224 | tf_op jit(solution)/shard_map/all_gather | solution.py:433
  8.5 6.1 %collective-permute-start = (bf16[512,512]{1,0:T(8,128)(2,1)S(1)}, bf16[512,512]{1,0:T(8,128)(2,1)S(1)}, u32[]{:S(2)}, u32[]{:S(2)}) collective-permute-start(bf16[512,512]{1,0:T(8,128)(2,1)S(1)} %get-tuple-element.243), channel_id=1, source_target_pairs={{0,8},{8,0},{1,9},{9,1},{2,10},{10,2},{3,11},{11,3},{4,12},{12,4},... | collective-permute-start | bytes 1572872 | tf_op jit(solution)/shard_map/ppermute | solution.py:22
  11.8 10.8 %copy-start.8 = (bf16[512,1024]{1,0:T(8,128)(2,1)S(1)}, bf16[512,1024]{1,0:T(8,128)(2,1)}, u32[]{:S(2)}) copy-start(bf16[512,1024]{1,0:T(8,128)(2,1)} %q_ref.1) | copy-start | bytes 3145732
  11.8 10.8 %copy-start.9 = (bf16[512,128]{1,0:T(8,128)(2,1)S(1)}, bf16[512,128]{1,0:T(8,128)(2,1)}, u32[]{:S(2)}) copy-start(bf16[512,128]{1,0:T(8,128)(2,1)} %k_ref.3) | copy-start | bytes 393220
  14.7 79.3 %copy-start = (bf16[1024,512]{1,0:T(8,128)(2,1)}, bf16[1024,512]{1,0:T(8,128)(2,1)S(1)}, u32[]{:S(2)}) copy-start(bf16[1024,512]{1,0:T(8,128)(2,1)S(1)} %pad_maximum_fusion.2.refs_0_) | copy-start | bytes 3145732
  14.7 27.5 %collective-permute-start.3 = (bf16[1024,512]{1,0:T(8,128)(2,1)S(1)}, bf16[1024,512]{1,0:T(8,128)(2,1)S(1)}, u32[]{:S(2)}, u32[]{:S(2)}) collective-permute-start(bf16[1024,512]{1,0:T(8,128)(2,1)S(1)} %pad_maximum_fusion.2.refs_0_), channel_id=1, source_target_pairs={{0,2},{2,4},{4,6},{6,0},{1,3},{3,5},{5,7},{7,1},{8,10},{10,12},{12... | collective-permute-start | bytes 3145736 | tf_op jit(solution)/shard_map/ppermute | solution.py:22
  16.5 28.5 %collective-permute-start.2 = (bf16[1024,512]{1,0:T(8,128)(2,1)S(1)}, bf16[1024,512]{1,0:T(8,128)(2,1)S(1)}, u32[]{:S(2)}, u32[]{:S(2)}) collective-permute-start(bf16[1024,512]{1,0:T(8,128)(2,1)S(1)} %pad_maximum_fusion.2.refs_0_), channel_id=1, source_target_pairs={{0,6},{2,0},{4,2},{6,4},{1,7},{3,1},{5,3},{7,5},{8,14},{10,8},{12,... | collective-permute-start | bytes 3145736 | tf_op jit(solution)/shard_map/ppermute | solution.py:22
  18.7 26.3 %collective-permute-start.1 = (bf16[1024,512]{1,0:T(8,128)(2,1)S(1)}, bf16[1024,512]{1,0:T(8,128)(2,1)}, u32[]{:S(2)}, u32[]{:S(2)}) collective-permute-start(bf16[1024,512]{1,0:T(8,128)(2,1)S(1)} %pad_maximum_fusion.2.refs_0_), channel_id=1, source_target_pairs={{0,1},{1,0},{2,3},{3,2},{4,5},{5,4},{6,7},{7,6},{8,9},{9,8},{10,11... | collective-permute-start | bytes 3145736 | tf_op jit(solution)/shard_map/ppermute | solution.py:22
  19.9 27.9 %collective-permute-start.5 = (bf16[512,1024]{1,0:T(8,128)(2,1)}, bf16[512,1024]{1,0:T(8,128)(2,1)}, u32[]{:S(2)}, u32[]{:S(2)}) collective-permute-start(bf16[512,1024]{1,0:T(8,128)(2,1)} %shard_map.120.refs_6_.refs_8_), channel_id=1, source_target_pairs={{0,16},{16,32},{32,48},{48,0},{1,17},{17,33},{33,49},{49,1},{2,18}... | collective-permute-start | bytes 3145736 | tf_op jit(solution)/shard_map/ppermute | solution.py:22
  21.2 26.6 %collective-permute-start.4 = (bf16[512,1024]{1,0:T(8,128)(2,1)}, bf16[512,1024]{1,0:T(8,128)(2,1)S(1)}, u32[]{:S(2)}, u32[]{:S(2)}) collective-permute-start(bf16[512,1024]{1,0:T(8,128)(2,1)} %shard_map.120.refs_6_.refs_8_), channel_id=1, source_target_pairs={{0,48},{16,0},{32,16},{48,32},{1,49},{17,1},{33,17},{49,33},{2,50}... | collective-permute-start | bytes 3145736 | tf_op jit(solution)/shard_map/ppermute | solution.py:22
  25.5 1.4 copy-start.4
  29.7 1.3 copy-start.5
  42.2 51.8 %copy-start.10 = (bf16[1024,512]{1,0:T(8,128)(2,1)}, bf16[1024,512]{1,0:T(8,128)(2,1)S(1)}, u32[]{:S(2)}) copy-start(bf16[1024,512]{1,0:T(8,128)(2,1)S(1)} %collective-permute-done.3.refs_4_.refs_6_) | copy-start | bytes 3145732
  42.2 32.7 %collective-permute-start.8 = (bf16[512,1024]{1,0:T(8,128)(2,1)}, bf16[512,1024]{1,0:T(8,128)(2,1)}, u32[]{:S(2)}, u32[]{:S(2)}) collective-permute-start(bf16[512,1024]{1,0:T(8,128)(2,1)} %shard_map.120.refs_6_.refs_8_), channel_id=1, source_target_pairs={{0,64},{64,0},{1,65},{65,1},{2,66},{66,2},{3,67},{67,3},{4,68},{68... | collective-permute-start | bytes 3145736 | tf_op jit(solution)/shard_map/ppermute | solution.py:22
  45.0 1.0 copy-start.11
  47.8 1.0 copy-start.15
  48.8 26.6 %collective-permute-start.9 = (bf16[512,1024]{1,0:T(8,128)(2,1)}, bf16[512,1024]{1,0:T(8,128)(2,1)}, u32[]{:S(2)}, u32[]{:S(2)}) collective-permute-start(bf16[512,1024]{1,0:T(8,128)(2,1)} %collective-permute-done.5.refs_9_.refs_14_), channel_id=1, source_target_pairs={{0,16},{16,32},{32,48},{48,0},{1,17},{17,33},{33,49},{49,1},{2,18}... | collective-permute-start | bytes 3145736 | tf_op jit(solution)/shard_map/ppermute | solution.py:22
  49.7 25.7 %collective-permute-start.7 = (bf16[1024,512]{1,0:T(8,128)(2,1)}, bf16[1024,512]{1,0:T(8,128)(2,1)S(1)}, u32[]{:S(2)}, u32[]{:S(2)}) collective-permute-start(bf16[1024,512]{1,0:T(8,128)(2,1)} %collective-permute-done.1.refs_1_), channel_id=1, source_target_pairs={{0,2},{2,4},{4,6},{6,0},{1,3},{3,5},{5,7},{7,1},{8,10},{10,12},{12... | collective-permute-start | bytes 3145736 | tf_op jit(solution)/shard_map/ppermute | solution.py:22
  49.7 25.7 %collective-permute-start.6 = (bf16[1024,512]{1,0:T(8,128)(2,1)}, bf16[1024,512]{1,0:T(8,128)(2,1)}, u32[]{:S(2)}, u32[]{:S(2)}) collective-permute-start(bf16[1024,512]{1,0:T(8,128)(2,1)} %collective-permute-done.1.refs_1_), channel_id=1, source_target_pairs={{0,6},{2,0},{4,2},{6,4},{1,7},{3,1},{5,3},{7,5},{8,14},{10,8},{12,... | collective-permute-start | bytes 3145736 | tf_op jit(solution)/shard_map/ppermute | solution.py:22
  75.4 7.7 %copy-start.12 = (bf16[1024,512]{1,0:T(8,128)(2,1)}, bf16[1024,512]{1,0:T(8,128)(2,1)S(1)}, u32[]{:S(2)}) copy-start(bf16[1024,512]{1,0:T(8,128)(2,1)S(1)} %collective-permute-done.7.refs_5_.refs_7_) | copy-start | bytes 3145732
  75.4 28.1 %collective-permute-start.14 = (bf16[512,1024]{1,0:T(8,128)(2,1)}, bf16[512,1024]{1,0:T(8,128)(2,1)S(1)}, u32[]{:S(2)}, u32[]{:S(2)}) collective-permute-start(bf16[512,1024]{1,0:T(8,128)(2,1)} %collective-permute-done.8.refs_10_.refs_9_), channel_id=1, source_target_pairs={{0,16},{16,32},{32,48},{48,0},{1,17},{17,33},{33,49},{49,1},{2,18}... | collective-permute-start | bytes 3145736 | tf_op jit(solution)/shard_map/ppermute | solution.py:22
  76.3 27.7 %collective-permute-start.12 = (bf16[512,1024]{1,0:T(8,128)(2,1)}, bf16[512,1024]{1,0:T(8,128)(2,1)S(1)}, u32[]{:S(2)}, u32[]{:S(2)}) collective-permute-start(bf16[512,1024]{1,0:T(8,128)(2,1)} %collective-permute-done.8.refs_10_.refs_9_), channel_id=1, source_target_pairs={{0,48},{16,0},{32,16},{48,32},{1,49},{17,1},{33,17},{49,33},{2,50}... | collective-permute-start | bytes 3145736 | tf_op jit(solution)/shard_map/ppermute | solution.py:22
  78.2 24.8 %collective-permute-start.11 = (bf16[1024,512]{1,0:T(8,128)(2,1)}, bf16[1024,512]{1,0:T(8,128)(2,1)S(1)}, u32[]{:S(2)}, u32[]{:S(2)}) collective-permute-start(bf16[1024,512]{1,0:T(8,128)(2,1)} %collective-permute-done.6.refs_3_), channel_id=1, source_target_pairs={{0,6},{2,0},{4,2},{6,4},{1,7},{3,1},{5,3},{7,5},{8,14},{10,8},{12,... | collective-permute-start | bytes 3145736 | tf_op jit(solution)/shard_map/ppermute | solution.py:22
  80.5 23.1 %collective-permute-start.10 = (bf16[1024,512]{1,0:T(8,128)(2,1)S(1)}, bf16[1024,512]{1,0:T(8,128)(2,1)S(1)}, u32[]{:S(2)}, u32[]{:S(2)}) collective-permute-start(bf16[1024,512]{1,0:T(8,128)(2,1)S(1)} %collective-permute-done.3.refs_4_.refs_6_), channel_id=1, source_target_pairs={{0,2},{2,4},{4,6},{6,0},{1,3},{3,5},{5,7},{7,1},{8,10},{10,12},{12... | collective-permute-start | bytes 3145736 | tf_op jit(solution)/shard_map/ppermute | solution.py:22
  80.5 23.1 %collective-permute-start.13 = (bf16[512,1024]{1,0:T(8,128)(2,1)}, bf16[512,1024]{1,0:T(8,128)(2,1)}, u32[]{:S(2)}, u32[]{:S(2)}) collective-permute-start(bf16[512,1024]{1,0:T(8,128)(2,1)} %collective-permute-done.9.refs_8_.refs_12_), channel_id=1, source_target_pairs={{0,64},{64,0},{1,65},{65,1},{2,66},{66,2},{3,67},{67,3},{4,68},{68... | collective-permute-start | bytes 3145736 | tf_op jit(solution)/shard_map/ppermute | solution.py:22
  94.0 12.0 %copy-start.2 = (bf16[1024,512]{1,0:T(8,128)(2,1)S(1)}, bf16[1024,512]{1,0:T(8,128)(2,1)}, u32[]{:S(2)}) copy-start(bf16[1024,512]{1,0:T(8,128)(2,1)} %shard_map.124.first) | copy-start | bytes 3145732
  103.0 1.0 copy-start.13
  105.0 1.0 copy-start.19
  106.0 13.7 %collective-permute-start.15 = (bf16[1024,512]{1,0:T(8,128)(2,1)S(1)}, bf16[1024,512]{1,0:T(8,128)(2,1)S(1)}, u32[]{:S(2)}, u32[]{:S(2)}) collective-permute-start(bf16[1024,512]{1,0:T(8,128)(2,1)S(1)} %copy-done.2), channel_id=1, source_target_pairs={{0,8},{8,0},{1,9},{9,1},{2,10},{10,2},{3,11},{11,3},{4,12},{12,4},... | collective-permute-start | bytes 3145736 | tf_op jit(solution)/shard_map/ppermute | solution.py:22
  119.7 6.2 %copy-start.3 = (bf16[1024,512]{1,0:T(8,128)(2,1)}, bf16[1024,512]{1,0:T(8,128)(2,1)S(1)}, u32[]{:S(2)}) copy-start(bf16[1024,512]{1,0:T(8,128)(2,1)S(1)} %collective-permute-done.15.second) | copy-start | bytes 3145732
  119.7 6.2 %collective-permute-start.16 = (bf16[512,1024]{1,0:T(8,128)(2,1)S(1)}, bf16[512,1024]{1,0:T(8,128)(2,1)S(1)}, u32[]{:S(2)}, u32[]{:S(2)}) collective-permute-start(bf16[512,1024]{1,0:T(8,128)(2,1)S(1)} %get-tuple-element.180), channel_id=1, source_target_pairs={{0,8},{8,0},{1,9},{9,1},{2,10},{10,2},{3,11},{11,3},{4,12},{12,4},... | collective-permute-start | bytes 3145736 | tf_op jit(solution)/shard_map/ppermute | solution.py:22
  125.9 2.8 %copy-start.17 = (bf16[512,1024]{1,0:T(8,128)(2,1)}, bf16[512,1024]{1,0:T(8,128)(2,1)S(1)}, u32[]{:S(2)}) copy-start(bf16[512,1024]{1,0:T(8,128)(2,1)S(1)} %collective-permute-done.16.b_ref) | copy-start | bytes 3145732
  125.9 29.3 %collective-permute-start.17 = (bf16[1024,512]{1,0:T(8,128)(2,1)}, bf16[1024,512]{1,0:T(8,128)(2,1)}, u32[]{:S(2)}, u32[]{:S(2)}) collective-permute-start(bf16[1024,512]{1,0:T(8,128)(2,1)} %get-tuple-element.202), channel_id=1, source_target_pairs={{0,16},{16,32},{32,48},{48,0},{1,17},{17,33},{33,49},{49,1},{2,18}... | collective-permute-start | bytes 3145736 | tf_op jit(solution)/shard_map/ppermute | solution.py:22
  126.0 29.2 %collective-permute-start.18 = (bf16[1024,512]{1,0:T(8,128)(2,1)}, bf16[1024,512]{1,0:T(8,128)(2,1)}, u32[]{:S(2)}, u32[]{:S(2)}) collective-permute-start(bf16[1024,512]{1,0:T(8,128)(2,1)} %get-tuple-element.203), channel_id=1, source_target_pairs={{0,48},{16,0},{32,16},{48,32},{1,49},{17,1},{33,17},{49,33},{2,50}... | collective-permute-start | bytes 3145736 | tf_op jit(solution)/shard_map/ppermute | solution.py:22
  128.7 26.6 %collective-permute-start.19 = (bf16[1024,512]{1,0:T(8,128)(2,1)S(1)}, bf16[1024,512]{1,0:T(8,128)(2,1)S(1)}, u32[]{:S(2)}, u32[]{:S(2)}) collective-permute-start(bf16[1024,512]{1,0:T(8,128)(2,1)S(1)} %get-tuple-element.204), channel_id=1, source_target_pairs={{0,64},{64,0},{1,65},{65,1},{2,66},{66,2},{3,67},{67,3},{4,68},{68... | collective-permute-start | bytes 3145736 | tf_op jit(solution)/shard_map/ppermute | solution.py:22
  144.8 10.5 %copy-start.20 = (bf16[8,128,512]{2,1,0:T(8,128)(2,1)S(1)}, bf16[8,128,512]{2,1,0:T(8,128)(2,1)}, u32[]{:S(2)}) copy-start(bf16[8,128,512]{2,1,0:T(8,128)(2,1)} %get-tuple-element.229) | copy-start | bytes 3145732
  155.3 3.9 %copy-start.16 = (f32[8,128,512]{2,1,0:T(8,128)S(1)}, f32[8,128,512]{2,1,0:T(8,128)}, u32[]{:S(2)}) copy-start(f32[8,128,512]{2,1,0:T(8,128)} %get-tuple-element.228) | copy-start | bytes 6291460
  155.3 3.9 %collective-permute-start.22 = (bf16[8,128,512]{2,1,0:T(8,128)(2,1)S(1)}, bf16[8,128,512]{2,1,0:T(8,128)(2,1)S(1)}, u32[]{:S(2)}, u32[]{:S(2)}) collective-permute-start(bf16[8,128,512]{2,1,0:T(8,128)(2,1)S(1)} %copy-done.20), channel_id=1, source_target_pairs={{0,8},{8,0},{1,9},{9,1},{2,10},{10,2},{3,11},{11,3},{4,12},{12,4},... | collective-permute-start | bytes 3145736 | tf_op jit(solution)/shard_map/ppermute | solution.py:22
  157.3 13.6 %collective-permute-start.21 = (bf16[512,512]{1,0:T(8,128)(2,1)S(1)}, bf16[512,512]{1,0:T(8,128)(2,1)S(1)}, u32[]{:S(2)}, u32[]{:S(2)}) collective-permute-start(bf16[512,512]{1,0:T(8,128)(2,1)S(1)} %get-tuple-element.240), channel_id=1, source_target_pairs={{0,48},{16,0},{32,16},{48,32},{1,49},{17,1},{33,17},{49,33},{2,50}... | collective-permute-start | bytes 1572872 | tf_op jit(solution)/shard_map/ppermute | solution.py:22
  157.4 14.6 %collective-permute-start.20 = (bf16[512,512]{1,0:T(8,128)(2,1)S(1)}, bf16[512,512]{1,0:T(8,128)(2,1)S(1)}, u32[]{:S(2)}, u32[]{:S(2)}) collective-permute-start(bf16[512,512]{1,0:T(8,128)(2,1)S(1)} %get-tuple-element.241), channel_id=1, source_target_pairs={{0,16},{16,32},{32,48},{48,0},{1,17},{17,33},{33,49},{49,1},{2,18}... | collective-permute-start | bytes 1572872 | tf_op jit(solution)/shard_map/ppermute | solution.py:22
  159.7 14.9 %collective-permute-start.23 = (bf16[4,128,512]{2,1,0:T(8,128)(2,1)S(1)}, bf16[4,128,512]{2,1,0:T(8,128)(2,1)S(1)}, u32[]{:S(2)}, u32[]{:S(2)}) collective-permute-start(bf16[4,128,512]{2,1,0:T(8,128)(2,1)S(1)} %fusion), channel_id=1, source_target_pairs={{0,64},{64,0},{1,65},{65,1},{2,66},{66,2},{3,67},{67,3},{4,68},{68... | collective-permute-start | bytes 1572872 | tf_op jit(solution)/shard_map/ppermute | solution.py:22
  175.3 29.7 %copy-start.1 = (s32[1024,512]{1,0:T(8,128)S(1)}, s32[1024,512]{1,0:T(8,128)}, u32[]{:S(2)}) copy-start(s32[1024,512]{1,0:T(8,128)} %refs_8_.1) | copy-start | bytes 6291460
  175.3 29.7 %copy-start.6 = (s32[512,128]{1,0:T(8,128)S(1)}, s32[512,128]{1,0:T(8,128)}, u32[]{:S(2)}) copy-start(s32[512,128]{1,0:T(8,128)} %refs_9_.1) | copy-start | bytes 786436
  175.4 29.6 %collective-permute-start.25 = (bf16[1152,512]{1,0:T(8,128)(2,1)S(1)}, bf16[1152,512]{1,0:T(8,128)(2,1)S(1)}, u32[]{:S(2)}, u32[]{:S(2)}) collective-permute-start(bf16[1152,512]{1,0:T(8,128)(2,1)S(1)} %pad_maximum_fusion), channel_id=1, source_target_pairs={{0,16},{16,32},{32,48},{48,0},{1,17},{17,33},{33,49},{49,1},{2,18}... | collective-permute-start | bytes 3538952 | tf_op jit(solution)/shard_map/ppermute | solution.py:22
  175.6 29.4 %collective-permute-start.26 = (bf16[1152,512]{1,0:T(8,128)(2,1)S(1)}, bf16[1152,512]{1,0:T(8,128)(2,1)S(1)}, u32[]{:S(2)}, u32[]{:S(2)}) collective-permute-start(bf16[1152,512]{1,0:T(8,128)(2,1)S(1)} %pad_maximum_fusion.1), channel_id=1, source_target_pairs={{0,48},{16,0},{32,16},{48,32},{1,49},{17,1},{33,17},{49,33},{2,50}... | collective-permute-start | bytes 3538952 | tf_op jit(solution)/shard_map/ppermute | solution.py:22
  178.3 26.7 %collective-permute-start.24 = (bf16[1024,512]{1,0:T(8,128)(2,1)S(1)}, bf16[1024,512]{1,0:T(8,128)(2,1)S(1)}, u32[]{:S(2)}, u32[]{:S(2)}) collective-permute-start(bf16[1024,512]{1,0:T(8,128)(2,1)S(1)} %add_convert_fusion), channel_id=1, source_target_pairs={{0,64},{64,0},{1,65},{65,1},{2,66},{66,2},{3,67},{67,3},{4,68},{68... | collective-permute-start | bytes 3145736 | tf_op jit(solution)/shard_map/ppermute | solution.py:22
  181.3 23.7 %collective-permute-start.27 = (bf16[128,512]{1,0:T(8,128)(2,1)S(1)}, bf16[128,512]{1,0:T(8,128)(2,1)S(1)}, u32[]{:S(2)}, u32[]{:S(2)}) collective-permute-start(bf16[128,512]{1,0:T(8,128)(2,1)S(1)} %get-tuple-element.244), channel_id=1, source_target_pairs={{0,32},{16,48},{32,0},{48,16},{1,33},{17,49},{33,1},{49,17},{2,34}... | collective-permute-start | bytes 393224 | tf_op jit(solution)/shard_map/ppermute | solution.py:22
  (2 other events, 1.9 us)
Sparse Core Ops, SparseCore 0:
  11.8 58.4 all-gather.1

commit v4 on v3

--- a/solution.py
+++ b/solution.py
@@ -155,7 +155,9 @@
         fetch.start()
         for h in range(2 * half):
             head = slice(h * HD, (h + 1) * HD)
-            attended_grad = (a_ref[:, head] + b_ref[:, head].astype(F32)).astype(BF16)
+            attended_grad = (
+                a_ref[:, head].astype(F32) + b_ref[:, head].astype(F32)
+            ).astype(BF16)
             more = jnp.dot(
                 (p_low, p_high)[h // half][h % half], attended_grad, preferred_element_type=F32
             )
@@ -309,7 +311,7 @@
         lax.fori_loop(0, count, one, 0)
         if last:
             start.wait()
-            own[...] = total[:half] + earlier[:half]
+            own[...] = (total[:half] + earlier[:half]).astype(BF16)
             other[...] = (total[half:] + earlier[half:]).astype(BF16)
 
     whole = pl.BlockSpec(memory_space=pltpu.VMEM)
@@ -323,10 +325,7 @@
     if last:
         sums = [pltpu.VMEM((rows, heads), F32)] * 2
         scratch = sums + [pltpu.SemaphoreType.DMA] + scratch
-        out_shape = (
-            jax.ShapeDtypeStruct((half, heads), F32),
-            jax.ShapeDtypeStruct((half, heads), BF16),
-        )
+        out_shape = (jax.ShapeDtypeStruct((half, heads), BF16),) * 2
     else:
         out_shape = jax.ShapeDtypeStruct((rows, heads), F32)
     return pl.pallas_call(

time: 217 us -> 217 us (level)
    unnamed x42 -> x44, local copies, waits for them, and re-layouts: 7.22 us -> 8.15 us
  transfers between devices with their start and end apart: 29 -> 29, of which waited for: 10 -> 11; matrix products, arithmetic and copies ran while one was open for 2% -> 2% of each run, Pallas kernels for 31% -> 31%
where the time goes in v4:
time: 217 us; the launch traced here: 215 us
  waiting for transfers between devices  70.4 us (32%)
  Pallas kernels  69.1 us (32%)
  starting transfers between devices  46.6 us (21%)
  between operations  14.5 us (7%)
  local copies, waits for them, and re-layouts  10.3 us (5%)
  other arithmetic  4.04 us (2%)
    ppermute x28, waiting for transfers between devices, shift(): return lax.ppermute(x, axis, [(i, (i + step) % n) for i in range(n)])  70.4 us
    ppermute x28, starting transfers between devices, shift(): return lax.ppermute(x, axis, [(i, (i + step) % n) for i in range(n)])  46.6 us
    pallas_call x2, Pallas kernels, head_grads(): pl.pallas_call(kernel, out_shape=out_shape, grid_spec=pltpu.PrefetchScala...  18.2 us
    pallas_call x2, Pallas kernels, weight_parts(): pl.pallas_call(kernel, out_shape=(jax.ShapeDtypeStruct((heads, depth), BF...  16.4 us
    pallas_call x1, Pallas kernels, value_terms(): pl.pallas_call(kernel, out_shape=(jax.ShapeDtypeStruct((count, HD, width)...  11 us
    pallas_call x1, Pallas kernels, attended_heads(): pl.pallas_call(kernel, out_shape=jax.ShapeDtypeStruct((heads * columns, r...  10.8 us
    unnamed x44, local copies, waits for them, and re-layouts  8.15 us
    pallas_call x2, Pallas kernels, attention_probs(): pl.pallas_call(kernel, out_shape=jax.ShapeDtypeStruct((count, length, len...  5.71 us
  transfers between devices with their start and end apart: 29, of which 11 were waited for; matrix products, arithmetic and copies ran while one was open for 2% of the time, Pallas kernels for 31%

profile of v4, /device:TPU:1, one launch (start us, length us, event | category | flops | bytes accessed | tf_op | source)
XLA Modules:
  0.0 215.0 jit_solution(11478071081933796133)
XLA Ops:
  7.2 1.3 constant_dynamic-slice_fusion.1
  8.5 1.5 collective-permute-start
  10.0 1.6 shard_map.123
  11.9 2.7 %shard_map.120.refs_6_.refs_8_ = bf16[512,1024]{1,0:T(8,128)(2,1)} custom-call(s32[1024,512]{1,0:T(8,128)} %refs_8_.1, f32[8,512]{1,0:T(8,128)} %steps_ref.2), custom_call_target="tpu_custom_call" | custom-call | flops 1048576 | bytes 65536 | tf_op jit(solution)/shard_map/pallas_call | solution.py:53
  14.6 1.8 collective-permute-start.3
  16.4 2.2 %collective-permute-start.2 = (bf16[1024,512]{1,0:T(8,128)(2,1)S(1)}, bf16[1024,512]{1,0:T(8,128)(2,1)S(1)}, u32[]{:S(2)}, u32[]{:S(2)}) collective-permute-start(bf16[1024,512]{1,0:T(8,128)(2,1)S(1)} %pad_maximum_fusion.2.refs_0_), channel_id=1, source_target_pairs={{0,6},{2,0},{4,2},{6,4},{1,7},{3,1},{5,3},{7,5},{8,14},{10,8},{12,... | collective-permute-start | bytes 3145736 | tf_op jit(solution)/shard_map/ppermute | solution.py:22
  18.6 1.2 collective-permute-start.1
  19.8 1.3 collective-permute-start.5
  21.1 1.4 collective-permute-start.4
  22.6 2.9 %shard_map.122.p_high = bf16[4,512,512]{2,1,0:T(8,128)(2,1)S(1)} custom-call(bf16[512,1024]{1,0:T(8,128)(2,1)S(1)} %copy-done.9, bf16[512,128]{1,0:T(8,128)(2,1)S(1)} %copy-done.10, s32[512,1]{1,0:T(8,128)S(1)} %copy.13.down_ref, s32[1,512]{1,0:T(1,128)S(1)} %copy-done.8), custom_call_target="tpu_custom_call" | custom-call | flops 34359738368 | bytes 16777216 | tf_op jit(solution)/shard_map/pallas_call | solution.py:84
  25.5 1.3 copy-done.4
  26.8 2.9 %shard_map.121.p_low = bf16[4,512,512]{2,1,0:T(8,128)(2,1)S(1)} custom-call(bf16[512,1024]{1,0:T(8,128)(2,1)S(1)} %copy-done.9, bf16[512,128]{1,0:T(8,128)(2,1)S(1)} %copy-done.10, s32[512,1]{1,0:T(8,128)S(1)} %copy.13.down_ref, s32[1,512]{1,0:T(1,128)S(1)} %copy-done.8), custom_call_target="tpu_custom_call" | custom-call | flops 34359738368 | bytes 16777216 | tf_op jit(solution)/shard_map/pallas_call | solution.py:84
  29.7 1.3 copy-done.5
  31.0 11.2 %collective-permute-done.3.refs_4_.refs_6_ = bf16[1024,512]{1,0:T(8,128)(2,1)S(1)} collective-permute-done((bf16[1024,512]{1,0:T(8,128)(2,1)S(1)}, bf16[1024,512]{1,0:T(8,128)(2,1)S(1)}, u32[]{:S(2)}, u32[]{:S(2)}) %collective-permute-start.3) | collective-permute-done | bytes 1048608 | tf_op jit(solution)/shard_map/ppermute | solution.py:22
  42.2 2.7 %collective-permute-start.8 = (bf16[512,1024]{1,0:T(8,128)(2,1)}, bf16[512,1024]{1,0:T(8,128)(2,1)}, u32[]{:S(2)}, u32[]{:S(2)}) collective-permute-start(bf16[512,1024]{1,0:T(8,128)(2,1)} %shard_map.120.refs_6_.refs_8_), channel_id=1, source_target_pairs={{0,64},{64,0},{1,65},{65,1},{2,66},{66,2},{3,67},{67,3},{4,68},{68... | collective-permute-start | bytes 3145736 | tf_op jit(solution)/shard_map/ppermute | solution.py:22
  44.9 1.0 copy-done.12
  45.9 1.8 collective-permute-done.5.refs_9_.refs_14_
  47.8 1.0 copy-done.16
  48.7 0.9 collective-permute-start.9
  49.7 2.7 %collective-permute-start.6 = (bf16[1024,512]{1,0:T(8,128)(2,1)}, bf16[1024,512]{1,0:T(8,128)(2,1)}, u32[]{:S(2)}, u32[]{:S(2)}) collective-permute-start(bf16[1024,512]{1,0:T(8,128)(2,1)} %collective-permute-done.1.refs_1_), channel_id=1, source_target_pairs={{0,6},{2,0},{4,2},{6,4},{1,7},{3,1},{5,3},{7,5},{8,14},{10,8},{12,... | collective-permute-start | bytes 3145736 | tf_op jit(solution)/shard_map/ppermute | solution.py:22
  52.4 22.4 %collective-permute-done.8.refs_10_.refs_9_ = bf16[512,1024]{1,0:T(8,128)(2,1)} collective-permute-done((bf16[512,1024]{1,0:T(8,128)(2,1)}, bf16[512,1024]{1,0:T(8,128)(2,1)}, u32[]{:S(2)}, u32[]{:S(2)}) %collective-permute-start.8) | collective-permute-done | bytes 1048608 | tf_op jit(solution)/shard_map/ppermute | solution.py:22
  75.4 0.9 collective-permute-start.14
  76.3 1.8 collective-permute-start.12
  78.1 2.3 %collective-permute-start.11 = (bf16[1024,512]{1,0:T(8,128)(2,1)}, bf16[1024,512]{1,0:T(8,128)(2,1)S(1)}, u32[]{:S(2)}, u32[]{:S(2)}) collective-permute-start(bf16[1024,512]{1,0:T(8,128)(2,1)} %collective-permute-done.6.refs_3_), channel_id=1, source_target_pairs={{0,6},{2,0},{4,2},{6,4},{1,7},{3,1},{5,3},{7,5},{8,14},{10,8},{12,... | collective-permute-start | bytes 3145736 | tf_op jit(solution)/shard_map/ppermute | solution.py:22
  80.4 2.7 %collective-permute-start.13 = (bf16[512,1024]{1,0:T(8,128)(2,1)}, bf16[512,1024]{1,0:T(8,128)(2,1)}, u32[]{:S(2)}, u32[]{:S(2)}) collective-permute-start(bf16[512,1024]{1,0:T(8,128)(2,1)} %collective-permute-done.9.refs_8_.refs_12_), channel_id=1, source_target_pairs={{0,64},{64,0},{1,65},{65,1},{2,66},{66,2},{3,67},{67,3},{4,68},{68... | collective-permute-start | bytes 3145736 | tf_op jit(solution)/shard_map/ppermute | solution.py:22
  83.1 10.8 %shard_map.124.first = bf16[1024,512]{1,0:T(8,128)(2,1)} custom-call(bf16[512,8192]{1,0:T(8,128)(2,1)} %h_ref.3, bf16[8192,128]{1,0:T(8,128)(2,1)} %all-gather.2.cloned.1.call-done.v_ref, bf16[4,512,512]{2,1,0:T(8,128)(2,1)} %copy-done.5, bf16[4,512,512]{2,1,0:T(8,128)(2,1)} %copy-done.4), custom_call_target="tpu_custom_call" | custom-call | flops 34359738368 | bytes 16777216 | tf_op jit(solution)/shard_map/pallas_call | solution.py:129
  94.0 9.0 %shard_map.125.refs_16_ = f32[1024,1024]{1,0:T(8,128)} custom-call(s32[5]{0:T(128)S(1)} %stack.127.which_ref, s32[5]{0:T(128)S(1)} %compare_convert_fusion.use_ref, bf16[1024,512]{1,0:T(8,128)(2,1)S(1)} %pad_maximum_fusion.2.refs_0_, bf16[1024,512]{1,0:T(8,128)(2,1)} %collective-permute-done.1.refs_1_, bf16[1024,512]{1,0:T(8,128)(2,1)} %copy-done.12, ...), custom_call_target="tpu_custom_call" | custom-call | flops 1048576 | bytes 65536 | tf_op jit(solution)/shard_map/pallas_call | solution.py:331
  104.4 0.5 copy-done.19
  104.9 1.0 copy-done.20
  105.9 3.8 %collective-permute-start.15 = (bf16[1024,512]{1,0:T(8,128)(2,1)S(1)}, bf16[1024,512]{1,0:T(8,128)(2,1)S(1)}, u32[]{:S(2)}, u32[]{:S(2)}) collective-permute-start(bf16[1024,512]{1,0:T(8,128)(2,1)S(1)} %copy-done.2), channel_id=1, source_target_pairs={{0,8},{8,0},{1,9},{9,1},{2,10},{10,2},{3,11},{11,3},{4,12},{12,4},... | collective-permute-start | bytes 3145736 | tf_op jit(solution)/shard_map/ppermute | solution.py:22
  110.0 9.2 %shard_map.126 = (bf16[512,1024]{1,0:T(8,128)(2,1)S(1)}, bf16[512,1024]{1,0:T(8,128)(2,1)}) custom-call(s32[8]{0:T(128)S(1)} %stack.120.which_ref, s32[8]{0:T(128)S(1)} %convert_element_type.54.use_ref, bf16[1024,512]{1,0:T(8,128)(2,1)} %copy-done, bf16[1024,512]{1,0:T(8,128)(2,1)} %collective-permute-done.1.refs_1_, bf16[1024,512]{1,0:T(8,128)(2,1)} %copy-done.12, ...), custom_call_target="tpu_custom_call" | custom-call | flops 1048576 | bytes 65536 | tf_op jit(solution)/shard_map/pallas_call | solution.py:331
  119.2 1.0 copy-done.7
  120.3 6.0 %shard_map.127 = (bf16[1024,512]{1,0:T(8,128)(2,1)}, bf16[1024,512]{1,0:T(8,128)(2,1)}, bf16[1024,512]{1,0:T(8,128)(2,1)S(1)}) custom-call(s32[3]{0:T(128)S(1)} %pad_add_fusion.order_ref, bf16[1024,512]{1,0:T(8,128)(2,1)S(1)} %copy-done.2, bf16[1024,512]{1,0:T(8,128)(2,1)S(1)} %collective-permute-done.15.second, bf16[1024,512]{1,0:T(8,128)(2,1)} %copy-done, ...), custom_call_target="tpu_custom_call" | custom-call | flops 1048576 | bytes 65536 | tf_op jit(solution)/shard_map/pallas_call | solution.py:377
  126.4 2.7 %collective-permute-start.18 = (bf16[1024,512]{1,0:T(8,128)(2,1)}, bf16[1024,512]{1,0:T(8,128)(2,1)}, u32[]{:S(2)}, u32[]{:S(2)}) collective-permute-start(bf16[1024,512]{1,0:T(8,128)(2,1)} %get-tuple-element.203), channel_id=1, source_target_pairs={{0,48},{16,0},{32,16},{48,32},{1,49},{17,1},{33,17},{49,33},{2,50}... | collective-permute-start | bytes 3145736 | tf_op jit(solution)/shard_map/ppermute | solution.py:22
  129.1 4.3 %collective-permute-start.19 = (bf16[1024,512]{1,0:T(8,128)(2,1)S(1)}, bf16[1024,512]{1,0:T(8,128)(2,1)S(1)}, u32[]{:S(2)}, u32[]{:S(2)}) collective-permute-start(bf16[1024,512]{1,0:T(8,128)(2,1)S(1)} %get-tuple-element.204), channel_id=1, source_target_pairs={{0,64},{64,0},{1,65},{65,1},{2,66},{66,2},{3,67},{67,3},{4,68},{68... | collective-permute-start | bytes 3145736 | tf_op jit(solution)/shard_map/ppermute | solution.py:22
  134.0 11.0 %shard_map.128 = (f32[8,128,512]{2,1,0:T(8,128)}, bf16[8,128,512]{2,1,0:T(8,128)(2,1)}) custom-call(s32[8]{0:T(128)} %get-tuple-element.248.own_at, s32[8]{0:T(128)} %get-tuple-element.247.other_at, bf16[512,8192]{1,0:T(8,128)(2,1)} %h_ref.3, bf16[512,1024]{1,0:T(8,128)(2,1)} %copy-done.7, bf16[512,1024]{1,0:T(8,128)(2,1)} %copy-done.18, ...), custom_call_target="tpu_custom_call" | custom-call | flops 1048576 | bytes 65536 | tf_op jit(solution)/shard_map/pallas_call | solution.py:183
  145.0 10.4 %shard_map.129 = (bf16[1024,512]{1,0:T(8,128)(2,1)S(1)}, bf16[1024,512]{1,0:T(8,128)(2,1)S(1)}, bf16[1024,512]{1,0:T(8,128)(2,1)S(1)}, bf16[1024,512]{1,0:T(8,128)(2,1)S(1)}, bf16[1024,512]{1,0:T(8,128)(2,1)S(1)}) custom-call(s32[5]{0:T(128)S(1)} %stack.129.order_ref, bf16[1024,512]{1,0:T(8,128)(2,1)} %shard_map.124.first, bf16[1024,512]{1,0:T(8,128)(2,1)} %copy-done.3, ...), custom_call_target="tpu_custom_call" | custom-call | flops 1048576 | bytes 65536 | tf_op jit(solution)/shard_map/pallas_call | solution.py:377
  155.8 1.7 collective-permute-start.22
  157.9 1.5 collective-permute-start.20
  160.2 3.3 %collective-permute-start.23 = (bf16[4,128,512]{2,1,0:T(8,128)(2,1)S(1)}, bf16[4,128,512]{2,1,0:T(8,128)(2,1)S(1)}, u32[]{:S(2)}, u32[]{:S(2)}) collective-permute-start(bf16[4,128,512]{2,1,0:T(8,128)(2,1)S(1)} %fusion), channel_id=1, source_target_pairs={{0,64},{64,0},{1,65},{65,1},{2,66},{66,2},{3,67},{67,3},{4,68},{68... | collective-permute-start | bytes 1572872 | tf_op jit(solution)/shard_map/ppermute | solution.py:22
  163.5 2.0 add_convert_fusion
  165.5 5.9 %collective-permute-done.21 = bf16[512,512]{1,0:T(8,128)(2,1)S(1)} collective-permute-done((bf16[512,512]{1,0:T(8,128)(2,1)S(1)}, bf16[512,512]{1,0:T(8,128)(2,1)S(1)}, u32[]{:S(2)}, u32[]{:S(2)}) %collective-permute-start.21) | collective-permute-done | bytes 524320 | tf_op jit(solution)/shard_map/ppermute | solution.py:22
  171.5 1.1 collective-permute-done.20
  172.5 2.6 %collective-permute-done.23 = bf16[4,128,512]{2,1,0:T(8,128)(2,1)S(1)} collective-permute-done((bf16[4,128,512]{2,1,0:T(8,128)(2,1)S(1)}, bf16[4,128,512]{2,1,0:T(8,128)(2,1)S(1)}, u32[]{:S(2)}, u32[]{:S(2)}) %collective-permute-start.23) | collective-permute-done | bytes 524320 | tf_op jit(solution)/shard_map/ppermute | solution.py:22
  176.1 2.7 %collective-permute-start.26 = (bf16[1152,512]{1,0:T(8,128)(2,1)S(1)}, bf16[1152,512]{1,0:T(8,128)(2,1)S(1)}, u32[]{:S(2)}, u32[]{:S(2)}) collective-permute-start(bf16[1152,512]{1,0:T(8,128)(2,1)S(1)} %pad_maximum_fusion.1), channel_id=1, source_target_pairs={{0,48},{16,0},{32,16},{48,32},{1,49},{17,1},{33,17},{49,33},{2,50}... | collective-permute-start | bytes 3538952 | tf_op jit(solution)/shard_map/ppermute | solution.py:22
  178.8 3.0 %collective-permute-start.24 = (bf16[1024,512]{1,0:T(8,128)(2,1)S(1)}, bf16[1024,512]{1,0:T(8,128)(2,1)S(1)}, u32[]{:S(2)}, u32[]{:S(2)}) collective-permute-start(bf16[1024,512]{1,0:T(8,128)(2,1)S(1)} %add_convert_fusion), channel_id=1, source_target_pairs={{0,64},{64,0},{1,65},{65,1},{2,66},{66,2},{3,67},{67,3},{4,68},{68... | collective-permute-start | bytes 3145736 | tf_op jit(solution)/shard_map/ppermute | solution.py:22
  181.8 23.7 %collective-permute-done.27.refs_7_ = bf16[128,512]{1,0:T(8,128)(2,1)S(1)} collective-permute-done((bf16[128,512]{1,0:T(8,128)(2,1)S(1)}, bf16[128,512]{1,0:T(8,128)(2,1)S(1)}, u32[]{:S(2)}, u32[]{:S(2)}) %collective-permute-start.27) | collective-permute-done | bytes 131104 | tf_op jit(solution)/shard_map/ppermute | solution.py:22
  205.5 2.6 %shard_map.130 = (f32[8,512]{1,0:T(8,128)}, f32[4,128]{1,0:T(4,128)}, f32[1024,512]{1,0:T(8,128)}, f32[512,128]{1,0:T(8,128)}) custom-call(bf16[1024,512]{1,0:T(8,128)(2,1)S(1)} %get-tuple-element.230.refs_0_, bf16[1024,512]{1,0:T(8,128)(2,1)S(1)} %collective-permute-done.24.refs_1_, bf16[1152,512]{1,0:T(8,128)(2,1)S(1)} %collective-permute-done.25.refs_2_.refs_4_, ...), custom_call_target="tpu_custom_call" | custom-call | flops 1048576 | bytes 65536 | tf_op jit(solution)/shard_map/pallas_call | solution.py:246
  (93 shorter events, 5.9 us)
Async XLA Ops:
  7.2 4.5 %copy-start.8 = (s32[1,512]{1,0:T(1,128)S(1)}, s32[1,512]{1,0:T(1,128)}, u32[]{:S(2)}) copy-start(s32[1,512]{1,0:T(1,128)} %along_ref.3) | copy-start | bytes 6148
  7.2 68.2 %all-gather.2.cloned.1.call-start = ((), (), s32[]{:S(2)}) async-start(), calls=%async_computation | async-start | bytes 2228224 | tf_op jit(solution)/shard_map/all_gather | solution.py:432
  8.5 6.1 %collective-permute-start = (bf16[512,512]{1,0:T(8,128)(2,1)S(1)}, bf16[512,512]{1,0:T(8,128)(2,1)S(1)}, u32[]{:S(2)}, u32[]{:S(2)}) collective-permute-start(bf16[512,512]{1,0:T(8,128)(2,1)S(1)} %get-tuple-element.243), channel_id=1, source_target_pairs={{0,8},{8,0},{1,9},{9,1},{2,10},{10,2},{3,11},{11,3},{4,12},{12,4},... | collective-permute-start | bytes 1572872 | tf_op jit(solution)/shard_map/ppermute | solution.py:22
  11.8 10.8 %copy-start.9 = (bf16[512,1024]{1,0:T(8,128)(2,1)S(1)}, bf16[512,1024]{1,0:T(8,128)(2,1)}, u32[]{:S(2)}) copy-start(bf16[512,1024]{1,0:T(8,128)(2,1)} %q_ref.1) | copy-start | bytes 3145732
  11.8 10.7 %copy-start.10 = (bf16[512,128]{1,0:T(8,128)(2,1)S(1)}, bf16[512,128]{1,0:T(8,128)(2,1)}, u32[]{:S(2)}) copy-start(bf16[512,128]{1,0:T(8,128)(2,1)} %k_ref.3) | copy-start | bytes 393220
  14.6 79.3 %copy-start = (bf16[1024,512]{1,0:T(8,128)(2,1)}, bf16[1024,512]{1,0:T(8,128)(2,1)S(1)}, u32[]{:S(2)}) copy-start(bf16[1024,512]{1,0:T(8,128)(2,1)S(1)} %pad_maximum_fusion.2.refs_0_) | copy-start | bytes 3145732
  14.6 27.5 %collective-permute-start.3 = (bf16[1024,512]{1,0:T(8,128)(2,1)S(1)}, bf16[1024,512]{1,0:T(8,128)(2,1)S(1)}, u32[]{:S(2)}, u32[]{:S(2)}) collective-permute-start(bf16[1024,512]{1,0:T(8,128)(2,1)S(1)} %pad_maximum_fusion.2.refs_0_), channel_id=1, source_target_pairs={{0,2},{2,4},{4,6},{6,0},{1,3},{3,5},{5,7},{7,1},{8,10},{10,12},{12... | collective-permute-start | bytes 3145736 | tf_op jit(solution)/shard_map/ppermute | solution.py:22
  16.4 28.5 %collective-permute-start.2 = (bf16[1024,512]{1,0:T(8,128)(2,1)S(1)}, bf16[1024,512]{1,0:T(8,128)(2,1)S(1)}, u32[]{:S(2)}, u32[]{:S(2)}) collective-permute-start(bf16[1024,512]{1,0:T(8,128)(2,1)S(1)} %pad_maximum_fusion.2.refs_0_), channel_id=1, source_target_pairs={{0,6},{2,0},{4,2},{6,4},{1,7},{3,1},{5,3},{7,5},{8,14},{10,8},{12,... | collective-permute-start | bytes 3145736 | tf_op jit(solution)/shard_map/ppermute | solution.py:22
  18.6 26.3 %collective-permute-start.1 = (bf16[1024,512]{1,0:T(8,128)(2,1)S(1)}, bf16[1024,512]{1,0:T(8,128)(2,1)}, u32[]{:S(2)}, u32[]{:S(2)}) collective-permute-start(bf16[1024,512]{1,0:T(8,128)(2,1)S(1)} %pad_maximum_fusion.2.refs_0_), channel_id=1, source_target_pairs={{0,1},{1,0},{2,3},{3,2},{4,5},{5,4},{6,7},{7,6},{8,9},{9,8},{10,11... | collective-permute-start | bytes 3145736 | tf_op jit(solution)/shard_map/ppermute | solution.py:22
  19.8 27.9 %collective-permute-start.5 = (bf16[512,1024]{1,0:T(8,128)(2,1)}, bf16[512,1024]{1,0:T(8,128)(2,1)}, u32[]{:S(2)}, u32[]{:S(2)}) collective-permute-start(bf16[512,1024]{1,0:T(8,128)(2,1)} %shard_map.120.refs_6_.refs_8_), channel_id=1, source_target_pairs={{0,16},{16,32},{32,48},{48,0},{1,17},{17,33},{33,49},{49,1},{2,18}... | collective-permute-start | bytes 3145736 | tf_op jit(solution)/shard_map/ppermute | solution.py:22
  21.1 26.6 %collective-permute-start.4 = (bf16[512,1024]{1,0:T(8,128)(2,1)}, bf16[512,1024]{1,0:T(8,128)(2,1)S(1)}, u32[]{:S(2)}, u32[]{:S(2)}) collective-permute-start(bf16[512,1024]{1,0:T(8,128)(2,1)} %shard_map.120.refs_6_.refs_8_), channel_id=1, source_target_pairs={{0,48},{16,0},{32,16},{48,32},{1,49},{17,1},{33,17},{49,33},{2,50}... | collective-permute-start | bytes 3145736 | tf_op jit(solution)/shard_map/ppermute | solution.py:22
  25.5 1.4 copy-start.4
  29.7 1.3 copy-start.5
  42.2 51.8 %copy-start.11 = (bf16[1024,512]{1,0:T(8,128)(2,1)}, bf16[1024,512]{1,0:T(8,128)(2,1)S(1)}, u32[]{:S(2)}) copy-start(bf16[1024,512]{1,0:T(8,128)(2,1)S(1)} %collective-permute-done.3.refs_4_.refs_6_) | copy-start | bytes 3145732
  42.2 32.7 %collective-permute-start.8 = (bf16[512,1024]{1,0:T(8,128)(2,1)}, bf16[512,1024]{1,0:T(8,128)(2,1)}, u32[]{:S(2)}, u32[]{:S(2)}) collective-permute-start(bf16[512,1024]{1,0:T(8,128)(2,1)} %shard_map.120.refs_6_.refs_8_), channel_id=1, source_target_pairs={{0,64},{64,0},{1,65},{65,1},{2,66},{66,2},{3,67},{67,3},{4,68},{68... | collective-permute-start | bytes 3145736 | tf_op jit(solution)/shard_map/ppermute | solution.py:22
  47.8 1.0 copy-start.16
  48.7 26.6 %collective-permute-start.9 = (bf16[512,1024]{1,0:T(8,128)(2,1)}, bf16[512,1024]{1,0:T(8,128)(2,1)}, u32[]{:S(2)}, u32[]{:S(2)}) collective-permute-start(bf16[512,1024]{1,0:T(8,128)(2,1)} %collective-permute-done.5.refs_9_.refs_14_), channel_id=1, source_target_pairs={{0,16},{16,32},{32,48},{48,0},{1,17},{17,33},{33,49},{49,1},{2,18}... | collective-permute-start | bytes 3145736 | tf_op jit(solution)/shard_map/ppermute | solution.py:22
  49.7 25.7 %collective-permute-start.7 = (bf16[1024,512]{1,0:T(8,128)(2,1)}, bf16[1024,512]{1,0:T(8,128)(2,1)S(1)}, u32[]{:S(2)}, u32[]{:S(2)}) collective-permute-start(bf16[1024,512]{1,0:T(8,128)(2,1)} %collective-permute-done.1.refs_1_), channel_id=1, source_target_pairs={{0,2},{2,4},{4,6},{6,0},{1,3},{3,5},{5,7},{7,1},{8,10},{10,12},{12... | collective-permute-start | bytes 3145736 | tf_op jit(solution)/shard_map/ppermute | solution.py:22
  49.7 25.7 %collective-permute-start.6 = (bf16[1024,512]{1,0:T(8,128)(2,1)}, bf16[1024,512]{1,0:T(8,128)(2,1)}, u32[]{:S(2)}, u32[]{:S(2)}) collective-permute-start(bf16[1024,512]{1,0:T(8,128)(2,1)} %collective-permute-done.1.refs_1_), channel_id=1, source_target_pairs={{0,6},{2,0},{4,2},{6,4},{1,7},{3,1},{5,3},{7,5},{8,14},{10,8},{12,... | collective-permute-start | bytes 3145736 | tf_op jit(solution)/shard_map/ppermute | solution.py:22
  75.3 7.8 %copy-start.13 = (bf16[1024,512]{1,0:T(8,128)(2,1)}, bf16[1024,512]{1,0:T(8,128)(2,1)S(1)}, u32[]{:S(2)}) copy-start(bf16[1024,512]{1,0:T(8,128)(2,1)S(1)} %collective-permute-done.7.refs_5_.refs_7_) | copy-start | bytes 3145732
  75.4 28.1 %collective-permute-start.14 = (bf16[512,1024]{1,0:T(8,128)(2,1)}, bf16[512,1024]{1,0:T(8,128)(2,1)S(1)}, u32[]{:S(2)}, u32[]{:S(2)}) collective-permute-start(bf16[512,1024]{1,0:T(8,128)(2,1)} %collective-permute-done.8.refs_10_.refs_9_), channel_id=1, source_target_pairs={{0,16},{16,32},{32,48},{48,0},{1,17},{17,33},{33,49},{49,1},{2,18}... | collective-permute-start | bytes 3145736 | tf_op jit(solution)/shard_map/ppermute | solution.py:22
  76.3 27.7 %collective-permute-start.12 = (bf16[512,1024]{1,0:T(8,128)(2,1)}, bf16[512,1024]{1,0:T(8,128)(2,1)S(1)}, u32[]{:S(2)}, u32[]{:S(2)}) collective-permute-start(bf16[512,1024]{1,0:T(8,128)(2,1)} %collective-permute-done.8.refs_10_.refs_9_), channel_id=1, source_target_pairs={{0,48},{16,0},{32,16},{48,32},{1,49},{17,1},{33,17},{49,33},{2,50}... | collective-permute-start | bytes 3145736 | tf_op jit(solution)/shard_map/ppermute | solution.py:22
  78.1 24.8 %collective-permute-start.11 = (bf16[1024,512]{1,0:T(8,128)(2,1)}, bf16[1024,512]{1,0:T(8,128)(2,1)S(1)}, u32[]{:S(2)}, u32[]{:S(2)}) collective-permute-start(bf16[1024,512]{1,0:T(8,128)(2,1)} %collective-permute-done.6.refs_3_), channel_id=1, source_target_pairs={{0,6},{2,0},{4,2},{6,4},{1,7},{3,1},{5,3},{7,5},{8,14},{10,8},{12,... | collective-permute-start | bytes 3145736 | tf_op jit(solution)/shard_map/ppermute | solution.py:22
  80.4 23.0 %collective-permute-start.10 = (bf16[1024,512]{1,0:T(8,128)(2,1)S(1)}, bf16[1024,512]{1,0:T(8,128)(2,1)S(1)}, u32[]{:S(2)}, u32[]{:S(2)}) collective-permute-start(bf16[1024,512]{1,0:T(8,128)(2,1)S(1)} %collective-permute-done.3.refs_4_.refs_6_), channel_id=1, source_target_pairs={{0,2},{2,4},{4,6},{6,0},{1,3},{3,5},{5,7},{7,1},{8,10},{10,12},{12... | collective-permute-start | bytes 3145736 | tf_op jit(solution)/shard_map/ppermute | solution.py:22
  80.4 23.0 %collective-permute-start.13 = (bf16[512,1024]{1,0:T(8,128)(2,1)}, bf16[512,1024]{1,0:T(8,128)(2,1)}, u32[]{:S(2)}, u32[]{:S(2)}) collective-permute-start(bf16[512,1024]{1,0:T(8,128)(2,1)} %collective-permute-done.9.refs_8_.refs_12_), channel_id=1, source_target_pairs={{0,64},{64,0},{1,65},{65,1},{2,66},{66,2},{3,67},{67,3},{4,68},{68... | collective-permute-start | bytes 3145736 | tf_op jit(solution)/shard_map/ppermute | solution.py:22
  93.9 12.0 %copy-start.2 = (bf16[1024,512]{1,0:T(8,128)(2,1)S(1)}, bf16[1024,512]{1,0:T(8,128)(2,1)}, u32[]{:S(2)}) copy-start(bf16[1024,512]{1,0:T(8,128)(2,1)} %shard_map.124.first) | copy-start | bytes 3145732
  103.0 1.0 copy-start.14
  104.9 1.0 copy-start.20
  105.9 14.3 %collective-permute-start.15 = (bf16[1024,512]{1,0:T(8,128)(2,1)S(1)}, bf16[1024,512]{1,0:T(8,128)(2,1)S(1)}, u32[]{:S(2)}, u32[]{:S(2)}) collective-permute-start(bf16[1024,512]{1,0:T(8,128)(2,1)S(1)} %copy-done.2), channel_id=1, source_target_pairs={{0,8},{8,0},{1,9},{9,1},{2,10},{10,2},{3,11},{11,3},{4,12},{12,4},... | collective-permute-start | bytes 3145736 | tf_op jit(solution)/shard_map/ppermute | solution.py:22
  119.2 1.0 copy-start.7
  120.2 6.1 %copy-start.3 = (bf16[1024,512]{1,0:T(8,128)(2,1)}, bf16[1024,512]{1,0:T(8,128)(2,1)S(1)}, u32[]{:S(2)}) copy-start(bf16[1024,512]{1,0:T(8,128)(2,1)S(1)} %collective-permute-done.15.second) | copy-start | bytes 3145732
  120.2 6.1 %collective-permute-start.16 = (bf16[512,1024]{1,0:T(8,128)(2,1)}, bf16[512,1024]{1,0:T(8,128)(2,1)S(1)}, u32[]{:S(2)}, u32[]{:S(2)}) collective-permute-start(bf16[512,1024]{1,0:T(8,128)(2,1)} %get-tuple-element.180), channel_id=1, source_target_pairs={{0,8},{8,0},{1,9},{9,1},{2,10},{10,2},{3,11},{11,3},{4,12},{12,4},... | collective-permute-start | bytes 3145736 | tf_op jit(solution)/shard_map/ppermute | solution.py:22
  126.3 2.8 %copy-start.18 = (bf16[512,1024]{1,0:T(8,128)(2,1)}, bf16[512,1024]{1,0:T(8,128)(2,1)S(1)}, u32[]{:S(2)}) copy-start(bf16[512,1024]{1,0:T(8,128)(2,1)S(1)} %collective-permute-done.16.b_ref) | copy-start | bytes 3145732
  126.3 29.1 %collective-permute-start.17 = (bf16[1024,512]{1,0:T(8,128)(2,1)}, bf16[1024,512]{1,0:T(8,128)(2,1)}, u32[]{:S(2)}, u32[]{:S(2)}) collective-permute-start(bf16[1024,512]{1,0:T(8,128)(2,1)} %get-tuple-element.202), channel_id=1, source_target_pairs={{0,16},{16,32},{32,48},{48,0},{1,17},{17,33},{33,49},{49,1},{2,18}... | collective-permute-start | bytes 3145736 | tf_op jit(solution)/shard_map/ppermute | solution.py:22
  126.4 29.1 %collective-permute-start.18 = (bf16[1024,512]{1,0:T(8,128)(2,1)}, bf16[1024,512]{1,0:T(8,128)(2,1)}, u32[]{:S(2)}, u32[]{:S(2)}) collective-permute-start(bf16[1024,512]{1,0:T(8,128)(2,1)} %get-tuple-element.203), channel_id=1, source_target_pairs={{0,48},{16,0},{32,16},{48,32},{1,49},{17,1},{33,17},{49,33},{2,50}... | collective-permute-start | bytes 3145736 | tf_op jit(solution)/shard_map/ppermute | solution.py:22
  129.1 26.7 %collective-permute-start.19 = (bf16[1024,512]{1,0:T(8,128)(2,1)S(1)}, bf16[1024,512]{1,0:T(8,128)(2,1)S(1)}, u32[]{:S(2)}, u32[]{:S(2)}) collective-permute-start(bf16[1024,512]{1,0:T(8,128)(2,1)S(1)} %get-tuple-element.204), channel_id=1, source_target_pairs={{0,64},{64,0},{1,65},{65,1},{2,66},{66,2},{3,67},{67,3},{4,68},{68... | collective-permute-start | bytes 3145736 | tf_op jit(solution)/shard_map/ppermute | solution.py:22
  145.0 10.7 %copy-start.21 = (bf16[8,128,512]{2,1,0:T(8,128)(2,1)S(1)}, bf16[8,128,512]{2,1,0:T(8,128)(2,1)}, u32[]{:S(2)}) copy-start(bf16[8,128,512]{2,1,0:T(8,128)(2,1)} %get-tuple-element.229) | copy-start | bytes 3145732
  155.8 4.0 %copy-start.17 = (f32[8,128,512]{2,1,0:T(8,128)S(1)}, f32[8,128,512]{2,1,0:T(8,128)}, u32[]{:S(2)}) copy-start(f32[8,128,512]{2,1,0:T(8,128)} %get-tuple-element.228) | copy-start | bytes 6291460
  155.8 4.0 %collective-permute-start.22 = (bf16[8,128,512]{2,1,0:T(8,128)(2,1)S(1)}, bf16[8,128,512]{2,1,0:T(8,128)(2,1)S(1)}, u32[]{:S(2)}, u32[]{:S(2)}) collective-permute-start(bf16[8,128,512]{2,1,0:T(8,128)(2,1)S(1)} %copy-done.21), channel_id=1, source_target_pairs={{0,8},{8,0},{1,9},{9,1},{2,10},{10,2},{3,11},{11,3},{4,12},{12,4},... | collective-permute-start | bytes 3145736 | tf_op jit(solution)/shard_map/ppermute | solution.py:22
  157.8 13.6 %collective-permute-start.21 = (bf16[512,512]{1,0:T(8,128)(2,1)S(1)}, bf16[512,512]{1,0:T(8,128)(2,1)S(1)}, u32[]{:S(2)}, u32[]{:S(2)}) collective-permute-start(bf16[512,512]{1,0:T(8,128)(2,1)S(1)} %get-tuple-element.240), channel_id=1, source_target_pairs={{0,48},{16,0},{32,16},{48,32},{1,49},{17,1},{33,17},{49,33},{2,50}... | collective-permute-start | bytes 1572872 | tf_op jit(solution)/shard_map/ppermute | solution.py:22
  157.9 14.6 %collective-permute-start.20 = (bf16[512,512]{1,0:T(8,128)(2,1)S(1)}, bf16[512,512]{1,0:T(8,128)(2,1)S(1)}, u32[]{:S(2)}, u32[]{:S(2)}) collective-permute-start(bf16[512,512]{1,0:T(8,128)(2,1)S(1)} %get-tuple-element.241), channel_id=1, source_target_pairs={{0,16},{16,32},{32,48},{48,0},{1,17},{17,33},{33,49},{49,1},{2,18}... | collective-permute-start | bytes 1572872 | tf_op jit(solution)/shard_map/ppermute | solution.py:22
  160.2 14.9 %collective-permute-start.23 = (bf16[4,128,512]{2,1,0:T(8,128)(2,1)S(1)}, bf16[4,128,512]{2,1,0:T(8,128)(2,1)S(1)}, u32[]{:S(2)}, u32[]{:S(2)}) collective-permute-start(bf16[4,128,512]{2,1,0:T(8,128)(2,1)S(1)} %fusion), channel_id=1, source_target_pairs={{0,64},{64,0},{1,65},{65,1},{2,66},{66,2},{3,67},{67,3},{4,68},{68... | collective-permute-start | bytes 1572872 | tf_op jit(solution)/shard_map/ppermute | solution.py:22
  175.8 29.7 %copy-start.1 = (s32[1024,512]{1,0:T(8,128)S(1)}, s32[1024,512]{1,0:T(8,128)}, u32[]{:S(2)}) copy-start(s32[1024,512]{1,0:T(8,128)} %refs_8_.1) | copy-start | bytes 6291460
  175.8 29.7 %copy-start.6 = (s32[512,128]{1,0:T(8,128)S(1)}, s32[512,128]{1,0:T(8,128)}, u32[]{:S(2)}) copy-start(s32[512,128]{1,0:T(8,128)} %refs_9_.1) | copy-start | bytes 786436
  175.9 29.6 %collective-permute-start.25 = (bf16[1152,512]{1,0:T(8,128)(2,1)S(1)}, bf16[1152,512]{1,0:T(8,128)(2,1)S(1)}, u32[]{:S(2)}, u32[]{:S(2)}) collective-permute-start(bf16[1152,512]{1,0:T(8,128)(2,1)S(1)} %pad_maximum_fusion), channel_id=1, source_target_pairs={{0,16},{16,32},{32,48},{48,0},{1,17},{17,33},{33,49},{49,1},{2,18}... | collective-permute-start | bytes 3538952 | tf_op jit(solution)/shard_map/ppermute | solution.py:22
  176.1 29.4 %collective-permute-start.26 = (bf16[1152,512]{1,0:T(8,128)(2,1)S(1)}, bf16[1152,512]{1,0:T(8,128)(2,1)S(1)}, u32[]{:S(2)}, u32[]{:S(2)}) collective-permute-start(bf16[1152,512]{1,0:T(8,128)(2,1)S(1)} %pad_maximum_fusion.1), channel_id=1, source_target_pairs={{0,48},{16,0},{32,16},{48,32},{1,49},{17,1},{33,17},{49,33},{2,50}... | collective-permute-start | bytes 3538952 | tf_op jit(solution)/shard_map/ppermute | solution.py:22
  178.8 26.7 %collective-permute-start.24 = (bf16[1024,512]{1,0:T(8,128)(2,1)S(1)}, bf16[1024,512]{1,0:T(8,128)(2,1)S(1)}, u32[]{:S(2)}, u32[]{:S(2)}) collective-permute-start(bf16[1024,512]{1,0:T(8,128)(2,1)S(1)} %add_convert_fusion), channel_id=1, source_target_pairs={{0,64},{64,0},{1,65},{65,1},{2,66},{66,2},{3,67},{67,3},{4,68},{68... | collective-permute-start | bytes 3145736 | tf_op jit(solution)/shard_map/ppermute | solution.py:22
  181.8 23.7 %collective-permute-start.27 = (bf16[128,512]{1,0:T(8,128)(2,1)S(1)}, bf16[128,512]{1,0:T(8,128)(2,1)S(1)}, u32[]{:S(2)}, u32[]{:S(2)}) collective-permute-start(bf16[128,512]{1,0:T(8,128)(2,1)S(1)} %get-tuple-element.244), channel_id=1, source_target_pairs={{0,32},{16,48},{32,0},{48,16},{1,33},{17,49},{33,1},{49,17},{2,34}... | collective-permute-start | bytes 393224 | tf_op jit(solution)/shard_map/ppermute | solution.py:22
  (3 other events, 2.9 us)
Sparse Core Ops, SparseCore 0:
  11.8 58.5 all-gather.1
